TPU v7x, 32 devices: a whole 2x2x4 slice. The times are simulated.
32 devices in a mesh: dp: 4 (over z), seq: 8 (over y, x, core).
Axes of the slice: x: 2, y: 2, z: 4, core: 2. Of those that a mesh axis runs over, the one named last changes fastest.
Arguments:
- hidden_in: bfloat16 [4, 2048, 1152], P('dp', 'seq'), may hold values from -6 to 6
- lengths: int32 [4, 8], P('dp'), may hold values from 64 to 384, as said below
- timesteps: int32 [4, 8], P('dp'), may hold values from 0 to 999
- head_mask: int32 [4, 2, 8, 16], P('dp'), may hold values 0 or 1
- group_mask: int32 [4, 2, 8, 16], P('dp'), may hold values 0 or 1
- skip_mask: int32 [4, 2, 2048], P('dp', None, 'seq'), may hold values 0 or 1
- modulation_weight: bfloat16 [2, 1152, 6912], P(None, 'dp', 'seq'), may hold values from -0.1875 to 0.1875
- joint_weight: bfloat16 [2, 1152, 3456], P(None, 'dp', 'seq'), may hold values from -0.25 to 0.25
- project_weight: bfloat16 [2, 1152, 1152], P(None, 'dp', 'seq'), may hold values from -0.5 to 0.5
- expand_weight: bfloat16 [2, 1152, 4608], P(None, 'dp', 'seq'), may hold values from -0.1875 to 0.1875
- reduce_weight: bfloat16 [2, 4608, 1152], P(None, 'dp', 'seq'), may hold values from -0.09375 to 0.09375
- cotangent: bfloat16 [4, 2048, 1152], P('dp', 'seq'), may hold values from -6 to 6
Outputs:
- final_state: bfloat16 [4, 2048, 1152], P('dp', 'seq')
- input_grad: float32 [4, 2048, 1152], P('dp', 'seq')
- modulation_grad: float32 [2, 1152, 6912], P(None, 'dp', 'seq')
- joint_grad: float32 [2, 1152, 3456], P(None, 'dp', 'seq')
- project_grad: float32 [2, 1152, 1152], P(None, 'dp', 'seq')
- expand_grad: float32 [2, 1152, 4608], P(None, 'dp', 'seq')
- reduce_grad: float32 [2, 4608, 1152], P(None, 'dp', 'seq')
Inputs may be any that keep to these rules, and one draw needn't show every extreme that they name: `lengths`: in every row the crops follow one another from the row's start and padding of 1 to 64 tokens fills the rest. Crop c, for c < 7, ends (c + 1) * 256 + u tokens into the row with 64 <= u <= 128, so every boundary between consecutive blocks of 256 tokens lies inside a crop and a crop lies within two such blocks.
All inputs are finite; a program needn't handle non-finite values. No bound on the sum of `head_mask` or of `group_mask` or of `skip_mask` on one device may be relied on, other than what follows from the above.
Results may differ from a plain program's by a relative error of at most 0.04.
Values may be sent and summed in bfloat16 or wider, within the bound.
No kernel may reach another device: no remote copies, remote signals or barrier semaphores. Data moves between devices by JAX's collectives and lax.ppermute only.
A program may use at most 320 MiB of HBM per device.

v0:
```python
import math

import jax
import jax.numpy as jnp
from jax import lax
from jax.sharding import PartitionSpec as P

D = 1152
HEADS = 16
HEAD_DIM = 72
FF = 4608
GROUPS = 16
LAYERS = 2


EPS = 1e-06
HIGH = lax.Precision.HIGHEST
NEGATIVE = -1e30


def extended(value, sides, width):
    for axis, dim in sides:
        devices, length = (lax.axis_size(axis), value.shape[dim])
        up = [(i, (i + 1) % devices) for i in range(devices - 1)]
        down = [(j, i) for i, j in up]
        last = lax.slice_in_dim(value, length - width, length, axis=dim)
        leading = lax.slice_in_dim(value, 0, width, axis=dim)
        before = lax.ppermute(last, axis, up)
        after = lax.ppermute(leading, axis, down)
        value = jnp.concatenate([before, value, after], axis=dim)
    return value


def shifted(value, axis, steps):
    count = lax.axis_size(axis)
    leading, last = (max(0, -steps), min(count, count - steps))
    return lax.ppermute(value, axis, [(source, source + steps) for source in range(leading, last)])


def layer_norm(stream):
    center = stream - jnp.mean(stream, axis=-1, keepdims=True)
    spread = jnp.mean(center * center, axis=-1, keepdims=True)
    return center * lax.rsqrt(spread + EPS)


def modulate(stream, offset, stretch):
    return layer_norm(stream) * (1.0 + stretch) + offset


def step_embed(stamps, breadth):
    halfway = breadth // 2
    frequency = jnp.exp(-math.log(10000.0) * jnp.arange(halfway, dtype=jnp.float32) / halfway)
    angles = stamps.astype(jnp.float32)[..., None] * frequency
    return jnp.concatenate([jnp.cos(angles), jnp.sin(angles)], axis=-1)


def segment_of(places, bounds):
    return jnp.sum((places[:, None] >= bounds[None, :]).astype(jnp.int32), axis=-1)


def through_rows(left, right, precision=None):
    return lax.dot_general(
        left,
        right,
        (((0,), (0,)), ((), ())),
        precision=precision,
        preferred_element_type=jnp.float32,
    )


def against_cols(left, right):
    return lax.dot_general(
        left, right, (((1,), (1,)), ((), ())), preferred_element_type=jnp.float32
    )


def fetch(mod_part, joint_part, project_part, expand_part, reduce_part):
    rows_whole = (
        lax.all_gather(mod_part, "dp", axis=0, tiled=True),
        lax.all_gather(joint_part, "dp", axis=0, tiled=True),
        lax.all_gather(project_part, "dp", axis=0, tiled=True),
        lax.all_gather(expand_part, "dp", axis=0, tiled=True),
        lax.all_gather(reduce_part, "dp", axis=0, tiled=True),
    )
    return (
        lax.all_gather(rows_whole[0], "seq", axis=1, tiled=True),
        lax.all_gather(rows_whole[1], "seq", axis=1, tiled=True),
        lax.all_gather(rows_whole[2], "seq", axis=1, tiled=True),
        lax.all_gather(rows_whole[3], "seq", axis=1, tiled=True),
        lax.all_gather(rows_whole[4], "seq", axis=1, tiled=True),
    )


def reduce_grads(grads):
    columns = (
        lax.psum_scatter(
            grads[0].astype(jnp.bfloat16), "seq", scatter_dimension=1, tiled=True
        ).astype(jnp.float32),
        lax.psum_scatter(
            grads[1].astype(jnp.bfloat16), "seq", scatter_dimension=1, tiled=True
        ).astype(jnp.float32),
        lax.psum_scatter(
            grads[2].astype(jnp.bfloat16), "seq", scatter_dimension=1, tiled=True
        ).astype(jnp.float32),
        lax.psum_scatter(
            grads[3].astype(jnp.bfloat16), "seq", scatter_dimension=1, tiled=True
        ).astype(jnp.float32),
        lax.psum_scatter(
            grads[4].astype(jnp.bfloat16), "seq", scatter_dimension=1, tiled=True
        ).astype(jnp.float32),
    )
    return (
        lax.psum_scatter(
            columns[0].astype(jnp.bfloat16), "dp", scatter_dimension=0, tiled=True
        ).astype(jnp.float32),
        lax.psum_scatter(
            columns[1].astype(jnp.bfloat16), "dp", scatter_dimension=0, tiled=True
        ).astype(jnp.float32),
        lax.psum_scatter(
            columns[2].astype(jnp.bfloat16), "dp", scatter_dimension=0, tiled=True
        ).astype(jnp.float32),
        lax.psum_scatter(
            columns[3].astype(jnp.bfloat16), "dp", scatter_dimension=0, tiled=True
        ).astype(jnp.float32),
        lax.psum_scatter(
            columns[4].astype(jnp.bfloat16), "dp", scatter_dimension=0, tiled=True
        ).astype(jnp.float32),
    )


def token_masks(onehot, living, heads_row, groups_row, skips_row):
    head_tok = jnp.dot(onehot, heads_row.astype(jnp.float32), precision=HIGH)
    group_tok = jnp.dot(onehot, groups_row.astype(jnp.float32), precision=HIGH)
    channel_tok = jnp.repeat(group_tok, FF // GROUPS, axis=-1)
    keeping = skips_row.astype(jnp.float32) * living
    return (head_tok, channel_tok, keeping)


def split_heads(rows):
    count = rows.shape[0]
    return jnp.transpose(rows.reshape(count, HEADS, HEAD_DIM), (1, 0, 2))


def join_heads(heads):
    count = heads.shape[1]
    return jnp.transpose(heads, (1, 0, 2)).reshape(count, D)


def span_attend(queries, key_rows, value_rows, segment, bounds):
    tokens = queries.shape[0]
    my_place = lax.axis_index("seq")
    whole = lax.axis_size("seq") * tokens
    pairs = jnp.concatenate([key_rows, value_rows], axis=-1)
    padded = extended(pairs, (("seq", 0),), tokens)
    key_places = (my_place - 1) * tokens + jnp.arange(3 * tokens, dtype=jnp.int32)
    inside = (key_places >= 0) & (key_places < whole)
    key_segment = jnp.where(inside, segment_of(key_places, bounds), -1)
    allowed = segment[:, None] == key_segment[None, :]
    factor = HEAD_DIM ** (-0.5)

    def one_head(item):
        query_one, key_one, value_one = item
        scores = against_cols(query_one, key_one) * factor
        masked = jnp.where(allowed, scores, NEGATIVE)
        highest = jnp.max(masked, axis=-1)
        weights = jnp.where(allowed, jnp.exp(masked - highest[:, None]), 0.0)
        total = jnp.sum(weights, axis=-1)
        probs = (weights / total[:, None]).astype(jnp.bfloat16)
        return (
            jnp.dot(probs, value_one, preferred_element_type=jnp.float32),
            highest + jnp.log(total),
        )

    summed, log_total = lax.map(
        one_head, (split_heads(queries), split_heads(padded[:, :D]), split_heads(padded[:, D:]))
    )
    attended = jnp.transpose(summed, (1, 0, 2))
    return (attended, log_total, padded, allowed)


def span_backward(queries, padded, allowed, d_attended, attended, log_total):
    tokens = queries.shape[0]
    factor = HEAD_DIM ** (-0.5)
    balance = jnp.transpose(jnp.sum(d_attended.astype(jnp.float32) * attended, axis=-1))

    def one_head(item):
        query_one, key_one, value_one, grad_one, total_one, balance_one = item
        scores = against_cols(query_one, key_one) * factor
        probs = jnp.where(allowed, jnp.exp(scores - total_one[:, None]), 0.0)
        d_value = through_rows(probs.astype(jnp.bfloat16), grad_one)
        d_probs = against_cols(grad_one, value_one)
        d_scores = (probs * (d_probs - balance_one[:, None])).astype(jnp.bfloat16)
        d_query = jnp.dot(d_scores, key_one, preferred_element_type=jnp.float32) * factor
        d_key = through_rows(d_scores, query_one) * factor
        return (d_query, d_key, d_value)

    d_query, d_key, d_value = lax.map(
        one_head,
        (
            split_heads(queries),
            split_heads(padded[:, :D]),
            split_heads(padded[:, D:]),
            jnp.transpose(d_attended, (1, 0, 2)),
            log_total,
            balance,
        ),
    )
    d_pairs = jnp.concatenate([join_heads(d_key), join_heads(d_value)], axis=-1)
    from_above = shifted(d_pairs[:tokens].astype(jnp.bfloat16), "seq", -1).astype(jnp.float32)
    from_below = shifted(d_pairs[2 * tokens :].astype(jnp.bfloat16), "seq", 1).astype(jnp.float32)
    own = d_pairs[tokens : 2 * tokens] + from_above + from_below
    return (join_heads(d_query), own[:, :D], own[:, D:])


def layer_forward(stream, modulation, weights, masks, onehot, living, segment, bounds):
    head_tok, channel_tok, keeping = masks
    tokens = stream.shape[0]
    tokmod = jnp.dot(onehot, modulation, precision=HIGH)
    offset_one, stretch_one, gate_one, offset_two, stretch_two, gate_two = jnp.split(
        tokmod, 6, axis=-1
    )
    normed_one = modulate(stream, offset_one, stretch_one).astype(jnp.bfloat16)
    joint = jnp.dot(normed_one, weights[1], preferred_element_type=jnp.float32).astype(jnp.bfloat16)
    queries, key_rows, value_rows = jnp.split(joint, 3, axis=-1)
    attended, log_total, padded, allowed = span_attend(
        queries, key_rows, value_rows, segment, bounds
    )
    mixed = (attended * head_tok[:, :, None]).reshape(tokens, D).astype(jnp.bfloat16)
    branch = jnp.dot(mixed, weights[2], preferred_element_type=jnp.float32)
    middle = stream + gate_one * branch * living[:, None]
    normed_two = modulate(middle, offset_two, stretch_two).astype(jnp.bfloat16)
    pre_act = jnp.dot(normed_two, weights[3], preferred_element_type=jnp.float32)
    activated = (jax.nn.gelu(pre_act, approximate=True) * channel_tok).astype(jnp.bfloat16)
    feedout = jnp.dot(activated, weights[4], preferred_element_type=jnp.float32)
    result = middle + gate_two * feedout * keeping[:, None]
    record = (
        stream,
        tokmod,
        normed_one,
        queries,
        padded,
        allowed,
        attended,
        log_total,
        mixed,
        branch,
        middle,
        normed_two,
        pre_act,
        activated,
        feedout,
    )
    return (result, record)


def layer_backward(adjoint, record, weights, masks, onehot, living, condition):
    (
        stream,
        tokmod,
        normed_one,
        queries,
        padded,
        allowed,
        attended,
        log_total,
        mixed,
        branch,
        middle,
        normed_two,
        pre_act,
        activated,
        feedout,
    ) = record
    head_tok, channel_tok, keeping = masks
    tokens = stream.shape[0]
    offset_one, stretch_one, gate_one, offset_two, stretch_two, gate_two = jnp.split(
        tokmod, 6, axis=-1
    )
    d_feed = (adjoint * gate_two * keeping[:, None]).astype(jnp.bfloat16)
    d_gate_two = adjoint * feedout * keeping[:, None]
    g_reduce = through_rows(activated, d_feed)
    d_active = against_cols(d_feed, weights[4])
    _, gelu_back = jax.vjp(lambda inner: jax.nn.gelu(inner, approximate=True), pre_act)
    d_pre = gelu_back(d_active * channel_tok)[0].astype(jnp.bfloat16)
    g_expand = through_rows(normed_two, d_pre)
    d_normed_two = against_cols(d_pre, weights[3])
    _, second_back = jax.vjp(modulate, middle, offset_two, stretch_two)
    d_middle, d_offset_two, d_stretch_two = second_back(d_normed_two)
    d_middle = d_middle + adjoint
    d_branch = (d_middle * gate_one * living[:, None]).astype(jnp.bfloat16)
    d_gate_one = d_middle * branch * living[:, None]
    g_project = through_rows(mixed, d_branch)
    d_mixed = against_cols(d_branch, weights[2])
    d_attended = (d_mixed.reshape(tokens, HEADS, HEAD_DIM) * head_tok[:, :, None]).astype(
        jnp.bfloat16
    )
    d_query, d_key, d_value = span_backward(
        queries, padded, allowed, d_attended, attended, log_total
    )
    d_joint = jnp.concatenate([d_query, d_key, d_value], axis=-1).astype(jnp.bfloat16)
    g_joint = through_rows(normed_one, d_joint)
    d_normed_one = against_cols(d_joint, weights[1])
    _, first_back = jax.vjp(modulate, stream, offset_one, stretch_one)
    d_stream, d_offset_one, d_stretch_one = first_back(d_normed_one)
    d_stream = d_stream + d_middle
    d_tokmod = jnp.concatenate(
        [d_offset_one, d_stretch_one, d_gate_one, d_offset_two, d_stretch_two, d_gate_two], axis=-1
    )
    d_modulation = through_rows(onehot, d_tokmod, HIGH)
    g_modulation = through_rows(condition.astype(jnp.float32), d_modulation, HIGH)
    return (d_stream, (g_modulation, g_joint, g_project, g_expand, g_reduce))


def shards(
    hidden_in,
    lengths,
    timesteps,
    head_mask,
    group_mask,
    skip_mask,
    modulation_weight,
    joint_weight,
    project_weight,
    expand_weight,
    reduce_weight,
    cotangent,
):
    tokens = hidden_in.shape[1]
    my_place = lax.axis_index("seq")
    bounds = jnp.cumsum(lengths[0])
    places = my_place * tokens + jnp.arange(tokens, dtype=jnp.int32)
    segment = segment_of(places, bounds)
    crop_count = lengths.shape[1]
    onehot = (segment[:, None] == jnp.arange(crop_count, dtype=jnp.int32)[None, :]).astype(
        jnp.float32
    )
    living = (segment < crop_count).astype(jnp.float32)
    condition = jax.nn.silu(step_embed(timesteps[0], D)).astype(jnp.bfloat16)
    stream = hidden_in[0].astype(jnp.float32)
    records = []
    for number in range(LAYERS):
        weights = fetch(
            modulation_weight[number],
            joint_weight[number],
            project_weight[number],
            expand_weight[number],
            reduce_weight[number],
        )
        masks = token_masks(
            onehot, living, head_mask[0, number], group_mask[0, number], skip_mask[0, number]
        )
        modulation = jnp.dot(condition, weights[0], preferred_element_type=jnp.float32)
        stream, record = layer_forward(
            stream, modulation, weights, masks, onehot, living, segment, bounds
        )
        records.append((masks, record))
    final_state = stream.astype(jnp.bfloat16)[None]
    adjoint = cotangent[0].astype(jnp.float32)
    owned = [None] * LAYERS
    for number in reversed(range(LAYERS)):
        weights = fetch(
            modulation_weight[number],
            joint_weight[number],
            project_weight[number],
            expand_weight[number],
            reduce_weight[number],
        )
        masks, record = records[number]
        adjoint, layer_grads = layer_backward(
            adjoint, record, weights, masks, onehot, living, condition
        )
        owned[number] = reduce_grads(layer_grads)
    modulation_grad = jnp.stack([owned[number][0] for number in range(LAYERS)])
    joint_grad = jnp.stack([owned[number][1] for number in range(LAYERS)])
    project_grad = jnp.stack([owned[number][2] for number in range(LAYERS)])
    expand_grad = jnp.stack([owned[number][3] for number in range(LAYERS)])
    reduce_grad = jnp.stack([owned[number][4] for number in range(LAYERS)])
    return (
        final_state,
        adjoint[None],
        modulation_grad,
        joint_grad,
        project_grad,
        expand_grad,
        reduce_grad,
    )


def solution(mesh):
    in_specs = (
        P("dp", "seq", None),
        P("dp", None),
        P("dp", None),
        P("dp", None, None, None),
        P("dp", None, None, None),
        P("dp", None, "seq"),
        P(None, "dp", "seq"),
        P(None, "dp", "seq"),
        P(None, "dp", "seq"),
        P(None, "dp", "seq"),
        P(None, "dp", "seq"),
        P("dp", "seq", None),
    )
    out_specs = (
        P("dp", "seq", None),
        P("dp", "seq", None),
        P(None, "dp", "seq"),
        P(None, "dp", "seq"),
        P(None, "dp", "seq"),
        P(None, "dp", "seq"),
        P(None, "dp", "seq"),
    )
    return jax.shard_map(shards, mesh=mesh, in_specs=in_specs, out_specs=out_specs, check_vma=False)
```

profile of v0, /device:TPU:0, one launch (start us, length us, event | category | flops | bytes accessed | tf_op | source)
XLA Modules:
  0.0 2366.0 jit_solution(2754825928731489722)
XLA Ops:
  13.0 45.2 %all-gather.37.cloned.1.call-done = bf16[1,1152,864]{2,1,0:T(8,128)(2,1)} async-done(((bf16[1,288,864]{2,1,0:T(8,128)(2,1)}), bf16[1,1152,864]{2,1,0:T(8,128)(2,1)}) %all-gather.37.cloned.1.call-update) | async-done | bytes 1990672 | tf_op jit(solution)/shard_map/all_gather | solution.py:79
  62.4 38.5 %all-gather.2 = bf16[1,1152,432]{2,1,0:T(8,128)(2,1)S(1)} all-gather(bf16[1,288,432]{2,1,0:T(8,128)(2,1)S(1)} %get-tuple-element.688), channel_id=4, replica_groups=mesh['dp'=4,'seq'=8] {'dp'}, dimensions={1}, use_global_device_ids=true | all-gather | bytes 1244160 | tf_op jit(solution)/shard_map/all_gather | solution.py:80
  102.5 15.5 all-gather.53.cloned.1.call-done
  122.4 40.3 %all-gather.4 = bf16[1,1152,144]{2,0,1:T(2,128)(2,1)S(1)} all-gather(bf16[1,288,144]{2,0,1:T(2,128)(2,1)S(1)} %copy.245), channel_id=6, replica_groups=mesh['dp'=4,'seq'=8] {'dp'}, dimensions={1}, use_global_device_ids=true | all-gather | bytes 414720 | tf_op jit(solution)/shard_map/all_gather | solution.py:81
  172.5 31.5 %all-gather.49.cloned.1.call-done = bf16[1,4608,144]{1,2,0:T(8,128)(2,1)} async-done(((bf16[1,1152,144]{1,2,0:T(8,128)(2,1)}), bf16[1,4608,144]{1,2,0:T(8,128)(2,1)}) %all-gather.49.cloned.1.call-update) | async-done | bytes 1327120 | tf_op jit(solution)/shard_map/all_gather | solution.py:83
  204.0 34.1 %all-gather.12 = bf16[1,1152,432]{2,1,0:T(8,128)(2,1)S(1)} all-gather(bf16[1,288,432]{2,1,0:T(8,128)(2,1)S(1)} %get-tuple-element.687), channel_id=14, replica_groups=mesh['dp'=4,'seq'=8] {'dp'}, dimensions={1}, use_global_device_ids=true | all-gather | bytes 1244160 | tf_op jit(solution)/shard_map/all_gather | solution.py:80
  240.7 29.0 %all-gather.14 = bf16[1,1152,144]{2,0,1:T(2,128)(2,1)S(1)} all-gather(bf16[1,288,144]{2,0,1:T(2,128)(2,1)S(1)} %copy.246), channel_id=16, replica_groups=mesh['dp'=4,'seq'=8] {'dp'}, dimensions={1}, use_global_device_ids=true | all-gather | bytes 414720 | tf_op jit(solution)/shard_map/all_gather | solution.py:81
  287.4 57.3 %all-gather.39.cloned.1.call-done = bf16[1,1152,6912]{1,2,0:T(8,128)(2,1)} async-done(((bf16[1,1152,864]{1,2,0:T(8,128)(2,1)}), bf16[1,1152,6912]{1,2,0:T(8,128)(2,1)}) %all-gather.39.cloned.1.call-update) | async-done | bytes 15925264 | tf_op jit(solution)/shard_map/all_gather | solution.py:86
  344.7 9.7 fusion.104
  360.7 39.2 %all-gather.41.cloned.1.call-done = bf16[1,1152,3456]{1,2,0:T(8,128)(2,1)} async-done(((bf16[1,1152,432]{1,2,0:T(8,128)(2,1)}), bf16[1,1152,3456]{1,2,0:T(8,128)(2,1)}) %all-gather.41.cloned.1.call-update) | async-done | bytes 7962640 | tf_op jit(solution)/shard_map/all_gather | solution.py:87
  412.4 95.3 %all-gather.55.cloned.1.call-done = bf16[1,1152,6912]{1,2,0:T(8,128)(2,1)} async-done(((bf16[1,1152,864]{1,2,0:T(8,128)(2,1)}), bf16[1,1152,6912]{1,2,0:T(8,128)(2,1)}) %all-gather.55.cloned.1.call-update) | async-done | bytes 15925264 | tf_op jit(solution)/shard_map/all_gather | solution.py:86
  507.7 9.7 fusion.102
  540.7 49.9 %while.56 = (s32[]{:T(128)}, f32[16,256,72]{1,2,0:T(8,128)S(1)}, f32[16,256]{1,0:T(8,128)S(1)}, bf16[16,256,72]{2,1,0:T(8,128)(2,1)}, bf16[16,768,72]{2,1,0:T(8,...) while((s32[]{:T(128)}, f32[16,256,72]{1,2,0:T(8,128)S(1)}, ...), condition=%wide.region_8.9_spmd.clone, body=%wide.region_5.8_spmd.clone.sunk | while | flops 59178752 | bytes 2917481 | solution.py:174
  599.6 7.0 all-gather.47.cloned.1.call-done
  606.6 13.7 multiply_convert_fusion.1
  620.4 52.0 %all-gather.51.cloned.1.call-done = bf16[1,4608,1152]{1,2,0:T(8,128)(2,1)} async-done(((bf16[1,4608,144]{1,2,0:T(8,128)(2,1)}), bf16[1,4608,1152]{1,2,0:T(8,128)(2,1)}) %all-gather.51.cloned.1.call-update) | async-done | bytes 10616848 | tf_op jit(solution)/shard_map/all_gather | solution.py:90
  672.3 9.4 fusion.251
  684.3 43.0 %all-gather.57.cloned.1.call-done = bf16[1,1152,3456]{1,2,0:T(8,128)(2,1)} async-done(((bf16[1,1152,432]{1,2,0:T(8,128)(2,1)}), bf16[1,1152,3456]{1,2,0:T(8,128)(2,1)}) %all-gather.57.cloned.1.call-update) | async-done | bytes 7962640 | tf_op jit(solution)/shard_map/all_gather | solution.py:87
  739.0 22.7 all-gather.65.cloned.1.call-done
  796.4 50.1 %while.57 = (s32[]{:T(128)}, f32[16,256,72]{1,2,0:T(8,128)S(1)}, f32[16,256]{1,0:T(8,128)S(1)}, bf16[16,256,72]{2,1,0:T(8,128)(2,1)}, bf16[16,768,72]{2,1,0:T(8,...) while((s32[]{:T(128)}, f32[16,256,72]{1,2,0:T(8,128)S(1)}, ...), condition=%wide.region_16.17_spmd.clone, body=%wide.region_13.16_spmd.clone.sunk | while | flops 59178752 | bytes 2917481 | solution.py:174
  859.0 12.4 multiply_convert_fusion
  871.4 53.2 %all-gather.67.cloned.1.call-done = bf16[1,4608,1152]{1,2,0:T(8,128)(2,1)} async-done(((bf16[1,4608,144]{1,2,0:T(8,128)(2,1)}), bf16[1,4608,1152]{1,2,0:T(8,128)(2,1)}) %all-gather.67.cloned.1.call-update) | async-done | bytes 10616848 | tf_op jit(solution)/shard_map/all_gather | solution.py:90
  924.6 10.3 fusion.157
  935.0 8.4 multiply_reduce_fusion.2
  959.0 125.8 %while.58 = (s32[]{:T(128)}, bf16[16,256,72]{1,2,0:T(8,128)(2,1)}, f32[16,768,72]{1,2,0:T(8,128)S(1)}, f32[16,768,72]{1,2,0:T(8,128)}, bf16[16,256,72]{2,1,0:T(8...) while((s32[]{:T(128)}, bf16[16,256,72]{1,2,0:T(8,128)(2,1)}, ...), condition=%wide.region_23.24_spmd.clone, body=%wide.region_22.23_spmd.clone.sunk | while | flops 143204352 | bytes 4865153 | solution.py:197
  1099.6 7.3 constant_dynamic-update-slice_fusion.3
  1111.4 10.6 fusion.150
  1122.1 8.5 multiply_reduce_fusion
  1149.6 126.5 %while.59 = (s32[]{:T(128)}, bf16[16,256,72]{1,2,0:T(8,128)(2,1)}, f32[16,768,72]{1,2,0:T(8,128)S(1)}, f32[16,768,72]{1,2,0:T(8,128)}, bf16[16,256,72]{2,1,0:T(8...) while((s32[]{:T(128)}, bf16[16,256,72]{1,2,0:T(8,128)(2,1)}, ...), condition=%wide.region_30.31_spmd.clone, body=%wide.region_29.30_spmd.clone.sunk | while | flops 143204352 | bytes 4865153 | solution.py:197
  1280.2 20.7 collective-permute-start.7
  1354.0 15.4 convolution_convert_fusion
  1386.8 15.4 convolution_convert_fusion.1
  1412.3 83.3 %reduce-scatter.59.cloned.1.call-done = bf16[4608,144]{0,1:T(8,128)(2,1)} async-done(((bf16[4608,1152]{0,1:T(8,128)(2,1)}), bf16[4608,144]{0,1:T(8,128)(2,1)}) %reduce-scatter.59.cloned.1.call-update) | async-done | bytes 1327120 | tf_op jit(solution)/shard_map/reduce_scatter | solution.py:108
  1499.6 81.7 %reduce-scatter.55.cloned.1.call-done = bf16[1152,576]{0,1:T(8,128)(2,1)} async-done(((bf16[1152,4608]{0,1:T(8,128)(2,1)}), bf16[1152,576]{0,1:T(8,128)(2,1)}) %reduce-scatter.55.cloned.1.call-update) | async-done | bytes 1327120 | tf_op jit(solution)/shard_map/reduce_scatter | solution.py:105
  1583.9 83.1 %reduce-scatter.53.cloned.1.call-done = bf16[1152,576]{0,1:T(8,128)(2,1)} async-done(((bf16[1152,4608]{0,1:T(8,128)(2,1)}), bf16[1152,576]{0,1:T(8,128)(2,1)}) %reduce-scatter.53.cloned.1.call-update) | async-done | bytes 1327120 | tf_op jit(solution)/shard_map/reduce_scatter | solution.py:105
  1669.7 83.0 %reduce-scatter.57.cloned.1.call-done = bf16[4608,144]{0,1:T(8,128)(2,1)} async-done(((bf16[4608,1152]{0,1:T(8,128)(2,1)}), bf16[4608,144]{0,1:T(8,128)(2,1)}) %reduce-scatter.57.cloned.1.call-update) | async-done | bytes 1327120 | tf_op jit(solution)/shard_map/reduce_scatter | solution.py:108
  1756.5 112.7 %reduce-scatter.43.cloned.1.call-done = bf16[1152,864]{0,1:T(8,128)(2,1)} async-done(((bf16[1152,6912]{0,1:T(8,128)(2,1)}), bf16[1152,864]{0,1:T(8,128)(2,1)}) %reduce-scatter.43.cloned.1.call-update) | async-done | bytes 1990672 | tf_op jit(solution)/shard_map/reduce_scatter | solution.py:96
  1873.4 112.7 %reduce-scatter.41.cloned.1.call-done = bf16[1152,864]{0,1:T(8,128)(2,1)} async-done(((bf16[1152,6912]{0,1:T(8,128)(2,1)}), bf16[1152,864]{0,1:T(8,128)(2,1)}) %reduce-scatter.41.cloned.1.call-update) | async-done | bytes 1990672 | tf_op jit(solution)/shard_map/reduce_scatter | solution.py:96
  1990.1 20.0 reduce-scatter.71.cloned.1.call-done
  2011.2 21.6 reduce-scatter.69.cloned.1.call-done
  2034.7 28.6 %reduce-scatter.67.cloned.1.call-done = bf16[288,432]{1,0:T(8,128)(2,1)} async-done(((bf16[1152,432]{1,0:T(8,128)(2,1)}), bf16[288,432]{1,0:T(8,128)(2,1)}) %reduce-scatter.67.cloned.1.call-update) | async-done | bytes 248848
  2064.4 29.5 %reduce-scatter.65.cloned.1.call-done = bf16[288,432]{1,0:T(8,128)(2,1)} async-done(((bf16[1152,432]{1,0:T(8,128)(2,1)}), bf16[288,432]{1,0:T(8,128)(2,1)}) %reduce-scatter.65.cloned.1.call-update) | async-done | bytes 248848
  2096.7 46.3 %reduce-scatter.79.cloned.1.call-done = bf16[1152,144]{1,0:T(8,128)(2,1)} async-done(((bf16[4608,144]{1,0:T(8,128)(2,1)}), bf16[1152,144]{1,0:T(8,128)(2,1)}) %reduce-scatter.79.cloned.1.call-update) | async-done | bytes 331792
  2144.3 34.9 %reduce-scatter.75.cloned.1.call-done = bf16[288,576]{1,0:T(8,128)(2,1)} async-done(((bf16[1152,576]{1,0:T(8,128)(2,1)}), bf16[288,576]{1,0:T(8,128)(2,1)}) %reduce-scatter.75.cloned.1.call-update) | async-done | bytes 331792
  2180.4 33.7 %reduce-scatter.73.cloned.1.call-done = bf16[288,576]{1,0:T(8,128)(2,1)} async-done(((bf16[1152,576]{1,0:T(8,128)(2,1)}), bf16[288,576]{1,0:T(8,128)(2,1)}) %reduce-scatter.73.cloned.1.call-update) | async-done | bytes 331792
  2217.2 46.2 %reduce-scatter.77.cloned.1.call-done = bf16[1152,144]{1,0:T(8,128)(2,1)} async-done(((bf16[4608,144]{1,0:T(8,128)(2,1)}), bf16[1152,144]{1,0:T(8,128)(2,1)}) %reduce-scatter.77.cloned.1.call-update) | async-done | bytes 331792
  2265.9 43.1 %reduce-scatter.63.cloned.1.call-done = bf16[288,864]{1,0:T(8,128)(2,1)} async-done(((bf16[1152,864]{1,0:T(8,128)(2,1)}), bf16[288,864]{1,0:T(8,128)(2,1)}) %reduce-scatter.63.cloned.1.call-update) | async-done | bytes 497680
  2310.4 43.4 %reduce-scatter.61.cloned.1.call-done = bf16[288,864]{1,0:T(8,128)(2,1)} async-done(((bf16[1152,864]{1,0:T(8,128)(2,1)}), bf16[288,864]{1,0:T(8,128)(2,1)}) %reduce-scatter.61.cloned.1.call-update) | async-done | bytes 497680
  (845 shorter events, 688.7 us)
Async XLA Ops:
  7.2 51.0 %all-gather.37.cloned.1.call-start = ((), (), s32[]{:S(2)}) async-start(), calls=%async_computation.30 | async-start | bytes 2580480 | tf_op jit(solution)/shard_map/all_gather | solution.py:79
  9.6 108.4 %all-gather.53.cloned.1.call-start = ((), (), s32[]{:S(2)}) async-start(), calls=%async_computation.38 | async-start | bytes 2580480 | tf_op jit(solution)/shard_map/all_gather | solution.py:79
  10.3 159.5 %all-gather.45.cloned.1.call-start = ((), (), s32[]{:S(2)}) async-start(), calls=%async_computation.34 | async-start | bytes 1843200 | tf_op jit(solution)/shard_map/all_gather | solution.py:82
  11.3 192.6 %all-gather.49.cloned.1.call-start = ((), (), s32[]{:S(2)}) async-start(), calls=%async_computation.36 | async-start | bytes 1658880 | tf_op jit(solution)/shard_map/all_gather | solution.py:83
  12.3 272.2 %all-gather.61.cloned.1.call-start = ((), (), s32[]{:S(2)}) async-start(), calls=%async_computation.42 | async-start | bytes 1843200 | tf_op jit(solution)/shard_map/all_gather | solution.py:82
  12.9 331.8 %all-gather.39.cloned.1.call-start = ((), (), s32[]{:S(2)}) async-start(), calls=%async_computation.31 | async-start | bytes 17915904 | tf_op jit(solution)/shard_map/all_gather | solution.py:86
  62.3 337.5 %all-gather.41.cloned.1.call-start = ((), (), s32[]{:S(2)}) async-start(), calls=%async_computation.32 | async-start | bytes 8957952 | tf_op jit(solution)/shard_map/all_gather | solution.py:87
  102.4 405.2 %all-gather.55.cloned.1.call-start = ((), (), s32[]{:S(2)}) async-start(), calls=%async_computation.39 | async-start | bytes 17915904 | tf_op jit(solution)/shard_map/all_gather | solution.py:86
  122.1 469.3 %all-gather.43.cloned.1.call-start = ((), (), s32[]{:S(2)}) async-start(), calls=%async_computation.33 | async-start | bytes 2985984 | tf_op jit(solution)/shard_map/all_gather | solution.py:88
  165.4 441.2 %all-gather.47.cloned.1.call-start = ((), (), s32[]{:S(2)}) async-start(), calls=%async_computation.35 | async-start | bytes 11943936 | tf_op jit(solution)/shard_map/all_gather | solution.py:89
  172.5 499.9 %all-gather.51.cloned.1.call-start = ((), (), s32[]{:S(2)}) async-start(), calls=%async_computation.37 | async-start | bytes 11943936 | tf_op jit(solution)/shard_map/all_gather | solution.py:90
  204.0 523.3 %all-gather.57.cloned.1.call-start = ((), (), s32[]{:S(2)}) async-start(), calls=%async_computation.40 | async-start | bytes 8957952 | tf_op jit(solution)/shard_map/all_gather | solution.py:87
  239.6 522.1 %all-gather.65.cloned.1.call-start = ((), (), s32[]{:S(2)}) async-start(), calls=%async_computation.44 | async-start | bytes 1658880 | tf_op jit(solution)/shard_map/all_gather | solution.py:83
  240.4 607.2 %all-gather.59.cloned.1.call-start = ((), (), s32[]{:S(2)}) async-start(), calls=%async_computation.41 | async-start | bytes 2985984 | tf_op jit(solution)/shard_map/all_gather | solution.py:88
  272.3 586.7 %all-gather.63.cloned.1.call-start = ((), (), s32[]{:S(2)}) async-start(), calls=%async_computation.43 | async-start | bytes 11943936 | tf_op jit(solution)/shard_map/all_gather | solution.py:89
  283.3 389.0 %copy-start.99 = (f32[256]{0:T(256)}, f32[256]{0:T(256)S(1)}, u32[]{:S(2)}) copy-start(f32[256]{0:T(256)S(1)} %get-tuple-element.696) | copy-start | bytes 3076
  284.4 223.2 %copy-start.65 = (bf16[8,1152]{1,0:T(8,128)(2,1)}, bf16[8,1152]{1,0:T(8,128)(2,1)S(1)}, u32[]{:S(2)}) copy-start(bf16[8,1152]{1,0:T(8,128)(2,1)S(1)} %multiply_convert_fusion.7) | copy-start | bytes 55300
  287.1 637.5 %all-gather.67.cloned.1.call-start = ((), (), s32[]{:S(2)}) async-start(), calls=%async_computation.45 | async-start | bytes 11943936 | tf_op jit(solution)/shard_map/all_gather | solution.py:90
  405.7 116.7 %collective-permute-start = (bf16[256,2304]{1,0:T(8,128)(2,1)S(1)}, bf16[256,2304]{1,0:T(8,128)(2,1)}, u32[]{:S(2)}, u32[]{:S(2)}) collective-permute-start(bf16[256,2304]{1,0:T(8,128)(2,1)S(1)} %concatenate.48), channel_id=1, source_target_pairs={{0,1},{1,2},{2,3},{3,4},{4,5},{5,6},{6,7},{8,9},{9,10},{10,11},{11... | collective-permute-start | bytes 3538952 | tf_op jit(solution)/shard_map/ppermute | solution.py:28
  408.9 113.5 %collective-permute-start.1 = (bf16[256,2304]{1,0:T(8,128)(2,1)S(1)}, bf16[256,2304]{1,0:T(8,128)(2,1)}, u32[]{:S(2)}, u32[]{:S(2)}) collective-permute-start(bf16[256,2304]{1,0:T(8,128)(2,1)S(1)} %concatenate.48), channel_id=1, source_target_pairs={{1,0},{2,1},{3,2},{4,3},{5,4},{6,5},{7,6},{9,8},{10,9},{11,10},{12... | collective-permute-start | bytes 3538952 | tf_op jit(solution)/shard_map/ppermute | solution.py:29
  681.7 165.9 %copy-start.8 = (f32[256,1152]{1,0:T(8,128)}, f32[256,1152]{1,0:T(8,128)S(1)}, u32[]{:S(2)}) copy-start(f32[256,1152]{1,0:T(8,128)S(1)} %get-tuple-element.644) | copy-start | bytes 3538948
  734.3 41.6 %collective-permute-start.2 = (bf16[256,2304]{1,0:T(8,128)(2,1)S(1)}, bf16[256,2304]{1,0:T(8,128)(2,1)}, u32[]{:S(2)}, u32[]{:S(2)}) collective-permute-start(bf16[256,2304]{1,0:T(8,128)(2,1)S(1)} %concatenate.49), channel_id=1, source_target_pairs={{0,1},{1,2},{2,3},{3,4},{4,5},{5,6},{6,7},{8,9},{9,10},{10,11},{11... | collective-permute-start | bytes 3538952 | tf_op jit(solution)/shard_map/ppermute | solution.py:28
  737.5 38.4 %collective-permute-start.3 = (bf16[256,2304]{1,0:T(8,128)(2,1)S(1)}, bf16[256,2304]{1,0:T(8,128)(2,1)}, u32[]{:S(2)}, u32[]{:S(2)}) collective-permute-start(bf16[256,2304]{1,0:T(8,128)(2,1)S(1)} %concatenate.49), channel_id=1, source_target_pairs={{1,0},{2,1},{3,2},{4,3},{5,4},{6,5},{7,6},{9,8},{10,9},{11,10},{12... | collective-permute-start | bytes 3538952 | tf_op jit(solution)/shard_map/ppermute | solution.py:29
  761.8 640.5 %reduce-scatter.51.cloned.1.call-start = ((), (), s32[]{:S(2)}) async-start(), calls=%async_computation.25 | async-start | bytes 2985984 | tf_op jit(solution)/shard_map/reduce_scatter | solution.py:102
  852.3 97.5 %copy-start.80 = (f32[256]{0:T(256)}, f32[256]{0:T(256)S(1)}, u32[]{:S(2)}) copy-start(f32[256]{0:T(256)S(1)} %fusion.240) | copy-start | bytes 3076
  1088.7 8.4 collective-permute-start.4
  1090.0 7.1 collective-permute-start.5
  1096.6 307.9 %reduce-scatter.49.cloned.1.call-start = ((), (), s32[]{:S(2)}) async-start(), calls=%async_computation.24 | async-start | bytes 2985984 | tf_op jit(solution)/shard_map/reduce_scatter | solution.py:102
  1135.6 271.0 %reduce-scatter.47.cloned.1.call-start = ((), (), s32[]{:S(2)}) async-start(), calls=%async_computation.23 | async-start | bytes 8957952 | tf_op jit(solution)/shard_map/reduce_scatter | solution.py:99
  1147.3 262.6 %reduce-scatter.45.cloned.1.call-start = ((), (), s32[]{:S(2)}) async-start(), calls=%async_computation.22 | async-start | bytes 8957952 | tf_op jit(solution)/shard_map/reduce_scatter | solution.py:99
  1278.6 22.5 collective-permute-start.6
  1280.2 23.1 collective-permute-start.7
  1311.4 184.2 %reduce-scatter.59.cloned.1.call-start = ((), (), s32[]{:S(2)}) async-start(), calls=%async_computation.29 | async-start | bytes 11943936 | tf_op jit(solution)/shard_map/reduce_scatter | solution.py:108
  1318.8 262.5 %reduce-scatter.55.cloned.1.call-start = ((), (), s32[]{:S(2)}) async-start(), calls=%async_computation.27 | async-start | bytes 11943936 | tf_op jit(solution)/shard_map/reduce_scatter | solution.py:105
  1326.5 340.6 %reduce-scatter.53.cloned.1.call-start = ((), (), s32[]{:S(2)}) async-start(), calls=%async_computation.26 | async-start | bytes 11943936 | tf_op jit(solution)/shard_map/reduce_scatter | solution.py:105
  1334.2 418.4 %reduce-scatter.57.cloned.1.call-start = ((), (), s32[]{:S(2)}) async-start(), calls=%async_computation.28 | async-start | bytes 11943936 | tf_op jit(solution)/shard_map/reduce_scatter | solution.py:108
  1341.6 527.6 %reduce-scatter.43.cloned.1.call-start = ((), (), s32[]{:S(2)}) async-start(), calls=%async_computation.21 | async-start | bytes 17915904 | tf_op jit(solution)/shard_map/reduce_scatter | solution.py:96
  1369.4 616.6 %reduce-scatter.41.cloned.1.call-start = ((), (), s32[]{:S(2)}) async-start(), calls=%async_computation.20 | async-start | bytes 17915904 | tf_op jit(solution)/shard_map/reduce_scatter | solution.py:96
  1402.2 607.9 %reduce-scatter.71.cloned.1.call-start = ((), (), s32[]{:S(2)}) async-start(), calls=%async_computation.51 | async-start | bytes 737280
  1404.4 628.4 %reduce-scatter.69.cloned.1.call-start = ((), (), s32[]{:S(2)}) async-start(), calls=%async_computation.50 | async-start | bytes 737280
  1406.5 656.7 %reduce-scatter.67.cloned.1.call-start = ((), (), s32[]{:S(2)}) async-start(), calls=%async_computation.49 | async-start | bytes 1474560
  1409.0 684.9 %reduce-scatter.65.cloned.1.call-start = ((), (), s32[]{:S(2)}) async-start(), calls=%async_computation.48 | async-start | bytes 1474560
  1412.2 730.8 %reduce-scatter.79.cloned.1.call-start = ((), (), s32[]{:S(2)}) async-start(), calls=%async_computation.55 | async-start | bytes 2949120
  1499.4 679.8 %reduce-scatter.75.cloned.1.call-start = ((), (), s32[]{:S(2)}) async-start(), calls=%async_computation.53 | async-start | bytes 1843200
  1583.9 630.3 %reduce-scatter.73.cloned.1.call-start = ((), (), s32[]{:S(2)}) async-start(), calls=%async_computation.52 | async-start | bytes 1843200
  1669.7 593.8 %reduce-scatter.77.cloned.1.call-start = ((), (), s32[]{:S(2)}) async-start(), calls=%async_computation.54 | async-start | bytes 2949120
  1756.5 552.5 %reduce-scatter.63.cloned.1.call-start = ((), (), s32[]{:S(2)}) async-start(), calls=%async_computation.47 | async-start | bytes 2580480
  1873.3 480.5 %reduce-scatter.61.cloned.1.call-start = ((), (), s32[]{:S(2)}) async-start(), calls=%async_computation.46 | async-start | bytes 2580480
  (112 other events, 1113.0 us)
Sparse Core Ops, SparseCore 0:
  10.2 47.9 all-gather.36
  60.3 57.6 all-gather.52
  120.1 49.7 all-gather.44
  171.9 32.0 all-gather.48
  206.0 52.1 all-gather.60
  260.5 84.1 all-gather.38
  347.2 52.5 all-gather.40
  401.7 105.9 all-gather.54
  510.1 30.2 all-gather.42
  542.7 63.8 all-gather.46
  608.5 63.8 all-gather.50
  674.7 52.5 all-gather.56
  728.9 32.8 all-gather.64
  763.5 29.3 all-gather.58
  795.2 63.8 all-gather.62
  860.8 63.8 all-gather.66
  1096.7 44.7 reduce-scatter.50
  1145.2 56.9 reduce-scatter.48
  1205.7 69.9 reduce-scatter.46
  1311.5 98.2 reduce-scatter.44
  1413.3 82.1 reduce-scatter.58
  1499.1 82.1 reduce-scatter.54
  1584.8 82.2 reduce-scatter.52
  1670.4 82.2 reduce-scatter.56
  1756.3 112.9 reduce-scatter.42
  1873.2 112.8 reduce-scatter.40
  1988.2 21.9 reduce-scatter.70
  2012.5 20.2 reduce-scatter.68
  2035.7 27.4 reduce-scatter.66
  2066.0 27.8 reduce-scatter.64
  2096.2 46.7 reduce-scatter.78
  2145.9 33.2 reduce-scatter.74
  2181.5 32.6 reduce-scatter.72
  2216.5 46.9 reduce-scatter.76
  2266.3 42.6 reduce-scatter.62
  2311.3 42.4 reduce-scatter.60
where the time goes:
time: 2380 us; the launch traced here: 2370 us
  waiting for transfers between devices  1380 us (58%)
  matrix products  545 us (23%)
  local copies, waits for them, and re-layouts  189 us (8%)
  blocking collectives  142 us (6%)
  other arithmetic  53.4 us (2%)
  starting transfers between devices  40.3 us (2%)
    unnamed x46, waiting for transfers between devices  350 us
    reduce_scatter x2, waiting for transfers between devices, reduce_grads(): lax.psum_scatter(grads[0].astype(jnp.bfloat16), 'seq', scatter_dimension=...  225 us
    dot_general x104, matrix products, against_cols(): lax.dot_general(left, right, (((1,), (1,)), ((), ())), preferred_element_...  181 us
    dot_general x76, matrix products, through_rows(): lax.dot_general(left, right, (((0,), (0,)), ((), ())), precision=precisio...  169 us
    reduce_scatter x2, waiting for transfers between devices, reduce_grads(): lax.psum_scatter(grads[4].astype(jnp.bfloat16), 'seq', scatter_dimension=...  166 us
    reduce_scatter x2, waiting for transfers between devices, reduce_grads(): lax.psum_scatter(grads[3].astype(jnp.bfloat16), 'seq', scatter_dimension=...  165 us
    all_gather x2, waiting for transfers between devices, fetch(): lax.all_gather(rows_whole[0], 'seq', axis=1, tiled=True)  153 us
    all_gather x2, waiting for transfers between devices, fetch(): lax.all_gather(rows_whole[4], 'seq', axis=1, tiled=True)  105 us
  transfers between devices with their start and end apart: 44, of which 32 were waited for; matrix products, arithmetic and copies ran while one was open for 25% of the time, Pallas kernels for 0%

commit v1 on v0

v1 whole, which is shorter than its diff:
```python
import functools
import math

import jax
import jax.numpy as jnp
import numpy as np
from jax import lax
from jax.experimental import pallas as pl
from jax.experimental.pallas import tpu as pltpu
from jax.sharding import PartitionSpec as P

D = 1152
HEADS = 16
HEAD_DIM = 72
FF = 4608
GROUPS = 16
LAYERS = 2

TP = 4
LANES = 128
LOCAL_HEADS = HEADS // TP
WIDTH = -(-LOCAL_HEADS * HEAD_DIM // LANES) * LANES
AFTER = 128

EPS = 1e-06
HIGH = lax.Precision.HIGHEST
NEGATIVE = -1e30
FACTOR = HEAD_DIM ** (-0.5)
F32 = jnp.float32
BF16 = jnp.bfloat16


def sizes():
    seq = lax.axis_size("seq")
    return seq, seq // TP, lax.axis_size("dp")


def place():
    s = lax.axis_index("seq")
    return s // TP, s % TP


def device_of(unit, groups):
    return (unit % groups) * TP + unit // groups


def unit_table(seq, groups):
    return np.array([(s % TP) * groups + s // TP for s in range(seq)])


def my_unit():
    seq, groups, _ = sizes()
    group, member = place()
    return member * groups + group


def exchange(value, mask):
    seq = lax.axis_size("seq")
    return lax.ppermute(value, "seq", [(i, i ^ mask) for i in range(seq)])


def shifted(value, steps):
    count = lax.axis_size("seq")
    return lax.ppermute(
        value, "seq", [(i, i + steps) for i in range(count) if 0 <= i + steps < count]
    )


def dot(left, right):
    return jnp.dot(left, right, preferred_element_type=F32)


def through_rows(left, right):
    return lax.dot_general(left, right, (((0,), (0,)), ((), ())), preferred_element_type=F32)


def against_cols(left, right):
    return lax.dot_general(left, right, (((1,), (1,)), ((), ())), preferred_element_type=F32)


def spread(mine):
    _, member = place()
    got = {0: mine}
    for mask in range(2, TP, 2):
        got[mask] = exchange(mine, mask)
    for mask in range(0, TP, 2):
        got[mask + 1] = exchange(got[mask], 1)
    whole = jnp.zeros((TP,) + mine.shape, mine.dtype)
    for mask in range(TP):
        whole = lax.dynamic_update_index_in_dim(whole, got[mask], member ^ mask, 0)
    return whole.reshape((TP * mine.shape[0],) + mine.shape[1:])


def collect(parts):
    _, member = place()
    parts = parts.reshape((TP, parts.shape[0] // TP) + parts.shape[1:])

    def pick(mask):
        return lax.dynamic_index_in_dim(parts, member ^ mask, 0, keepdims=False)

    total = None
    for mask in reversed(range(0, TP, 2)):
        pair = pick(mask).astype(F32) + exchange(pick(mask + 1), 1).astype(F32)
        if mask:
            pair = exchange(pair.astype(BF16), mask).astype(F32)
        total = pair if total is None else total + pair
    return total


def kinds_of():
    seq, groups, _ = sizes()
    units = unit_table(seq, groups)
    pairs, kinds = [], np.zeros((3, seq), np.int32)
    for r in range(3):
        targets = [device_of((3 * s + r) % seq, groups) for s in range(seq)]
        pairs.append(list(enumerate(targets)))
        for s in range(seq):
            kinds[r, targets[s]] = (3 * s + r) // seq
    return pairs, jnp.asarray(kinds)[:, lax.axis_index("seq")]


def deal_joint(part):
    pairs, kinds = kinds_of()
    cols = part.shape[-1] // 3
    got = [
        lax.ppermute(part[..., r * cols : (r + 1) * cols], "seq", pairs[r]) for r in range(3)
    ]
    out = []
    for kind in range(3):
        out.append(
            jnp.where(kinds[0] == kind, got[0], jnp.where(kinds[1] == kind, got[1], got[2]))
        )
    return jnp.concatenate(out, axis=-1)


def return_joint(grad):
    pairs, kinds = kinds_of()
    cols = grad.shape[-1] // 3
    own = [grad[..., k * cols : (k + 1) * cols] for k in range(3)]
    back = []
    for r in range(3):
        piece = jnp.where(kinds[r] == 0, own[0], jnp.where(kinds[r] == 1, own[1], own[2]))
        back.append(lax.ppermute(piece, "seq", [(b, a) for a, b in pairs[r]]))
    return jnp.concatenate(back, axis=-1)


def expand_pairs(step):
    seq, groups, planes = sizes()
    ways = seq // planes
    pairs = []
    for s in range(seq):
        q = (s // ways + step) % planes
        pairs.append((s, device_of(planes * (s % ways) + q, groups)))
    return pairs


def deal_expand(part):
    seq, _, planes = sizes()
    ways = seq // planes
    cols = part.shape[-1] // planes
    s = lax.axis_index("seq")
    q_mine = my_unit() % planes
    out = jnp.zeros((planes,) + part.shape[:-1] + (cols,), part.dtype)
    blocks = jnp.stack([part[..., q * cols : (q + 1) * cols] for q in range(planes)])
    for step in range(planes):
        piece = lax.dynamic_index_in_dim(blocks, (s // ways + step) % planes, 0, keepdims=False)
        piece = lax.ppermute(piece, "seq", expand_pairs(step))
        out = lax.dynamic_update_index_in_dim(out, piece, (q_mine - step) % planes, 0)
    return jnp.concatenate([out[d] for d in range(planes)], axis=-1)


def return_expand(grad):
    seq, _, planes = sizes()
    ways = seq // planes
    cols = grad.shape[-1] // planes
    s = lax.axis_index("seq")
    q_mine = my_unit() % planes
    blocks = jnp.stack([grad[..., d * cols : (d + 1) * cols] for d in range(planes)])
    out = jnp.zeros_like(blocks)
    for step in range(planes):
        piece = lax.dynamic_index_in_dim(blocks, (q_mine - step) % planes, 0, keepdims=False)
        piece = lax.ppermute(piece, "seq", [(b, a) for a, b in expand_pairs(step)])
        out = lax.dynamic_update_index_in_dim(out, piece, (s // ways + step) % planes, 0)
    return jnp.concatenate([out[q] for q in range(planes)], axis=-1)


def deal_rows(part):
    seq, groups, _ = sizes()
    rows = part.shape[0] // seq
    chunks = part.reshape(TP, groups, rows, part.shape[1]).transpose(1, 0, 2, 3)
    chunks = lax.all_to_all(
        chunks.reshape(seq, rows, part.shape[1]), "seq", 0, 0, tiled=True
    )
    return jnp.concatenate([chunks[s] for s in range(seq)], axis=-1)


def return_rows(grad):
    seq, groups, _ = sizes()
    rows, cols = grad.shape[0], grad.shape[1] // seq
    chunks = jnp.stack([grad[:, s * cols : (s + 1) * cols] for s in range(seq)])
    chunks = lax.all_to_all(chunks, "seq", 0, 0, tiled=True)
    chunks = chunks.reshape(groups, TP, rows, cols).transpose(1, 0, 2, 3)
    return chunks.reshape(seq * rows, cols)


def fold(part, cols):
    return jnp.concatenate(
        [part[:, k * cols : (k + 1) * cols] for k in range(part.shape[1] // cols)], axis=0
    )


def unfold(part, rows):
    return jnp.concatenate(
        [part[k * rows : (k + 1) * rows] for k in range(part.shape[0] // rows)], axis=1
    )


def ordered(pieces):
    if len(pieces) != 2:
        return pieces
    group, _ = place()
    first, second = pieces
    return [jnp.where(group == 0, first, second), jnp.where(group == 0, second, first)]


def over_groups(part):
    seq, groups, _ = sizes()
    if groups == 1:
        return [part]
    if groups == 2:
        return [part, exchange(part, TP)]
    teams = [[g * TP + t for g in range(groups)] for t in range(TP)]
    every = lax.all_gather(part, "seq", axis_index_groups=teams)
    return [every[g] for g in range(groups)]


def group_sum(pieces):
    seq, groups, _ = sizes()
    if groups == 1:
        return pieces[0]
    if groups == 2:
        return pieces[0] + exchange(pieces[1].astype(BF16), TP).astype(F32)
    teams = [[g * TP + t for g in range(groups)] for t in range(TP)]
    stacked = jnp.stack([piece.astype(BF16) for piece in pieces])
    return lax.psum_scatter(
        stacked, "seq", scatter_dimension=0, axis_index_groups=teams, tiled=False
    ).astype(F32)


def slot_units():
    seq, groups, _ = sizes()
    group, member = place()
    if groups == 2:
        return [member * 2 + group, member * 2 + 1 - group]
    return [member * groups + g for g in range(groups)]


def over_planes(part):
    return lax.all_gather(part, "dp", axis=0, tiled=False)


def attention_weights(packed):
    seq, _, planes = sizes()
    cols = D // seq
    joint = ordered(over_groups(packed[:, :, : 3 * cols].reshape(D, 3 * cols)))
    project = ordered(over_groups(deal_rows(packed[:, :, 3 * cols :].reshape(D, cols))))
    blank = jnp.zeros((D, WIDTH - LOCAL_HEADS * HEAD_DIM), BF16)
    columns = []
    for kind in range(3):
        columns += [piece[:, kind * cols : (kind + 1) * cols] for piece in joint] + [blank]
    return (
        jnp.concatenate(columns, axis=1),
        jnp.concatenate(project + [blank.T], axis=0),
    )


def forward_weights(packed):
    seq, _, planes = sizes()
    height, width = D // planes, FF // seq
    expand = over_groups(packed[:, :height].reshape(D, width))
    rows = FF // (planes * seq)
    reduce = jnp.concatenate([unfold(packed[d, height:], rows) for d in range(planes)], axis=0)
    reduce = over_groups(reduce)
    return jnp.concatenate(expand, axis=1), jnp.concatenate(reduce, axis=0)


def head_tiles(head):
    low = head * HEAD_DIM // LANES * LANES
    high = -(-(head + 1) * HEAD_DIM // LANES) * LANES
    return low, high


def lanes_of(head, shape):
    low, high = head_tiles(head)
    lane = lax.broadcasted_iota(jnp.int32, shape, 1) + low
    return (lane >= head * HEAD_DIM) & (lane < (head + 1) * HEAD_DIM)


def attend_kernel(block, span, q_ref, kv_ref, segq_ref, segk_ref, head_ref, mixed_ref, lse_ref):
    window = pl.ds(pl.multiple_of(pl.program_id(0) * block, block), span)
    allowed = segq_ref[...] == segk_ref[0]
    tiles = [jnp.zeros((block, LANES), F32) for _ in range(WIDTH // LANES)]
    total = jnp.zeros((block, LANES), F32)
    lane = lax.broadcasted_iota(jnp.int32, (block, LANES), 1)
    for head in range(LOCAL_HEADS):
        low, high = head_tiles(head)
        mine = lanes_of(head, (block, high - low))
        query = jnp.where(mine, q_ref[:, low:high], 0)
        scores = against_cols(query, kv_ref[window, low:high]) * FACTOR
        scores = jnp.where(allowed, scores, NEGATIVE)
        highest = jnp.max(scores, axis=-1, keepdims=True)
        weights = jnp.exp(scores - highest)
        sums = jnp.sum(weights, axis=-1, keepdims=True)
        probs = (weights / sums).astype(BF16)
        out = dot(probs, kv_ref[window, WIDTH + low : WIDTH + high])
        out = jnp.where(mine, out, 0.0) * head_ref[:, head : head + 1]
        for k in range(low // LANES, high // LANES):
            at = k * LANES - low
            tiles[k] = tiles[k] + out[:, at : at + LANES]
        total = jnp.where(lane == head, highest + jnp.log(sums), total)
    for k, tile in enumerate(tiles):
        mixed_ref[:, k * LANES : (k + 1) * LANES] = tile.astype(BF16)
    lse_ref[...] = total


def attend_back_kernel(
    block,
    span,
    q_ref,
    kv_ref,
    grad_ref,
    mixed_ref,
    lse_ref,
    segq_ref,
    segk_ref,
    head_ref,
    dq_ref,
    dkv_ref,
    sum_ref,
):
    step = pl.program_id(0)

    @pl.when(step == 0)
    def _():
        sum_ref[...] = jnp.zeros_like(sum_ref)

    window = pl.ds(pl.multiple_of(step * block, block), span)
    allowed = segq_ref[...] == segk_ref[0]
    tiles = [jnp.zeros((block, LANES), F32) for _ in range(WIDTH // LANES)]
    for head in range(LOCAL_HEADS):
        low, high = head_tiles(head)
        mine = lanes_of(head, (block, high - low))
        query = jnp.where(mine, q_ref[:, low:high], 0)
        key = kv_ref[window, low:high]
        value = kv_ref[window, WIDTH + low : WIDTH + high]
        active = head_ref[:, head : head + 1]
        grad = jnp.where(mine, grad_ref[:, low:high].astype(F32) * active, 0.0)
        balance = jnp.sum(grad * mixed_ref[:, low:high].astype(F32), axis=-1, keepdims=True)
        grad = grad.astype(BF16)
        scores = against_cols(query, key) * FACTOR
        probs = jnp.where(allowed, jnp.exp(scores - lse_ref[:, head : head + 1]), 0.0)
        d_value = through_rows(probs.astype(BF16), grad)
        d_probs = against_cols(grad, value)
        d_scores = (probs * (d_probs - balance)).astype(BF16)
        d_query = jnp.where(mine, dot(d_scores, key), 0.0)
        d_key = through_rows(d_scores, query) * FACTOR
        sum_ref[window, low:high] += d_key
        sum_ref[window, WIDTH + low : WIDTH + high] += d_value
        for k in range(low // LANES, high // LANES):
            at = k * LANES - low
            tiles[k] = tiles[k] + d_query[:, at : at + LANES]
    for k, tile in enumerate(tiles):
        dq_ref[:, k * LANES : (k + 1) * LANES] = (tile * FACTOR).astype(BF16)

    @pl.when(step == pl.num_programs(0) - 1)
    def _():
        dkv_ref[...] = sum_ref[...].astype(BF16)


def kernel_params():
    return pltpu.CompilerParams(
        dimension_semantics=("arbitrary",), vmem_limit_bytes=48 * 1024 * 1024
    )


def attend(joint, pairs, segq, segk, heads):
    span = segk.shape[2]
    count = joint.shape[0]
    block = count // segk.shape[0]
    rows = lambda width: pl.BlockSpec((block, width), lambda b: (b, 0))
    whole = lambda array: pl.BlockSpec(array.shape, lambda b: (0, 0))
    return pl.pallas_call(
        functools.partial(attend_kernel, block, span),
        grid=(count // block,),
        in_specs=[
            rows(WIDTH),
            whole(pairs),
            rows(1),
            pl.BlockSpec((1, 1, span), lambda b: (b, 0, 0)),
            rows(LANES),
        ],
        out_specs=[rows(WIDTH), rows(LANES)],
        out_shape=[
            jax.ShapeDtypeStruct((count, WIDTH), BF16),
            jax.ShapeDtypeStruct((count, LANES), F32),
        ],
        compiler_params=kernel_params(),
        cost_estimate=pl.CostEstimate(
            flops=4 * count * span * LANES * LOCAL_HEADS,
            bytes_accessed=count * WIDTH * 8,
            transcendentals=count * span * LOCAL_HEADS,
        ),
        name="attend",
    )(joint, pairs, segq, segk, heads)


def attend_back(joint, pairs, grad, mixed, log_total, segq, segk, heads):
    span = segk.shape[2]
    count = joint.shape[0]
    block = count // segk.shape[0]
    rows = lambda width: pl.BlockSpec((block, width), lambda b: (b, 0))
    whole = lambda shape: pl.BlockSpec(shape, lambda b: (0, 0))
    return pl.pallas_call(
        functools.partial(attend_back_kernel, block, span),
        grid=(count // block,),
        in_specs=[
            rows(WIDTH),
            whole(pairs.shape),
            rows(WIDTH),
            rows(WIDTH),
            rows(LANES),
            rows(1),
            pl.BlockSpec((1, 1, span), lambda b: (b, 0, 0)),
            rows(LANES),
        ],
        out_specs=[rows(WIDTH), whole(pairs.shape)],
        out_shape=[
            jax.ShapeDtypeStruct((count, WIDTH), BF16),
            jax.ShapeDtypeStruct(pairs.shape, BF16),
        ],
        scratch_shapes=[pltpu.VMEM(pairs.shape, F32)],
        compiler_params=kernel_params(),
        cost_estimate=pl.CostEstimate(
            flops=10 * count * span * LANES * LOCAL_HEADS,
            bytes_accessed=count * WIDTH * 20,
            transcendentals=count * span * LOCAL_HEADS,
        ),
        name="attend_back",
    )(joint, pairs, grad, mixed, log_total, segq, segk, heads)


def with_halo(pairs, block):
    _, groups, _ = sizes()
    if groups == 1:
        before = jnp.zeros((block, pairs.shape[1]), pairs.dtype)
        after = jnp.zeros((AFTER, pairs.shape[1]), pairs.dtype)
    else:
        before = shifted(pairs[-block:], TP)
        after = shifted(pairs[:AFTER], -TP)
    return jnp.concatenate([before, pairs, after], axis=0)


def halo_back(d_pairs, block):
    _, groups, _ = sizes()
    own = d_pairs[block:-AFTER]
    if groups == 1:
        return own
    from_above = shifted(d_pairs[:block], -TP).astype(F32)
    from_below = shifted(d_pairs[-AFTER:], TP).astype(F32)
    count = own.shape[0]
    top = (own[:AFTER].astype(F32) + from_below).astype(BF16)
    bottom = (own[-block:].astype(F32) + from_above).astype(BF16)
    return jnp.concatenate([top, own[AFTER : count - block], bottom], axis=0)


def normed(stream):
    center = stream - jnp.mean(stream, axis=-1, keepdims=True)
    scale = lax.rsqrt(jnp.mean(center * center, axis=-1, keepdims=True) + EPS)
    return center * scale, scale


def norm_back(grad, unit, scale):
    mean = jnp.mean(grad, axis=-1, keepdims=True)
    slope = jnp.mean(grad * unit, axis=-1, keepdims=True)
    return scale * (grad - mean - unit * slope)


def per_token(vectors, sides):
    return sides[0] * vectors[0][None, :] + sides[1] * vectors[1][None, :]


def per_crop(value, sides):
    return jnp.stack([jnp.sum(value * sides[0], axis=0), jnp.sum(value * sides[1], axis=0)])


def step_embed(stamps, breadth):
    halfway = breadth // 2
    frequency = jnp.exp(-math.log(10000.0) * jnp.arange(halfway, dtype=F32) / halfway)
    angles = stamps.astype(F32)[..., None] * frequency
    return jnp.concatenate([jnp.cos(angles), jnp.sin(angles)], axis=-1)


def segment_of(places, bounds):
    return jnp.sum((places[:, None] >= bounds[None, :]).astype(jnp.int32), axis=-1)


def gelu_slope(value):
    root = math.sqrt(2.0 / math.pi)
    inner = root * (value + 0.044715 * value * value * value)
    curve = jnp.tanh(inner)
    slope = root * (1.0 + 3 * 0.044715 * value * value)
    return 0.5 * (1.0 + curve) + 0.5 * value * (1.0 - curve * curve) * slope


def layer_forward(stream, mod, weights, masks, context):
    w_joint, w_project, w_expand, w_reduce = weights
    head_tok, channel_tok, keeping = masks
    sides, living, segq, segk, block = context
    offset_one, stretch_one, gate_one, offset_two, stretch_two, gate_two = [
        per_token(mod[:, i], sides) for i in range(6)
    ]
    unit_one, _ = normed(stream)
    normed_one = spread((unit_one * (1.0 + stretch_one) + offset_one).astype(BF16))
    joint = dot(normed_one, w_joint).astype(BF16)
    pairs = with_halo(joint[:, WIDTH:], block)
    mixed, log_total = attend(joint, pairs, segq, segk, head_tok)
    branch = collect(dot(mixed, w_project).astype(BF16))
    middle = stream + gate_one * branch * living
    unit_two, _ = normed(middle)
    normed_two = spread((unit_two * (1.0 + stretch_two) + offset_two).astype(BF16))
    pre_act = dot(normed_two, w_expand)
    activated = (jax.nn.gelu(pre_act, approximate=True) * channel_tok).astype(BF16)
    feedout = collect(dot(activated, w_reduce).astype(BF16))
    result = middle + gate_two * feedout * keeping
    record = (
        stream,
        normed_one,
        joint,
        pairs,
        mixed,
        log_total,
        branch,
        middle,
        normed_two,
        pre_act.astype(BF16),
        activated,
        feedout,
    )
    return result, record


def layer_backward(adjoint, record, mod, weights, masks, context):
    (
        stream,
        normed_one,
        joint,
        pairs,
        mixed,
        log_total,
        branch,
        middle,
        normed_two,
        pre_act,
        activated,
        feedout,
    ) = record
    w_joint, w_project, w_expand, w_reduce = weights
    head_tok, channel_tok, keeping = masks
    sides, living, segq, segk, block = context
    offset_one, stretch_one, gate_one, offset_two, stretch_two, gate_two = [
        per_token(mod[:, i], sides) for i in range(6)
    ]
    d_feed = spread((adjoint * gate_two * keeping).astype(BF16))
    d_gate_two = per_crop(adjoint * feedout * keeping, sides)
    d_active = against_cols(d_feed, w_reduce)
    d_pre = (gelu_slope(pre_act.astype(F32)) * channel_tok * d_active).astype(BF16)
    d_normed_two = collect(against_cols(d_pre, w_expand).astype(BF16))
    g_reduce = through_rows(activated, d_feed)
    g_expand = through_rows(normed_two, d_pre)
    unit_two, scale_two = normed(middle)
    d_middle = adjoint + norm_back(d_normed_two * (1.0 + stretch_two), unit_two, scale_two)
    d_offset_two = per_crop(d_normed_two, sides)
    d_stretch_two = per_crop(d_normed_two * unit_two, sides)
    d_branch = spread((d_middle * gate_one * living).astype(BF16))
    d_gate_one = per_crop(d_middle * branch * living, sides)
    d_mixed = against_cols(d_branch, w_project).astype(BF16)
    g_project = through_rows(mixed, d_branch)
    d_query, d_pairs = attend_back(joint, pairs, d_mixed, mixed, log_total, segq, segk, head_tok)
    d_joint = jnp.concatenate([d_query, halo_back(d_pairs, block)], axis=-1)
    d_normed_one = collect(against_cols(d_joint, w_joint).astype(BF16))
    g_joint = through_rows(normed_one, d_joint)
    unit_one, scale_one = normed(stream)
    d_stream = d_middle + norm_back(d_normed_one * (1.0 + stretch_one), unit_one, scale_one)
    d_offset_one = per_crop(d_normed_one, sides)
    d_stretch_one = per_crop(d_normed_one * unit_one, sides)
    d_mod = jnp.stack(
        [d_offset_one, d_stretch_one, d_gate_one, d_offset_two, d_stretch_two, d_gate_two], axis=1
    )
    return d_stream, d_mod, (g_joint, g_project, g_expand, g_reduce)


def attention_grads(g_joint, g_project):
    seq, groups, planes = sizes()
    cols = D // seq
    joint = [
        jnp.concatenate(
            [
                g_joint[:, kind * WIDTH + slot * cols : kind * WIDTH + (slot + 1) * cols]
                for kind in range(3)
            ],
            axis=1,
        )
        for slot in range(groups)
    ]
    project = [g_project[slot * cols : (slot + 1) * cols] for slot in range(groups)]
    joint, project = group_sum(ordered(joint)), group_sum(ordered(project))
    project = return_rows(project.astype(BF16))
    packed = jnp.concatenate([joint.astype(BF16), project], axis=1)
    owned = lax.psum_scatter(packed, "dp", scatter_dimension=0, tiled=True)
    return return_joint(owned[:, : 3 * cols]).astype(F32), owned[:, 3 * cols :].astype(F32)


def forward_grads(g_expand, g_reduce):
    seq, groups, planes = sizes()
    width = FF // seq
    expand = group_sum([g_expand[:, slot * width : (slot + 1) * width] for slot in range(groups)])
    reduce = group_sum([g_reduce[slot * width : (slot + 1) * width] for slot in range(groups)])
    height, rows = D // planes, width // planes
    expand = expand.astype(BF16).reshape(planes, height, width)
    reduce = reduce.astype(BF16)
    reduce = jnp.stack([fold(reduce[d * rows : (d + 1) * rows], width) for d in range(planes)])
    packed = jnp.concatenate([expand, reduce], axis=1)
    owned = lax.psum_scatter(packed, "dp", scatter_dimension=0, tiled=False)
    return (
        return_expand(owned[:height]).astype(F32),
        return_rows(unfold(owned[height:], rows)).astype(F32),
    )


def shards(
    hidden_in,
    lengths,
    timesteps,
    head_mask,
    group_mask,
    skip_mask,
    modulation_weight,
    joint_weight,
    project_weight,
    expand_weight,
    reduce_weight,
    cotangent,
):
    seq, groups, planes = sizes()
    block = hidden_in.shape[1]
    crops = lengths.shape[1]
    mine = lax.axis_index("seq")
    plane = lax.axis_index("dp")
    group, member = place()
    both = ("dp", "seq")

    attention_packs = [
        jnp.concatenate([deal_joint(joint_weight[l]), project_weight[l]], axis=1)
        for l in range(LAYERS)
    ]
    forward_packs = [
        jnp.concatenate(
            [deal_expand(expand_weight[l]), fold(deal_rows(reduce_weight[l]), FF // seq)], axis=0
        )
        for l in range(LAYERS)
    ]
    height = D // planes
    gathered = [
        over_planes(attention_packs[0]),
        over_planes(forward_packs[0]),
        over_planes(jnp.concatenate([attention_packs[1], forward_packs[1]], axis=0)),
    ]
    weights = [
        attention_weights(gathered[0]) + forward_weights(gathered[1]),
        attention_weights(gathered[2][:, :height]) + forward_weights(gathered[2][:, height:]),
    ]

    stamps = lax.all_gather(timesteps[0], "dp", axis=0, tiled=True)
    embedded = jax.nn.silu(step_embed(stamps, D)).astype(BF16)
    condition = lax.dynamic_slice_in_dim(embedded, plane * height, height, axis=1)
    part = jnp.stack([dot(condition, modulation_weight[l]) for l in range(LAYERS)], axis=1)
    part = lax.all_to_all(part, both, 0, 0, tiled=True)
    part = jnp.sum(part.reshape((planes, seq) + part.shape[1:]), axis=0)
    mod_here = jnp.transpose(part, (1, 0, 2)).reshape(LAYERS, 6, D)
    mod_before = shifted(mod_here, 1)
    mods = jnp.stack([mod_before, mod_here], axis=1)

    bounds = jnp.cumsum(lengths[0])
    first = group * TP * block
    span = 2 * block + AFTER
    places = first - block + jnp.arange((TP + 1) * block + AFTER, dtype=jnp.int32)
    inside = (places >= 0) & (places < seq * block)
    segment = jnp.where(inside, segment_of(places, bounds), -1)
    segq = segment[block : (TP + 1) * block][:, None]
    segk = jnp.stack([segment[b * block : b * block + span] for b in range(TP)])[:, None, :]
    own = segment_of(mine * block + jnp.arange(block, dtype=jnp.int32), bounds)[:, None]
    sides = [(own == mine - 1).astype(F32), ((own == mine) & (own < crops)).astype(F32)]
    living = (own < crops).astype(F32)
    onehot = (segq == jnp.arange(crops, dtype=jnp.int32)[None, :]).astype(BF16)
    units = slot_units()
    heads_here = member * LOCAL_HEADS + jnp.arange(LOCAL_HEADS, dtype=jnp.int32)
    rows = FF // (planes * seq)
    within = jnp.arange(rows, dtype=jnp.int32)
    hidden_here = jnp.concatenate(
        [(FF // planes) * d + rows * unit + within for unit in units for d in range(planes)]
    )
    groups_here = hidden_here // (FF // GROUPS)
    context = (sides, living, segq, segk, block)
    masks = []
    for l in range(LAYERS):
        heads_on = jnp.take(head_mask[0, l], heads_here, axis=1).astype(BF16)
        heads_on = jnp.pad(heads_on, ((0, 0), (0, LANES - LOCAL_HEADS)))
        groups_on = jnp.take(group_mask[0, l], groups_here, axis=1).astype(BF16)
        masks.append(
            (
                dot(onehot, heads_on),
                dot(onehot, groups_on).astype(BF16),
                skip_mask[0, l].astype(F32)[:, None] * living,
            )
        )

    stream = hidden_in[0].astype(F32)
    records = []
    for l in range(LAYERS):
        stream, record = layer_forward(stream, mods[l], weights[l], masks[l], context)
        records.append(record)
    final_state = stream.astype(BF16)[None]
    adjoint = cotangent[0].astype(F32)
    owned, d_mods = [None] * LAYERS, [None] * LAYERS
    for l in reversed(range(LAYERS)):
        adjoint, d_mods[l], grads = layer_backward(
            adjoint, records[l], mods[l], weights[l], masks[l], context
        )
        owned[l] = attention_grads(*grads[:2]) + forward_grads(*grads[2:])

    d_mod = jnp.stack(d_mods, axis=1)
    d_mod = d_mod[1] + shifted(d_mod[0], -1)
    d_mod = jnp.transpose(d_mod.reshape(LAYERS, seq, 6 * D // seq), (1, 0, 2))
    d_mod = jnp.broadcast_to(d_mod[None], (planes,) + d_mod.shape)
    d_mod = d_mod.reshape((planes * seq,) + d_mod.shape[2:])
    d_mod = lax.all_to_all(d_mod, both, 0, 0, tiled=True)
    modulation_grad = jnp.stack(
        [
            lax.dot_general(
                condition.astype(F32),
                d_mod[:, l],
                (((0,), (0,)), ((), ())),
                precision=HIGH,
                preferred_element_type=F32,
            )
            for l in range(LAYERS)
        ]
    )
    joint_grad, project_grad, expand_grad, reduce_grad = [
        jnp.stack([owned[l][i] for l in range(LAYERS)]) for i in range(4)
    ]
    return (
        final_state,
        adjoint[None],
        modulation_grad,
        joint_grad,
        project_grad,
        expand_grad,
        reduce_grad,
    )


def solution(mesh):
    in_specs = (
        P("dp", "seq", None),
        P("dp", None),
        P("dp", None),
        P("dp", None, None, None),
        P("dp", None, None, None),
        P("dp", None, "seq"),
        P(None, "dp", "seq"),
        P(None, "dp", "seq"),
        P(None, "dp", "seq"),
        P(None, "dp", "seq"),
        P(None, "dp", "seq"),
        P("dp", "seq", None),
    )
    out_specs = (
        P("dp", "seq", None),
        P("dp", "seq", None),
        P(None, "dp", "seq"),
        P(None, "dp", "seq"),
        P(None, "dp", "seq"),
        P(None, "dp", "seq"),
        P(None, "dp", "seq"),
    )
    return jax.shard_map(shards, mesh=mesh, in_specs=in_specs, out_specs=out_specs, check_vma=False)
```

time: 2380 us -> 1020 us (0.43)
  waiting for transfers between devices: 1380 us -> 290 us
  matrix products: 545 us -> 115 us
  starting transfers between devices: 40.3 us -> 183 us
  blocking collectives: 142 us -> 8.44 us
  other arithmetic: 53.4 us -> 128 us
  Pallas kernels: 0 us -> 48.2 us
  local copies, waits for them, and re-layouts: 189 us -> 214 us
    reduce_scatter x10 -> x4, waiting for transfers between devices: 557 us -> 0.04 us  [the longest x2 0.02 us: forward_grads(): owned = lax.psum_scatter(packed, 'dp', scatter_dimension=0, tiled=False)]
    all_gather x16 -> x3, waiting for transfers between devices: 469 us -> 0.01 us  [over_planes(): return lax.all_gather(part, 'dp', axis=0, tiled=False)]
    unnamed x46 -> x7, waiting for transfers between devices: 350 us -> 0.11 us
    dot_general x156 -> x24, matrix products: 364 us -> 74.8 us  [the longest x14 39.5 us: dot(): return jnp.dot(left, right, preferred_element_type=F32)]
    ppermute x8 -> x102, waiting for transfers between devices: 2.4 us -> 238 us  [the longest x64 169 us: exchange(): return lax.ppermute(value, 'seq', [(i, i ^ mask) for i in range(seq)])]
    all_gather x4 -> x0, blocking collectives: 142 us -> none  [the longest x2 72.6 us: fetch(): lax.all_gather(joint_part, 'dp', axis=0, tiled=True)]
    dot_general x104 -> x8, matrix products: 181 us -> 40 us  [against_cols(): lax.dot_general(left, right, (((1,), (1,)), ((), ())), preferred_element_...]
    ppermute x8 -> x102, starting transfers between devices: 37.1 us -> 139 us  [the longest x64 50.4 us: exchange(): return lax.ppermute(value, 'seq', [(i, i ^ mask) for i in range(seq)])]
  transfers between devices with their start and end apart: 44 -> 119, of which waited for: 32 -> 46; matrix products, arithmetic and copies ran while one was open for 25% -> 42% of each run, Pallas kernels for 0% -> 3%
where the time goes in v1:
time: 1020 us; the launch traced here: 1010 us
  waiting for transfers between devices  290 us (28%)
  local copies, waits for them, and re-layouts  214 us (21%)
  starting transfers between devices  183 us (18%)
  other arithmetic  128 us (13%)
  matrix products  115 us (11%)
  Pallas kernels  48.2 us (5%)
  between operations  25.1 us (2%)
    ppermute x64, waiting for transfers between devices, exchange(): return lax.ppermute(value, 'seq', [(i, i ^ mask) for i in range(seq)])  169 us
    unnamed x488, local copies, waits for them, and re-layouts  54.5 us
    ppermute x64, starting transfers between devices, exchange(): return lax.ppermute(value, 'seq', [(i, i ^ mask) for i in range(seq)])  50.4 us
    ppermute x10, waiting for transfers between devices, shifted(): lax.ppermute(value, 'seq', [(i, i + steps) for i in range(count) if 0 <=...  49.6 us
    dot_general x8, matrix products, against_cols(): lax.dot_general(left, right, (((1,), (1,)), ((), ())), preferred_element_...  40 us
    dot_general x14, matrix products, dot(): return jnp.dot(left, right, preferred_element_type=F32)  39.5 us
    dot_general x8, matrix products, through_rows(): lax.dot_general(left, right, (((0,), (0,)), ((), ())), preferred_element_...  34 us
    pallas_call x2, Pallas kernels, attend_back(): pl.pallas_call(functools.partial(attend_back_kernel, block, span), grid=(...  27.5 us
  transfers between devices with their start and end apart: 119, of which 46 were waited for; matrix products, arithmetic and copies ran while one was open for 42% of the time, Pallas kernels for 3%

profile of v1, /device:TPU:0, one launch (start us, length us, event | category | flops | bytes accessed | tf_op | source)
XLA Modules:
  0.0 1011.0 jit_solution(16693519115715491786)
XLA Ops:
  27.4 8.4 all-reduce.2
  81.3 4.9 collective-permute-start.18
  120.6 9.5 collective-permute-done.2
  146.3 20.4 %all-to-all-done.1 = bf16[8,144,144]{2,1,0:T(8,128)(2,1)S(1)} async-done(((bf16[8,144,144]{2,1,0:T(8,128)(2,1)}), bf16[8,144,144]{2,1,0:T(8,128)(2,1)S(1)}, u32[]{:S(2)}, u32[]{:S(2)}) %all-to-all-start.1) | async-done | bytes 331808 | tf_op jit(solution)/shard_map/all_to_all | solution.py:191
  178.0 5.2 convolution_convert_fusion.11.q_ref
  187.3 6.6 collective-permute-done.9
  194.1 10.1 attend.2
  208.4 10.5 %maximum_bitcast_fusion = bf16[1,864,576]{2,1,0:T(8,128)(2,1)S(1)} fusion(bf16[144,144]{1,0:T(8,128)(2,1)S(1)} %get-tuple-element.262, bf16[144,144]{1,0:T(8,128)(2,1)S(1)} %get-tuple-element.263, bf16[144,144]{1,0:T(8,128)(2,1)S(1)} %get-tuple-element.264, bf16[144,144]{1,0:T(8,128)(2,1)S(1)} %get-tuple-element.265, ...), kind=kLoop, calls=%fused_computation.235 | loop fusion | flops 15925248 | bytes 1990656
  256.7 4.4 collective-permute-done.15
  267.0 24.9 %collective-permute-done.22 = bf16[576,1152]{1,0:T(8,128)(2,1)} collective-permute-done((bf16[576,1152]{1,0:T(8,128)(2,1)}, bf16[576,1152]{1,0:T(8,128)(2,1)}, u32[]{:S(2)}, u32[]{:S(2)}) %collective-permute-start.22) | collective-permute-done | bytes 1327136 | tf_op jit(solution)/shard_map/ppermute | solution.py:59
  295.3 5.3 fusion.37
  300.6 4.7 convolution_convert_fusion.10
  311.7 4.4 all-to-all-start.4
  358.1 12.2 %collective-permute-done.27 = bf16[256,1152]{1,0:T(8,128)(2,1)S(1)} collective-permute-done((bf16[256,1152]{1,0:T(8,128)(2,1)S(1)}, bf16[256,1152]{1,0:T(8,128)(2,1)S(1)}, u32[]{:S(2)}, u32[]{:S(2)}) %collective-permute-start.27) | collective-permute-done | bytes 589856 | tf_op jit(solution)/shard_map/ppermute | solution.py:59
  390.0 10.5 %attend.3 = (bf16[1024,384]{1,0:T(8,128)(2,1)S(1)}, f32[1024,128]{1,0:T(8,128)S(1)}) custom-call(bf16[1024,1152]{1,0:T(8,128)(2,1)} %copy-done.29, bf16[1408,768]{1,0:T(8,128)(2,1)S(1)} %pad_maximum_fusion.3.kv_ref, s32[1024,1]{1,0:T(8,128)S(1)} %copy.351.segq_ref, s32[4,1,640]{2,1,0:T(1,128)S(1)} %broadcast_in_dim.221.segk_ref, f32[1024,128]{1,0:T(8,128)S(1)} %fusion.92.head_ref), custom_call_target="tpu_custom_call" | custom-call | flops 1342177280 | bytes 3145728 | tf_op jit(solution)/shard_map/attend/pallas_call | solution.py:392
  404.7 9.0 maximum_maximum_fusion.4
  434.7 7.3 collective-permute-done.41
  457.9 7.2 collective-permute-done.44
  465.2 12.3 %collective-permute-done.52 = bf16[256,1152]{1,0:T(8,128)(2,1)} collective-permute-done((bf16[256,1152]{1,0:T(8,128)(2,1)}, bf16[256,1152]{1,0:T(8,128)(2,1)}, u32[]{:S(2)}, u32[]{:S(2)}) %collective-permute-start.52) | collective-permute-done | bytes 589856 | tf_op jit(solution)/shard_map/ppermute | solution.py:59
  483.6 5.3 fusion.36
  489.0 6.4 convolution_convert_fusion.8
  496.2 7.0 fusion.30
  508.1 5.2 fusion.178
  524.4 6.2 collective-permute-done.49
  530.6 11.8 %collective-permute-done.55 = bf16[256,1152]{1,0:T(8,128)(2,1)S(1)} collective-permute-done((bf16[256,1152]{1,0:T(8,128)(2,1)S(1)}, bf16[256,1152]{1,0:T(8,128)(2,1)S(1)}, u32[]{:S(2)}, u32[]{:S(2)}) %collective-permute-start.55) | collective-permute-done | bytes 589856 | tf_op jit(solution)/shard_map/ppermute | solution.py:59
  555.2 18.6 %collective-permute-done.97 = bf16[576,1152]{1,0:T(8,128)(2,1)} collective-permute-done((bf16[576,1152]{1,0:T(8,128)(2,1)}, bf16[576,1152]{1,0:T(8,128)(2,1)}, u32[]{:S(2)}, u32[]{:S(2)}) %collective-permute-start.97) | collective-permute-done | bytes 1327136 | tf_op jit(solution)/shard_map/ppermute | solution.py:59
  584.2 13.8 %attend_back.2 = (bf16[1024,384]{1,0:T(8,128)(2,1)S(1)}, bf16[1408,768]{1,0:T(8,128)(2,1)S(1)}) custom-call(bf16[1024,1152]{1,0:T(8,128)(2,1)} %copy-done.29, bf16[1408,768]{1,0:T(8,128)(2,1)} %copy-done.1, bf16[1024,384]{1,0:T(8,128)(2,1)S(1)} %convolution_convert_fusion.13.grad_ref, bf16[1024,384]{1,0:T(8,128)(2,1)S(1)} %copy-done.7, ...), custom_call_target="tpu_custom_call" | custom-call | flops 3355443200 | bytes 7864320 | tf_op jit(solution)/shard_map/attend_back/pallas_call | solution.py:423
  605.5 6.7 collective-permute-done.86
  623.6 6.0 convolution_convert_fusion.6
  647.1 5.5 collective-permute-done.63
  678.2 9.2 fusion.31
  702.9 8.2 fusion.148
  711.1 5.6 collective-permute-done.69
  726.0 5.2 fusion.177
  745.0 13.8 %attend_back.3 = (bf16[1024,384]{1,0:T(8,128)(2,1)S(1)}, bf16[1408,768]{1,0:T(8,128)(2,1)S(1)}) custom-call(bf16[1024,1152]{1,0:T(8,128)(2,1)} %copy-done.28, bf16[1408,768]{1,0:T(8,128)(2,1)} %copy-done, bf16[1024,384]{1,0:T(8,128)(2,1)S(1)} %convolution_convert_fusion.12.grad_ref, bf16[1024,384]{1,0:T(8,128)(2,1)S(1)} %copy-done.5, ...), custom_call_target="tpu_custom_call" | custom-call | flops 3355443200 | bytes 7864320 | tf_op jit(solution)/shard_map/attend_back/pallas_call | solution.py:423
  764.2 32.2 %collective-permute-done.74 = bf16[128,768]{1,0:T(8,128)(2,1)S(1)} collective-permute-done((bf16[128,768]{1,0:T(8,128)(2,1)S(1)}, bf16[128,768]{1,0:T(8,128)(2,1)S(1)}, u32[]{:S(2)}, u32[]{:S(2)}) %collective-permute-start.74) | collective-permute-done | bytes 196640 | tf_op jit(solution)/shard_map/ppermute | solution.py:64
  796.4 6.3 collective-permute-done.81
  808.1 5.1 fusion.102
  826.0 19.1 %all-to-all-done.6 = bf16[8,144,144]{2,1,0:T(8,128)(2,1)} async-done(((bf16[8,144,144]{2,1,0:T(8,128)(2,1)}), bf16[8,144,144]{2,1,0:T(8,128)(2,1)}, u32[]{:S(2)}, u32[]{:S(2)}) %all-to-all-start.6) | async-done | bytes 331808 | tf_op jit(solution)/shard_map/all_to_all | solution.py:201
  879.7 6.6 convolution_convert_fusion.4
  894.9 4.7 collective-permute-start.99
  900.7 5.4 collective-permute-done.99
  921.4 8.2 collective-permute-done.77
  936.8 6.9 all-to-all-start.5
  945.3 8.2 all-to-all-done.5
  977.7 6.6 all-to-all-start.8
  984.2 4.8 collective-permute-start.93
  992.0 4.6 collective-permute-done.93
  (1082 shorter events, 555.3 us)
Async XLA Ops:
  10.5 54.6 %collective-permute-start.32 = (bf16[288,144]{1,0:T(8,128)(2,1)}, bf16[288,144]{1,0:T(8,128)(2,1)}, u32[]{:S(2)}, u32[]{:S(2)}) collective-permute-start(bf16[288,144]{1,0:T(8,128)(2,1)} %get-tuple-element.260), channel_id=1, source_target_pairs={{0,0},{1,2},{2,4},{3,6},{4,1},{5,3},{6,5},{7,7},{8,8},{9,10},{10,1... | collective-permute-start | bytes 248840 | tf_op jit(solution)/shard_map/ppermute | solution.py:167
  13.4 54.3 %collective-permute-start.33 = (bf16[288,144]{1,0:T(8,128)(2,1)}, bf16[288,144]{1,0:T(8,128)(2,1)}, u32[]{:S(2)}, u32[]{:S(2)}) collective-permute-start(bf16[288,144]{1,0:T(8,128)(2,1)} %get-tuple-element.259), channel_id=1, source_target_pairs={{0,4},{1,6},{2,1},{3,3},{4,5},{5,7},{6,0},{7,2},{8,12},{9,14},{10,... | collective-permute-start | bytes 248840 | tf_op jit(solution)/shard_map/ppermute | solution.py:167
  17.3 52.0 %collective-permute-start.34 = (bf16[288,144]{1,0:T(8,128)(2,1)}, bf16[288,144]{1,0:T(8,128)(2,1)}, u32[]{:S(2)}, u32[]{:S(2)}) collective-permute-start(bf16[288,144]{1,0:T(8,128)(2,1)} %get-tuple-element.258), channel_id=1, source_target_pairs={{0,1},{1,3},{2,5},{3,7},{4,0},{5,2},{6,4},{7,6},{8,9},{9,11},{10,1... | collective-permute-start | bytes 248840 | tf_op jit(solution)/shard_map/ppermute | solution.py:167
  18.4 55.8 %collective-permute-start.35 = (bf16[288,144]{1,0:T(8,128)(2,1)}, bf16[288,144]{1,0:T(8,128)(2,1)}, u32[]{:S(2)}, u32[]{:S(2)}) collective-permute-start(bf16[288,144]{1,0:T(8,128)(2,1)} %get-tuple-element.257), channel_id=1, source_target_pairs={{0,5},{1,7},{2,0},{3,2},{4,4},{5,6},{6,1},{7,3},{8,13},{9,15},{10,... | collective-permute-start | bytes 248840 | tf_op jit(solution)/shard_map/ppermute | solution.py:167
  23.2 79.0 %collective-permute-start.29 = (bf16[288,144]{1,0:T(8,128)(2,1)}, bf16[288,144]{1,0:T(8,128)(2,1)}, u32[]{:S(2)}, u32[]{:S(2)}) collective-permute-start(bf16[288,144]{1,0:T(8,128)(2,1)} %get-tuple-element.325), channel_id=1, source_target_pairs={{0,0},{1,5},{2,3},{3,4},{4,2},{5,7},{6,1},{7,6},{8,8},{9,13},{10,1... | collective-permute-start | bytes 248840 | tf_op jit(solution)/shard_map/ppermute | solution.py:126
  38.1 59.7 %all-to-all-start = ((f32[32,2,864]{2,1,0:T(2,128)}), f32[32,2,864]{2,1,0:T(2,128)}, u32[]{:S(2)}, u32[]{:S(2)}) async-start(f32[32,2,864]{2,1,0:T(2,128)} %copy.343), calls=%async_computation | async-start | bytes 458752 | tf_op jit(solution)/shard_map/all_to_all | solution.py:687
  41.4 89.5 %all-gather.9.cloned.1.call-start = ((), (), s32[]{:S(2)}) async-start(), calls=%async_computation.16 | async-start | bytes 1843200 | tf_op jit(solution)/shard_map/all_gather | solution.py:259
  65.1 37.1 %collective-permute-start.30 = (bf16[288,144]{1,0:T(8,128)(2,1)}, bf16[288,144]{1,0:T(8,128)(2,1)}, u32[]{:S(2)}, u32[]{:S(2)}) collective-permute-start(bf16[288,144]{1,0:T(8,128)(2,1)} %get-tuple-element.324), channel_id=1, source_target_pairs={{0,4},{1,2},{2,7},{3,1},{4,6},{5,0},{6,5},{7,3},{8,12},{9,10},{10,... | collective-permute-start | bytes 248840 | tf_op jit(solution)/shard_map/ppermute | solution.py:126
  78.0 24.3 %collective-permute-start.31 = (bf16[288,144]{1,0:T(8,128)(2,1)}, bf16[288,144]{1,0:T(8,128)(2,1)}, u32[]{:S(2)}, u32[]{:S(2)}) collective-permute-start(bf16[288,144]{1,0:T(8,128)(2,1)} %get-tuple-element.323), channel_id=1, source_target_pairs={{0,1},{1,6},{2,0},{3,5},{4,3},{5,4},{6,2},{7,7},{8,9},{9,14},{10,8... | collective-permute-start | bytes 248840 | tf_op jit(solution)/shard_map/ppermute | solution.py:126
  101.4 123.7 %all-gather.11.cloned.1.call-start = ((), (), s32[]{:S(2)}) async-start(), calls=%async_computation.17 | async-start | bytes 3686400 | tf_op jit(solution)/shard_map/all_gather | solution.py:259
  135.7 38.7 %collective-permute-start.7 = (bf16[1152,432]{0,1:T(8,128)(2,1)}, bf16[1152,432]{0,1:T(8,128)(2,1)}, u32[]{:S(2)}, u32[]{:S(2)}) collective-permute-start(bf16[1152,432]{0,1:T(8,128)(2,1)} %copy.348), channel_id=1, source_target_pairs={{0,4},{1,5},{2,6},{3,7},{4,0},{5,1},{6,2},{7,3},{8,12},{9,13},{10,... | collective-permute-start | bytes 2985992 | tf_op jit(solution)/shard_map/ppermute | solution.py:59
  140.8 25.8 %all-to-all-start.1 = ((bf16[8,144,144]{2,1,0:T(8,128)(2,1)}), bf16[8,144,144]{2,1,0:T(8,128)(2,1)S(1)}, u32[]{:S(2)}, u32[]{:S(2)}) async-start(bf16[8,144,144]{2,1,0:T(8,128)(2,1)} %bitcast.32), calls=%async_computation.1 | async-start | bytes 1179648 | tf_op jit(solution)/shard_map/all_to_all | solution.py:191
  166.7 41.6 %all-to-all-start.3 = ((bf16[8,144,144]{2,1,0:T(8,128)(2,1)}), bf16[8,144,144]{2,1,0:T(8,128)(2,1)S(1)}, u32[]{:S(2)}, u32[]{:S(2)}) async-start(bf16[8,144,144]{2,1,0:T(8,128)(2,1)} %bitcast.122), calls=%async_computation.3 | async-start | bytes 1179648 | tf_op jit(solution)/shard_map/all_to_all | solution.py:191
  170.2 138.9 %all-gather.13.cloned.1.call-start = ((), (), s32[]{:S(2)}) async-start(), calls=%async_computation.18 | async-start | bytes 5160960 | tf_op jit(solution)/shard_map/all_gather | solution.py:259
  231.6 32.8 %collective-permute-start.21 = (bf16[1152,576]{0,1:T(8,128)(2,1)}, bf16[1152,576]{0,1:T(8,128)(2,1)}, u32[]{:S(2)}, u32[]{:S(2)}) collective-permute-start(bf16[1152,576]{0,1:T(8,128)(2,1)} %copy.354), channel_id=1, source_target_pairs={{0,4},{1,5},{2,6},{3,7},{4,0},{5,1},{6,2},{7,3},{8,12},{9,13},{10,... | collective-permute-start | bytes 3981320 | tf_op jit(solution)/shard_map/ppermute | solution.py:59
  248.1 43.9 %collective-permute-start.22 = (bf16[576,1152]{1,0:T(8,128)(2,1)}, bf16[576,1152]{1,0:T(8,128)(2,1)}, u32[]{:S(2)}, u32[]{:S(2)}) collective-permute-start(bf16[576,1152]{1,0:T(8,128)(2,1)} %pad_maximum_fusion.13), channel_id=1, source_target_pairs={{0,4},{1,5},{2,6},{3,7},{4,0},{5,1},{6,2},{7,3},{8,12},{9,13},{10,... | collective-permute-start | bytes 3981320 | tf_op jit(solution)/shard_map/ppermute | solution.py:59
  261.1 33.3 %collective-permute-start.16 = (bf16[256,1152]{1,0:T(8,128)(2,1)S(1)}, bf16[256,1152]{1,0:T(8,128)(2,1)S(1)}, u32[]{:S(2)}, u32[]{:S(2)}) collective-permute-start(bf16[256,1152]{1,0:T(8,128)(2,1)S(1)} %collective-permute-done.15), channel_id=1, source_target_pairs={{0,1},{1,0},{2,3},{3,2},{4,5},{5,4},{6,7},{7,6},{8,9},{9,8},{10,11... | collective-permute-start | bytes 1769480 | tf_op jit(solution)/shard_map/ppermute | solution.py:59
  306.5 27.4 %collective-permute-start.23 = (bf16[256,1152]{1,0:T(8,128)(2,1)}, bf16[256,1152]{1,0:T(8,128)(2,1)}, u32[]{:S(2)}, u32[]{:S(2)}) collective-permute-start(bf16[256,1152]{1,0:T(8,128)(2,1)} %get-tuple-element.190), channel_id=1, source_target_pairs={{0,1},{1,0},{2,3},{3,2},{4,5},{5,4},{6,7},{7,6},{8,9},{9,8},{10,11... | collective-permute-start | bytes 1769480 | tf_op jit(solution)/shard_map/ppermute | solution.py:59
  309.0 39.7 %collective-permute-start.25 = (bf16[256,1152]{1,0:T(8,128)(2,1)}, bf16[256,1152]{1,0:T(8,128)(2,1)}, u32[]{:S(2)}, u32[]{:S(2)}) collective-permute-start(bf16[256,1152]{1,0:T(8,128)(2,1)} %get-tuple-element.191), channel_id=1, source_target_pairs={{0,1},{1,0},{2,3},{3,2},{4,5},{5,4},{6,7},{7,6},{8,9},{9,8},{10,11... | collective-permute-start | bytes 1769480 | tf_op jit(solution)/shard_map/ppermute | solution.py:59
  311.7 31.5 %all-to-all-start.4 = ((bf16[8,144,144]{2,1,0:T(8,128)(2,1)}), bf16[8,144,144]{2,1,0:T(8,128)(2,1)}, u32[]{:S(2)}, u32[]{:S(2)}) async-start(bf16[8,144,144]{2,1,0:T(8,128)(2,1)} %bitcast.136), calls=%async_computation.4 | async-start | bytes 1179648 | tf_op jit(solution)/shard_map/all_to_all | solution.py:191
  321.7 34.5 %collective-permute-start.36 = (bf16[1152,432]{0,1:T(8,128)(2,1)}, bf16[1152,432]{0,1:T(8,128)(2,1)}, u32[]{:S(2)}, u32[]{:S(2)}) collective-permute-start(bf16[1152,432]{0,1:T(8,128)(2,1)} %copy.362), channel_id=1, source_target_pairs={{0,4},{1,5},{2,6},{3,7},{4,0},{5,1},{6,2},{7,3},{8,12},{9,13},{10,... | collective-permute-start | bytes 2985992 | tf_op jit(solution)/shard_map/ppermute | solution.py:59
  333.8 118.7 %collective-permute-start.46 = (bf16[1152,576]{0,1:T(8,128)(2,1)}, bf16[1152,576]{0,1:T(8,128)(2,1)}, u32[]{:S(2)}, u32[]{:S(2)}) collective-permute-start(bf16[1152,576]{0,1:T(8,128)(2,1)} %copy.368), channel_id=1, source_target_pairs={{0,4},{1,5},{2,6},{3,7},{4,0},{5,1},{6,2},{7,3},{8,12},{9,13},{10,... | collective-permute-start | bytes 3981320 | tf_op jit(solution)/shard_map/ppermute | solution.py:59
  347.2 35.9 %collective-permute-start.39 = (bf16[144,1152]{1,0:T(8,128)(2,1)}, bf16[144,1152]{1,0:T(8,128)(2,1)S(1)}, u32[]{:S(2)}, u32[]{:S(2)}) collective-permute-start(bf16[144,1152]{1,0:T(8,128)(2,1)} %concatenate.243), channel_id=1, source_target_pairs={{0,4},{1,5},{2,6},{3,7},{4,0},{5,1},{6,2},{7,3},{8,12},{9,13},{10,... | collective-permute-start | bytes 995336 | tf_op jit(solution)/shard_map/ppermute | solution.py:59
  416.3 39.0 %collective-permute-start.47 = (bf16[576,1152]{1,0:T(8,128)(2,1)}, bf16[576,1152]{1,0:T(8,128)(2,1)}, u32[]{:S(2)}, u32[]{:S(2)}) collective-permute-start(bf16[576,1152]{1,0:T(8,128)(2,1)} %copy.371), channel_id=1, source_target_pairs={{0,4},{1,5},{2,6},{3,7},{4,0},{5,1},{6,2},{7,3},{8,12},{9,13},{10,... | collective-permute-start | bytes 3981320 | tf_op jit(solution)/shard_map/ppermute | solution.py:59
  448.7 28.7 %collective-permute-start.43 = (bf16[256,1152]{1,0:T(8,128)(2,1)}, bf16[256,1152]{1,0:T(8,128)(2,1)}, u32[]{:S(2)}, u32[]{:S(2)}) collective-permute-start(bf16[256,1152]{1,0:T(8,128)(2,1)} %get-tuple-element.129), channel_id=1, source_target_pairs={{0,1},{1,0},{2,3},{3,2},{4,5},{5,4},{6,7},{7,6},{8,9},{9,8},{10,11... | collective-permute-start | bytes 1769480 | tf_op jit(solution)/shard_map/ppermute | solution.py:59
  449.8 27.6 %collective-permute-start.52 = (bf16[256,1152]{1,0:T(8,128)(2,1)}, bf16[256,1152]{1,0:T(8,128)(2,1)}, u32[]{:S(2)}, u32[]{:S(2)}) collective-permute-start(bf16[256,1152]{1,0:T(8,128)(2,1)} %get-tuple-element.350), channel_id=1, source_target_pairs={{0,2},{1,3},{2,0},{3,1},{4,6},{5,7},{6,4},{7,5},{8,10},{9,11},{10,... | collective-permute-start | bytes 1769480 | tf_op jit(solution)/shard_map/ppermute | solution.py:59
  514.1 38.7 %collective-permute-start.96 = (bf16[1152,576]{0,1:T(8,128)(2,1)S(1)}, bf16[1152,576]{0,1:T(8,128)(2,1)S(1)}, u32[]{:S(2)}, u32[]{:S(2)}) collective-permute-start(bf16[1152,576]{0,1:T(8,128)(2,1)S(1)} %slice.1891), channel_id=1, source_target_pairs={{0,4},{1,5},{2,6},{3,7},{4,0},{5,1},{6,2},{7,3},{8,12},{9,13},{10,... | collective-permute-start | bytes 3981320 | tf_op jit(solution)/shard_map/ppermute | solution.py:59
  515.6 26.7 %collective-permute-start.55 = (bf16[256,1152]{1,0:T(8,128)(2,1)S(1)}, bf16[256,1152]{1,0:T(8,128)(2,1)S(1)}, u32[]{:S(2)}, u32[]{:S(2)}) collective-permute-start(bf16[256,1152]{1,0:T(8,128)(2,1)S(1)} %fusion.73), channel_id=1, source_target_pairs={{0,2},{1,3},{2,0},{3,1},{4,6},{5,7},{6,4},{7,5},{8,10},{9,11},{10,... | collective-permute-start | bytes 1769480 | tf_op jit(solution)/shard_map/ppermute | solution.py:59
  522.4 51.4 %collective-permute-start.97 = (bf16[576,1152]{1,0:T(8,128)(2,1)}, bf16[576,1152]{1,0:T(8,128)(2,1)}, u32[]{:S(2)}, u32[]{:S(2)}) collective-permute-start(bf16[576,1152]{1,0:T(8,128)(2,1)} %slice.1890), channel_id=1, source_target_pairs={{0,4},{1,5},{2,6},{3,7},{4,0},{5,1},{6,2},{7,3},{8,12},{9,13},{10,... | collective-permute-start | bytes 3981320 | tf_op jit(solution)/shard_map/ppermute | solution.py:59
  549.3 29.7 %collective-permute-start.57 = (bf16[256,1152]{1,0:T(8,128)(2,1)S(1)}, bf16[256,1152]{1,0:T(8,128)(2,1)}, u32[]{:S(2)}, u32[]{:S(2)}) collective-permute-start(bf16[256,1152]{1,0:T(8,128)(2,1)S(1)} %get-tuple-element.125), channel_id=1, source_target_pairs={{0,1},{1,0},{2,3},{3,2},{4,5},{5,4},{6,7},{7,6},{8,9},{9,8},{10,11... | collective-permute-start | bytes 1769480 | tf_op jit(solution)/shard_map/ppermute | solution.py:59
  549.4 29.7 %collective-permute-start.58 = (bf16[256,1152]{1,0:T(8,128)(2,1)S(1)}, bf16[256,1152]{1,0:T(8,128)(2,1)}, u32[]{:S(2)}, u32[]{:S(2)}) collective-permute-start(bf16[256,1152]{1,0:T(8,128)(2,1)S(1)} %get-tuple-element.125), channel_id=1, source_target_pairs={{0,2},{1,3},{2,0},{3,1},{4,6},{5,7},{6,4},{7,5},{8,10},{9,11},{10,... | collective-permute-start | bytes 1769480 | tf_op jit(solution)/shard_map/ppermute | solution.py:59
  617.9 24.6 %all-to-all-start.7 = ((bf16[8,144,144]{2,1,0:T(8,128)(2,1)}), bf16[8,144,144]{2,1,0:T(8,128)(2,1)}, u32[]{:S(2)}, u32[]{:S(2)}) async-start(bf16[8,144,144]{2,1,0:T(8,128)(2,1)} %constant_dynamic-update-slice_fusion.36), calls=%async_computation.7 | async-start | bytes 1179648 | tf_op jit(solution)/shard_map/all_to_all | solution.py:201
  622.2 230.7 %reduce-scatter.15.cloned.1.call-start = ((), (), s32[]{:S(2)}) async-start(), calls=%async_computation.20 | async-start | bytes 1843200 | tf_op jit(solution)/shard_map/reduce_scatter | solution.py:619
  641.1 24.1 %collective-permute-start.85 = (bf16[1152,432]{0,1:T(8,128)(2,1)}, bf16[1152,432]{0,1:T(8,128)(2,1)}, u32[]{:S(2)}, u32[]{:S(2)}) collective-permute-start(bf16[1152,432]{0,1:T(8,128)(2,1)} %select_convert_fusion), channel_id=1, source_target_pairs={{0,4},{1,5},{2,6},{3,7},{4,0},{5,1},{6,2},{7,3},{8,12},{9,13},{10,... | collective-permute-start | bytes 2985992 | tf_op jit(solution)/shard_map/ppermute | solution.py:59
  670.6 200.2 %reduce-scatter.11.cloned.1.call-start = ((), (), s32[]{:S(2)}) async-start(), calls=%async_computation.15 | async-start | bytes 3686400 | tf_op jit(solution)/shard_map/reduce_scatter | solution.py:633
  732.6 126.0 %collective-permute-start.90 = (bf16[1152,576]{0,1:T(8,128)(2,1)}, bf16[1152,576]{0,1:T(8,128)(2,1)}, u32[]{:S(2)}, u32[]{:S(2)}) collective-permute-start(bf16[1152,576]{0,1:T(8,128)(2,1)} %slice.1893), channel_id=1, source_target_pairs={{0,4},{1,5},{2,6},{3,7},{4,0},{5,1},{6,2},{7,3},{8,12},{9,13},{10,... | collective-permute-start | bytes 3981320 | tf_op jit(solution)/shard_map/ppermute | solution.py:59
  735.2 128.9 %collective-permute-start.91 = (bf16[576,1152]{1,0:T(8,128)(2,1)}, bf16[576,1152]{1,0:T(8,128)(2,1)}, u32[]{:S(2)}, u32[]{:S(2)}) collective-permute-start(bf16[576,1152]{1,0:T(8,128)(2,1)} %slice.1892), channel_id=1, source_target_pairs={{0,4},{1,5},{2,6},{3,7},{4,0},{5,1},{6,2},{7,3},{8,12},{9,13},{10,... | collective-permute-start | bytes 3981320 | tf_op jit(solution)/shard_map/ppermute | solution.py:59
  758.8 37.6 %collective-permute-start.74 = (bf16[128,768]{1,0:T(8,128)(2,1)S(1)}, bf16[128,768]{1,0:T(8,128)(2,1)S(1)}, u32[]{:S(2)}, u32[]{:S(2)}) collective-permute-start(bf16[128,768]{1,0:T(8,128)(2,1)S(1)} %slice.1241), channel_id=1, source_target_pairs={{0,4},{1,5},{2,6},{3,7},{8,12},{9,13},{10,14},{11,15},{16,20},{17,... | collective-permute-start | bytes 589832 | tf_op jit(solution)/shard_map/ppermute | solution.py:64
  762.5 40.3 %collective-permute-start.81 = (bf16[144,1152]{1,0:T(8,128)(2,1)S(1)}, bf16[144,1152]{1,0:T(8,128)(2,1)S(1)}, u32[]{:S(2)}, u32[]{:S(2)}) collective-permute-start(bf16[144,1152]{1,0:T(8,128)(2,1)S(1)} %select_convert_fusion.3), channel_id=1, source_target_pairs={{0,4},{1,5},{2,6},{3,7},{4,0},{5,1},{6,2},{7,3},{8,12},{9,13},{10,... | collective-permute-start | bytes 995336 | tf_op jit(solution)/shard_map/ppermute | solution.py:59
  762.7 45.3 %collective-permute-start.75 = (bf16[256,768]{1,0:T(8,128)(2,1)S(1)}, bf16[256,768]{1,0:T(8,128)(2,1)S(1)}, u32[]{:S(2)}, u32[]{:S(2)}) collective-permute-start(bf16[256,768]{1,0:T(8,128)(2,1)S(1)} %slice.1244), channel_id=1, source_target_pairs={{4,0},{5,1},{6,2},{7,3},{12,8},{13,9},{14,10},{15,11},{20,16},{21,... | collective-permute-start | bytes 1179656 | tf_op jit(solution)/shard_map/ppermute | solution.py:64
  815.1 33.7 %collective-permute-start.80 = (bf16[1152,432]{0,1:T(8,128)(2,1)}, bf16[1152,432]{0,1:T(8,128)(2,1)}, u32[]{:S(2)}, u32[]{:S(2)}) collective-permute-start(bf16[1152,432]{0,1:T(8,128)(2,1)} %select_convert_fusion.1), channel_id=1, source_target_pairs={{0,4},{1,5},{2,6},{3,7},{4,0},{5,1},{6,2},{7,3},{8,12},{9,13},{10,... | collective-permute-start | bytes 2985992 | tf_op jit(solution)/shard_map/ppermute | solution.py:59
  818.1 27.0 %all-to-all-start.6 = ((bf16[8,144,144]{2,1,0:T(8,128)(2,1)}), bf16[8,144,144]{2,1,0:T(8,128)(2,1)}, u32[]{:S(2)}, u32[]{:S(2)}) async-start(bf16[8,144,144]{2,1,0:T(8,128)(2,1)} %constant_dynamic-update-slice_fusion.28), calls=%async_computation.6 | async-start | bytes 1179648 | tf_op jit(solution)/shard_map/all_to_all | solution.py:201
  822.3 134.0 %reduce-scatter.13.cloned.1.call-start = ((), (), s32[]{:S(2)}) async-start(), calls=%async_computation.19 | async-start | bytes 1843200 | tf_op jit(solution)/shard_map/reduce_scatter | solution.py:619
  852.8 117.0 %reduce-scatter.9.cloned.1.call-start = ((), (), s32[]{:S(2)}) async-start(), calls=%async_computation.14 | async-start | bytes 3686400 | tf_op jit(solution)/shard_map/reduce_scatter | solution.py:633
  855.8 105.6 %collective-permute-start.87 = (bf16[288,144]{1,0:T(8,128)(2,1)}, bf16[288,144]{1,0:T(8,128)(2,1)}, u32[]{:S(2)}, u32[]{:S(2)}) collective-permute-start(bf16[288,144]{1,0:T(8,128)(2,1)} %get-tuple-element.312), channel_id=1, source_target_pairs={{0,0},{5,1},{3,2},{4,3},{2,4},{7,5},{1,6},{6,7},{8,8},{13,9},{11,1... | collective-permute-start | bytes 248840 | tf_op jit(solution)/shard_map/ppermute | solution.py:143
  858.6 107.0 %collective-permute-start.88 = (bf16[288,144]{1,0:T(8,128)(2,1)}, bf16[288,144]{1,0:T(8,128)(2,1)}, u32[]{:S(2)}, u32[]{:S(2)}) collective-permute-start(bf16[288,144]{1,0:T(8,128)(2,1)} %get-tuple-element.313), channel_id=1, source_target_pairs={{4,0},{2,1},{7,2},{1,3},{6,4},{0,5},{5,6},{3,7},{12,8},{10,9},{15,... | collective-permute-start | bytes 248840 | tf_op jit(solution)/shard_map/ppermute | solution.py:143
  891.4 27.2 %all-to-all-start.9 = ((bf16[8,144,144]{2,1,0:T(8,128)(2,1)}), bf16[8,144,144]{2,1,0:T(8,128)(2,1)S(1)}, u32[]{:S(2)}, u32[]{:S(2)}) async-start(bf16[8,144,144]{2,1,0:T(8,128)(2,1)} %constant_dynamic-update-slice_fusion.52), calls=%async_computation.11 | async-start | bytes 1179648 | tf_op jit(solution)/shard_map/all_to_all | solution.py:201
  913.3 52.2 %collective-permute-start.89 = (bf16[288,144]{1,0:T(8,128)(2,1)}, bf16[288,144]{1,0:T(8,128)(2,1)}, u32[]{:S(2)}, u32[]{:S(2)}) collective-permute-start(bf16[288,144]{1,0:T(8,128)(2,1)} %get-tuple-element.314), channel_id=1, source_target_pairs={{1,0},{6,1},{0,2},{5,3},{3,4},{4,5},{2,6},{7,7},{9,8},{14,9},{8,10... | collective-permute-start | bytes 248840 | tf_op jit(solution)/shard_map/ppermute | solution.py:143
  (286 other events, 3871.4 us)
Sparse Core Ops, SparseCore 0:
  87.5 36.4 all-gather.8
  126.1 59.1 all-gather.10
  220.7 82.0 all-gather.12
  670.7 33.8 reduce-scatter.14
  706.9 56.0 reduce-scatter.10
  852.9 33.1 reduce-scatter.12
  888.6 56.0 reduce-scatter.8

commit v2 on v1

v2 whole, which is shorter than its diff:
```python
import functools
import math

import jax
import jax.numpy as jnp
import numpy as np
from jax import lax
from jax.experimental import pallas as pl
from jax.experimental.pallas import tpu as pltpu
from jax.sharding import Mesh
from jax.sharding import PartitionSpec as P

D = 1152
HEADS = 16
HEAD_DIM = 72
FF = 4608
GROUPS = 16
LAYERS = 2

TP = 4
LANES = 128
LOCAL_HEADS = HEADS // TP
LOCAL_FF = FF // TP
WIDTH = -(-LOCAL_HEADS * HEAD_DIM // LANES) * LANES
AFTER = 128
CHUNK = 256

SEQ = ("group", "member")
EVERY = ("dp", "group", "member")
OWNERS = ("dp", "group")

EPS = 1e-06
HIGH = lax.Precision.HIGHEST
NEGATIVE = -1e30
FACTOR = HEAD_DIM ** (-0.5)
F32 = jnp.float32
BF16 = jnp.bfloat16


def sizes():
    groups, planes = lax.axis_size("group"), lax.axis_size("dp")
    return groups * TP, groups, planes


def place():
    return lax.axis_index("group"), lax.axis_index("member")


def here():
    return jnp.stack([lax.axis_index("dp"), *place()])


def device_of(unit, groups):
    return (unit % groups) * TP + unit // groups


def unit_table(seq, groups):
    return np.array([(s % TP) * groups + s // TP for s in range(seq)])


def my_unit():
    _, groups, _ = sizes()
    group, member = place()
    return member * groups + group


def exchange(value, mask):
    seq, _, _ = sizes()
    return lax.ppermute(value, SEQ, [(i, i ^ mask) for i in range(seq)])


def shifted(value, steps):
    count, _, _ = sizes()
    return lax.ppermute(
        value, SEQ, [(i, i + steps) for i in range(count) if 0 <= i + steps < count]
    )


def from_plane(value, back):
    planes = lax.axis_size("dp")
    return lax.ppermute(value, "dp", [(d, (d + back) % planes) for d in range(planes)])


def after(value, *events):
    return lax.optimization_barrier((value,) + events)[0]


def dot(left, right):
    return jnp.dot(left, right, preferred_element_type=F32)


def through_rows(left, right):
    return lax.dot_general(left, right, (((0,), (0,)), ((), ())), preferred_element_type=F32)


def against_cols(left, right):
    return lax.dot_general(left, right, (((1,), (1,)), ((), ())), preferred_element_type=F32)


def near(mine):
    return [mine, exchange(mine, 1)]


def far(theirs):
    return [theirs, exchange(theirs, 1)]


def pair_sum(parts):
    return parts[0].astype(F32) + exchange(parts[1], 1).astype(F32)


def far_sum(pair):
    return exchange(pair.astype(BF16), 2).astype(F32)


def kinds_table(seq, groups):
    pairs, kinds = [], np.zeros((3, seq), np.int32)
    for r in range(3):
        targets = [device_of((3 * s + r) % seq, groups) for s in range(seq)]
        pairs.append(list(enumerate(targets)))
        for s in range(seq):
            kinds[r, targets[s]] = (3 * s + r) // seq
    return pairs, kinds


def my_kinds():
    seq, groups, _ = sizes()
    return jnp.asarray(kinds_table(seq, groups)[1])[:, lax.axis_index(SEQ)]


def deal_joint(joint):
    seq, groups, _ = sizes()
    pairs, _ = kinds_table(seq, groups)
    cols = joint.shape[1] // 3
    return [
        lax.ppermute(joint[:, r * cols : (r + 1) * cols], SEQ, pairs[r]) for r in range(3)
    ]


def return_joint(parts):
    seq, groups, _ = sizes()
    pairs, _ = kinds_table(seq, groups)
    back = [lax.ppermute(part, SEQ, [(b, a) for a, b in pairs[r]]) for r, part in enumerate(parts)]
    return jnp.concatenate(back, axis=1).astype(F32)


def choose(which, options):
    first, second, third = options
    return jnp.where(which == 0, first, jnp.where(which == 1, second, third))


def pack_attention_any(got, project):
    kinds = my_kinds()
    sent = [jnp.where(kinds[0] == k, got[0], jnp.where(kinds[1] == k, got[1], got[2])) for k in range(3)]
    return jnp.concatenate(sent + [project], axis=1)


def open_attention_any(stack):
    _, groups, planes = sizes()
    height, cols = stack.shape[1], stack.shape[2] // 4
    stack = stack.reshape(planes, groups, height, 4, cols)
    kinds = jnp.transpose(stack, (3, 0, 2, 1, 4)).reshape(4, D, groups * cols)
    blank = jnp.zeros((D, WIDTH - groups * cols), BF16)
    joint = jnp.concatenate([part for k in range(3) for part in (kinds[k], blank)], axis=1)
    return joint, kinds[3].reshape(TP, D // TP, groups * cols)


def join_project_any(got):
    _, groups, _ = sizes()
    rows = got.reshape(TP, D // TP, groups, -1).transpose(1, 2, 0, 3).reshape(D // TP, D)
    return jnp.concatenate([rows, jnp.zeros((WIDTH - D // TP, D), BF16)], axis=0)


def split_project_any(grad):
    _, groups, _ = sizes()
    chunks = grad[: D // TP].reshape(D // TP, groups, TP, -1).transpose(2, 0, 1, 3)
    return chunks.reshape(TP, D // TP, -1)


def split_attention_any(g_joint, got):
    _, groups, planes = sizes()
    cols = D // TP // groups
    parts = [g_joint[:, k * WIDTH : k * WIDTH + groups * cols] for k in range(3)]
    parts = jnp.stack(parts + [got.reshape(D, groups * cols)])
    parts = parts.reshape(4, planes, D // planes, groups, cols).transpose(1, 3, 2, 0, 4)
    return parts.reshape(planes * groups, D // planes, 4 * cols)


def unpack_attention_any(owned):
    kinds = my_kinds()
    cols = owned.shape[1] // 4
    own = [owned[:, k * cols : (k + 1) * cols] for k in range(4)]
    return [choose(kinds[r], own[:3]).astype(BF16) for r in range(3)] + [own[3].astype(F32)]


def pack_forward_any(expand, reduce):
    seq, groups, planes = sizes()
    cols, rows = expand.shape[1] // planes, reduce.shape[0] // seq
    chunks = []
    for unit in unit_table(seq, groups):
        q = unit % planes
        chunks += [expand[:, q * cols : (q + 1) * cols], reduce[unit * rows : (unit + 1) * rows]]
    chunks = jnp.concatenate([chunk.reshape(-1, cols) for chunk in chunks], axis=0)
    return chunks.reshape(seq, -1, cols)


def unpack_forward_any(got):
    seq, _, planes = sizes()
    ways, cols = seq // planes, got.shape[2]
    height, width = D // planes, got.shape[2] * planes
    mine = got.reshape((planes, ways) + got.shape[1:])
    mine = lax.dynamic_index_in_dim(mine, my_unit() // planes, 1, keepdims=False)
    expand = jnp.concatenate([mine[d, :height] for d in range(planes)], axis=1)
    reduce = got[:, height:].reshape(seq, cols, D // seq)
    reduce = jnp.concatenate([reduce[s] for s in range(seq)], axis=1)
    blocks = [reduce[:, k * width : (k + 1) * width] for k in range(D // width)]
    return jnp.concatenate([expand] + blocks, axis=0)


def open_forward_any(stack):
    _, groups, planes = sizes()
    height, width = D // planes, stack.shape[2]
    rows = width // planes
    stack = stack.reshape((planes, groups) + stack.shape[1:])
    expand = jnp.transpose(stack[:, :, :height], (0, 2, 1, 3)).reshape(D, groups * width)
    reduce = stack[:, :, height:].reshape(planes, groups, D // width, rows, width)
    reduce = jnp.transpose(reduce, (1, 0, 3, 2, 4)).reshape(groups * planes * rows, D)
    return expand, reduce


def split_forward_any(g_expand, g_reduce):
    _, groups, planes = sizes()
    height, width = D // planes, LOCAL_FF // groups
    rows = width // planes
    expand = g_expand.reshape(planes, height, groups, width).transpose(0, 2, 1, 3)
    reduce = g_reduce.reshape(groups, planes, rows, D // width, width).transpose(1, 0, 3, 2, 4)
    reduce = reduce.reshape(planes, groups, rows * D // width, width)
    stack = jnp.concatenate([expand, reduce], axis=2)
    return stack.reshape((planes * groups,) + stack.shape[2:])


def pack_return_any(owned):
    seq, _, planes = sizes()
    ways, height, width = seq // planes, D // planes, owned.shape[1]
    rows, cols = width // planes, width // planes
    blocks = owned[height:].reshape(D // width, rows, width)
    reduce = jnp.concatenate([blocks[k] for k in range(D // width)], axis=1)
    chunks = []
    for s in range(seq):
        d = s // ways
        chunks.append(owned[:height, d * cols : (d + 1) * cols])
        chunks.append(reduce[:, s * (D // seq) : (s + 1) * (D // seq)].reshape(-1, cols))
    return jnp.concatenate(chunks, axis=0).reshape(seq, -1, cols)


def unpack_return_any(got):
    seq, groups, planes = sizes()
    ways, cols, height = seq // planes, got.shape[2], D // planes
    got = jnp.swapaxes(got.reshape((groups, TP) + got.shape[1:]), 0, 1).reshape(got.shape)
    first = planes * (lax.axis_index(SEQ) % ways)
    mine = lax.dynamic_slice_in_dim(got[:, :height], first, planes)
    expand = jnp.concatenate([mine[q] for q in range(planes)], axis=1)
    return expand.astype(F32), got[:, height:].reshape(-1, D // seq).astype(F32)


def compact():
    seq, groups, planes = sizes()
    return groups == 2 and planes == 4 and D // seq % 16 == 0


def rearrange(body, arrays, outs, name):
    return pl.pallas_call(
        body,
        in_specs=[pl.BlockSpec(memory_space=pltpu.SMEM)]
        + [pl.BlockSpec(memory_space=pltpu.VMEM)] * len(arrays),
        out_specs=[pl.BlockSpec(memory_space=pltpu.VMEM)] * len(outs),
        out_shape=[jax.ShapeDtypeStruct(shape, dtype) for shape, dtype in outs],
        compiler_params=pltpu.CompilerParams(vmem_limit_bytes=48 * 1024 * 1024),
        cost_estimate=pl.CostEstimate(
            flops=0,
            bytes_accessed=sum(math.prod(shape) * 4 for shape, _ in outs),
            transcendentals=0,
        ),
        name=name,
    )(here(), *arrays)


def side_by_side(parts):
    return jnp.concatenate(parts, axis=1)


def kind_sent(me_ref, r):
    unit = me_ref[2] * 2 + me_ref[1]
    source = (3 * (unit + 8 - r)) % 8
    return (3 * source + r) // 8


def pack_attention_kernel(me_ref, a_ref, b_ref, c_ref, project_ref, out_ref):
    cols = a_ref.shape[1]
    first, second = kind_sent(me_ref, 0), kind_sent(me_ref, 1)
    for half in range(2):
        rows = slice(half * cols, (half + 1) * cols)
        a, b, c = a_ref[rows], b_ref[rows], c_ref[rows]
        parts = [jnp.where(first == k, a, jnp.where(second == k, b, c)) for k in range(3)]
        out_ref[:, half * 4 * cols : (half + 1) * 4 * cols] = side_by_side(
            parts + [project_ref[rows]]
        )


def by_plane(me_ref, refs):
    if len(refs) == 1:
        return [(d, refs[0][2 * d], refs[0][2 * d + 1]) for d in range(4)]
    got = []
    for step in range(4):
        own, other = refs[step][...], refs[4 + step][...]
        first = jnp.where(me_ref[1] == 0, own, other)
        second = jnp.where(me_ref[1] == 0, other, own)
        got.append(((me_ref[0] + 4 - step) % 4, first, second))
    return got


def rows_at(start, count):
    if isinstance(start, int):
        return slice(start, start + count)
    return pl.ds(pl.multiple_of(start, 16), count)


def open_attention_kernel(me_ref, *refs):
    *refs, joint_ref, project_ref = refs
    cols = refs[0].shape[-2]
    blank = jnp.zeros((cols, WIDTH - 2 * cols), BF16)
    for plane, first, second in by_plane(me_ref, refs):
        for half in range(2):
            pieces = [
                [piece[:, (4 * half + k) * cols : (4 * half + k + 1) * cols] for k in range(4)]
                for piece in (first, second)
            ]
            parts = []
            for kind in range(3):
                parts += [pieces[0][kind], pieces[1][kind], blank]
            joint_ref[rows_at(plane * 2 * cols + half * cols, cols)] = side_by_side(parts)
            project_ref[plane, half * cols : (half + 1) * cols] = side_by_side(
                [pieces[0][3], pieces[1][3]]
            )


def join_project_kernel(me_ref, got_ref, out_ref):
    cols = got_ref.shape[2] // 2
    rows = got_ref.shape[1]
    out_ref[:rows] = side_by_side(
        [got_ref[t][:, g * cols : (g + 1) * cols] for g in range(2) for t in range(4)]
    )
    out_ref[rows:] = jnp.zeros((out_ref.shape[0] - rows, out_ref.shape[1]), BF16)


def split_project_kernel(me_ref, grad_ref, out_ref):
    rows, cols = out_ref.shape[1], out_ref.shape[2] // 2
    for t in range(4):
        out_ref[t] = side_by_side(
            [grad_ref[:rows, (g * 4 + t) * cols : (g * 4 + t + 1) * cols] for g in range(2)]
        )


def pack_forward_kernel(me_ref, expand_ref, reduce_ref, out_ref):
    cols = reduce_ref.shape[1]
    for s, unit in enumerate(unit_table(8, 2)):
        at = slice(unit % 4 * cols, (unit % 4 + 1) * cols)
        out_ref[s] = side_by_side(
            [
                expand_ref[:cols, at],
                expand_ref[cols:, at],
                reduce_ref[unit * cols : (unit + 1) * cols],
            ]
        )


def unpack_forward_kernel(me_ref, got_ref, out_ref):
    cols = got_ref.shape[1]
    unit = me_ref[2] * 2 + me_ref[1]
    for half in range(2):
        parts = []
        for d in range(4):
            parts.append(got_ref[2 * d + unit // 4][:, half * cols : (half + 1) * cols])
        for s in range(4):
            parts.append(got_ref[4 * half + s][:, 2 * cols :])
        out_ref[half * cols : (half + 1) * cols] = side_by_side(parts)


def open_forward_kernel(me_ref, *refs):
    *refs, expand_ref, reduce_ref = refs
    height = refs[0].shape[-2]
    rows, width = height // 2, D // 2
    for plane, first, second in by_plane(me_ref, refs):
        expand_ref[rows_at(plane * height, height)] = side_by_side(
            [first[:, :width], second[:, :width]]
        )
        for group, piece in enumerate((first, second)):
            reduce_ref[rows_at(group * width + plane * rows, rows)] = side_by_side(
                [piece[:rows, width:], piece[rows:, width:]]
            )


def put_pieces(me_ref, outs, step, pair):
    if len(outs) == 1:
        outs[0][2 * step], outs[0][2 * step + 1] = pair
    else:
        outs[step][...] = jnp.where(me_ref[1] == 0, pair[0], pair[1])
        outs[4 + step][...] = jnp.where(me_ref[1] == 0, pair[1], pair[0])


def split_forward_kernel(me_ref, expand_ref, reduce_ref, *outs):
    height = outs[0].shape[-2]
    rows, width = height // 2, D // 2
    for step in range(4):
        plane = step if len(outs) == 1 else (me_ref[0] + 3 - step) % 4
        expand = expand_ref[rows_at(plane * height, height)]
        pair = []
        for group in range(2):
            reduce = reduce_ref[rows_at(group * width + plane * rows, rows)]
            part = expand[:, group * width : (group + 1) * width]
            upper = side_by_side([part[:rows], reduce[:, :width]])
            lower = side_by_side([part[rows:], reduce[:, width:]])
            pair.append(jnp.concatenate([upper, lower], axis=0))
        put_pieces(me_ref, outs, step, pair)


def pack_return_kernel(me_ref, whole_ref, out_ref):
    cols = out_ref.shape[1]
    for s in range(8):
        at = slice(s // 2 * cols, (s // 2 + 1) * cols)
        right = slice((4 + s % 4) * cols, (5 + s % 4) * cols)
        out_ref[s] = side_by_side(
            [
                whole_ref[:cols, at],
                whole_ref[cols:, at],
                whole_ref[s // 4 * cols : (s // 4 + 1) * cols, right],
            ]
        )


def unpack_return_kernel(me_ref, got_ref, expand_ref, reduce_ref):
    cols = got_ref.shape[1]
    for half in range(2):
        parts = []
        for q in range(4):
            device = q % 2 * 4 + 2 * (me_ref[2] % 2) + q // 2
            parts.append(got_ref[device][:, half * cols : (half + 1) * cols])
        expand_ref[half * cols : (half + 1) * cols] = side_by_side(parts).astype(F32)
    for s, unit in enumerate(unit_table(8, 2)):
        reduce_ref[unit * cols : (unit + 1) * cols] = got_ref[s][:, 2 * cols :].astype(F32)


def split_attention_kernel(me_ref, joint_ref, project_ref, *outs):
    cols = outs[0].shape[-2]
    for step in range(4):
        plane = step if len(outs) == 1 else (me_ref[0] + 3 - step) % 4
        parts = [[], []]
        for half in range(2):
            rows = joint_ref[rows_at(plane * 2 * cols + half * cols, cols)]
            project = project_ref[plane, half * cols : (half + 1) * cols]
            for group in range(2):
                for kind in range(3):
                    at = kind * WIDTH + group * cols
                    parts[group].append(rows[:, at : at + cols])
                parts[group].append(project[:, group * cols : (group + 1) * cols])
        put_pieces(me_ref, outs, step, [side_by_side(part) for part in parts])


def unpack_attention_kernel(me_ref, whole_ref, a_ref, b_ref, c_ref, project_ref):
    cols = whole_ref.shape[0]
    for half in range(2):
        rows = slice(half * cols, (half + 1) * cols)
        parts = []
        for k in range(4):
            at = (half * 4 + k) * cols
            parts.append(whole_ref[:, at : at + cols])
        for r, ref in enumerate((a_ref, b_ref, c_ref)):
            ref[rows] = choose(kind_sent(me_ref, r), parts[:3]).astype(BF16)
        project_ref[rows] = parts[3].astype(F32)


def pack_attention(joint, project):
    got = deal_joint(joint)
    if not compact():
        return pack_attention_any(got, project)
    cols = project.shape[1]
    outs = [((cols, 8 * cols), BF16)]
    return rearrange(pack_attention_kernel, [*got, project], outs, "pack_attention")[0]


def pack_forward(expand, reduce, *events):
    cols = reduce.shape[1]
    if compact():
        outs = [((8, cols, 3 * cols), BF16)]
        (chunks,) = rearrange(pack_forward_kernel, [expand, reduce], outs, "pack_forward")
    else:
        chunks = pack_forward_any(expand, reduce)
    got = after(lax.all_to_all(chunks, SEQ, 0, 0, tiled=True), *events)
    if not compact():
        return unpack_forward_any(got)
    return rearrange(
        unpack_forward_kernel, [got], [((2 * cols, 8 * cols), BF16)], "unpack_forward"
    )[0]


def gather_slow(pack):
    return [lax.all_gather(pack, OWNERS, axis=0, tiled=False)]


def gather_planes(pack):
    return [pack] + [from_plane(pack, back) for back in range(1, 4)]


def open_attention(pieces):
    if not compact():
        return open_attention_any(pieces[0])
    cols = D // 8
    outs = [((D, 3 * WIDTH), BF16), ((TP, 2 * cols, 2 * cols), BF16)]
    return rearrange(open_attention_kernel, pieces, outs, "open_attention")


def project_matrix(columns):
    got = lax.all_to_all(columns, "member", 0, 0, tiled=True)
    if not compact():
        return join_project_any(got)
    return rearrange(join_project_kernel, [got], [((WIDTH, D), BF16)], "join_project")[0]


def open_forward(pieces):
    if not compact():
        return open_forward_any(pieces[0])
    outs = [((D, D), BF16), ((D, D), BF16)]
    return rearrange(open_forward_kernel, pieces, outs, "open_forward")


def piece_outs(shape, fast):
    return [(shape, BF16)] * 8 if fast else [((8,) + shape, BF16)]


def split_project(g_project):
    if compact():
        outs = [((TP, D // TP, D // TP), BF16)]
        (chunks,) = rearrange(split_project_kernel, [g_project], outs, "split_project")
    else:
        chunks = split_project_any(g_project)
    return lax.all_to_all(chunks, "member", 0, 0, tiled=True)


def split_attention(g_joint, project, fast):
    if not compact():
        return [split_attention_any(g_joint, project)]
    outs = piece_outs((D // 8, D), fast)
    return rearrange(split_attention_kernel, [g_joint, project], outs, "split_attention")


def split_forward(g_expand, g_reduce, fast):
    if not compact():
        return [split_forward_any(g_expand, g_reduce)]
    outs = piece_outs((D // 4, D), fast)
    return rearrange(split_forward_kernel, [g_expand, g_reduce], outs, "split_forward")


def owner_sum(pieces, step, carried, *events):
    own, other = pieces[step], after(pieces[4 + step], *events)
    total = own.astype(F32) + exchange(other, TP).astype(F32)
    if step:
        total = total + from_plane(carried, 1).astype(F32)
    return total.astype(BF16)


def owner_sum_slow(pieces):
    return lax.psum_scatter(pieces[0], OWNERS, scatter_dimension=0, tiled=False)


def return_attention(owned):
    if compact():
        cols = D // 8
        outs = [((2 * cols, cols), BF16)] * 3 + [((2 * cols, cols), F32)]
        *parts, project = rearrange(unpack_attention_kernel, [owned], outs, "unpack_attention")
    else:
        *parts, project = unpack_attention_any(owned)
    return return_joint(parts), project


def return_forward(owned):
    cols = D // 8
    if compact():
        outs = [((8, cols, 3 * cols), BF16)]
        (chunks,) = rearrange(pack_return_kernel, [owned], outs, "pack_return")
    else:
        chunks = pack_return_any(owned)
    got = lax.all_to_all(chunks, SEQ, 0, 0, tiled=True)
    if not compact():
        return unpack_return_any(got)
    outs = [((2 * cols, 4 * cols), F32), ((8 * cols, cols), F32)]
    return rearrange(unpack_return_kernel, [got], outs, "unpack_return")


def half_call(body, half, chunks, matrices, tokens, into, partial, name):
    count = chunks[0].shape[0]

    def whole(array):
        return pl.BlockSpec(array.shape, lambda i: (0,) * array.ndim)

    def slot(shape):
        return pl.BlockSpec(shape, lambda i: (2 * half + i,) + (0,) * (len(shape) - 1))

    kept = [array for _, array in into if array is not None]
    operands = [*chunks, *matrices, *tokens]
    specs = [whole(array) for array in (*chunks, *matrices)]
    specs += [slot((array.shape[0] // TP,) + array.shape[1:]) for array in tokens]
    out_specs = [slot((count, width)) for width, _ in into]
    shapes = [jax.ShapeDtypeStruct((TP * count, width), BF16) for width, _ in into]
    if partial:
        out_specs += [pl.BlockSpec((count, D), lambda i: (0, 0))] * 2
        shapes += [jax.ShapeDtypeStruct((count, D), BF16)] * 2
    aliases = {len(operands) + k: k for k in range(len(kept))}
    work = sum(2 * 2 * count * math.prod(matrix.shape) for matrix in matrices)

    def kernel(a_ref, b_ref, *refs):
        n = len(matrices) + len(tokens)
        mine = pl.program_id(0) == 0
        rows = jnp.where(mine, a_ref[...], b_ref[...])
        body(rows, mine, refs[:n], refs[n + len(kept) :])

    return pl.pallas_call(
        kernel,
        grid=(2,),
        in_specs=specs + [pl.BlockSpec(memory_space=pl.ANY)] * len(kept),
        out_specs=out_specs,
        out_shape=shapes,
        input_output_aliases=aliases,
        compiler_params=kernel_params(),
        cost_estimate=pl.CostEstimate(
            flops=work, bytes_accessed=work // 512, transcendentals=2 * count * D
        ),
        name=name,
    )(*operands, *kept)


def put_partial(mine, value, a_ref, b_ref):
    value = value.astype(BF16)

    @pl.when(mine)
    def _():
        a_ref[...] = value

    @pl.when(jnp.logical_not(mine))
    def _():
        b_ref[...] = value


def chunks_of(width):
    return [slice(at, min(at + CHUNK, width)) for at in range(0, width, CHUNK)]


def joint_body(rows, mine, refs, outs):
    outs[0][...] = dot(rows, refs[0][...]).astype(BF16)


def forward_body(rows, mine, refs, outs):
    expand_ref, reduce_ref, sides_ref, active_ref = refs
    activated_ref, slope_ref, a_ref, b_ref = outs
    root = math.sqrt(2.0 / math.pi)
    before, now = sides_ref[:, 0:1], sides_ref[:, 1:2]
    for at in chunks_of(LOCAL_FF):
        pre = dot(rows, expand_ref[:, at])
        square = pre * pre
        curve = jnp.tanh(root * pre * (1.0 + 0.044715 * square))
        half = 0.5 + 0.5 * curve
        mask = before * active_ref[0, 0:1, at] + now * active_ref[0, 1:2, at]
        slope = half + pre * (half - half * half) * (2.0 * root * (1.0 + 0.134145 * square))
        activated_ref[:, at] = (pre * half * mask).astype(BF16)
        slope_ref[:, at] = (slope * mask).astype(BF16)
    put_partial(mine, dot(activated_ref[...], reduce_ref[...]), a_ref, b_ref)


def backward_body(rows, mine, refs, outs):
    expand_ref, reduce_ref, slope_ref = refs
    d_pre_ref, a_ref, b_ref = outs
    for at in chunks_of(LOCAL_FF):
        d_active = against_cols(rows, reduce_ref[at])
        d_pre_ref[:, at] = (d_active * slope_ref[:, at].astype(F32)).astype(BF16)
    put_partial(mine, against_cols(d_pre_ref[...], expand_ref[...]), a_ref, b_ref)


def head_tiles(head):
    low = head * HEAD_DIM // LANES * LANES
    high = -(-(head + 1) * HEAD_DIM // LANES) * LANES
    return low, high


def lanes_of(head, shape):
    low, high = head_tiles(head)
    lane = lax.broadcasted_iota(jnp.int32, shape, 1) + low
    return (lane >= head * HEAD_DIM) & (lane < (head + 1) * HEAD_DIM)


def key_tiles(refs, halos, block, base, low, high):
    before_ref, after_ref = halos
    prev_ref, here_ref, next_ref = refs
    prev = jnp.where(block == 0, before_ref[:, base + low : base + high], prev_ref[:, low:high])
    following = jnp.where(
        block == TP - 1, after_ref[:, base + low : base + high], next_ref[:, low:high]
    )
    return prev, here_ref[:, low:high], following


def attend_kernel(
    me_ref,
    q_ref,
    *refs,
):
    keys, values, halos = refs[0:3], refs[3:6], refs[6:8]
    segq_ref, segk_ref, head_ref, mixed_ref, lse_ref = refs[8:]
    block = pl.program_id(0) ^ me_ref[2]
    count = q_ref.shape[0]
    allowed = segq_ref[...] == segk_ref[0]
    tiles = [jnp.zeros((count, LANES), F32) for _ in range(WIDTH // LANES)]
    total = jnp.zeros((count, LANES), F32)
    lane = lax.broadcasted_iota(jnp.int32, (count, LANES), 1)
    for head in range(LOCAL_HEADS):
        low, high = head_tiles(head)
        mine = lanes_of(head, (count, high - low))
        query = jnp.where(mine, q_ref[:, low:high], 0)
        key = key_tiles(keys, halos, block, 0, low, high)
        scores = jnp.concatenate([against_cols(query, part) for part in key], axis=1) * FACTOR
        scores = jnp.where(allowed, scores, NEGATIVE)
        highest = jnp.max(scores, axis=-1, keepdims=True)
        weights = jnp.exp(scores - highest)
        sums = jnp.sum(weights, axis=-1, keepdims=True)
        probs = (weights / sums).astype(BF16)
        out, at = 0.0, 0
        for part in key_tiles(values, halos, block, WIDTH, low, high):
            out = out + dot(probs[:, at : at + part.shape[0]], part)
            at += part.shape[0]
        out = jnp.where(mine, out, 0.0) * head_ref[:, head : head + 1]
        for k in range(low // LANES, high // LANES):
            at = k * LANES - low
            tiles[k] = tiles[k] + out[:, at : at + LANES]
        total = jnp.where(lane == head, highest + jnp.log(sums), total)
    for k, tile in enumerate(tiles):
        mixed_ref[:, k * LANES : (k + 1) * LANES] = tile.astype(BF16)
    lse_ref[...] = total


def attend_back_kernel(me_ref, q_ref, *refs):
    keys, values, halos = refs[0:3], refs[3:6], refs[6:8]
    grad_ref, mixed_ref, lse_ref, segq_ref, segk_ref, head_ref = refs[8:14]
    d_joint_ref, d_before_ref, d_after_ref, sum_ref = refs[14:]
    step = pl.program_id(0)
    block = step ^ me_ref[2]
    count = q_ref.shape[0]

    @pl.when(step == 0)
    def _():
        sum_ref[...] = jnp.zeros_like(sum_ref)

    prev = jnp.where(block == 0, TP, jnp.maximum(block - 1, 0) ^ me_ref[2])
    following = jnp.where(block == TP - 1, TP + 1, jnp.minimum(block + 1, TP - 1) ^ me_ref[2])
    windows = [
        (pl.ds(pl.multiple_of(prev * count, count), count), 0),
        (pl.ds(pl.multiple_of(step * count, count), count), count),
        (pl.ds(pl.multiple_of(following * count, count), AFTER), 2 * count),
    ]
    rows = pl.ds(pl.multiple_of(step * count, count), count)
    allowed = segq_ref[...] == segk_ref[0]
    tiles = [jnp.zeros((count, LANES), F32) for _ in range(WIDTH // LANES)]
    for head in range(LOCAL_HEADS):
        low, high = head_tiles(head)
        mine = lanes_of(head, (count, high - low))
        query = jnp.where(mine, q_ref[:, low:high], 0)
        key = key_tiles(keys, halos, block, 0, low, high)
        value = key_tiles(values, halos, block, WIDTH, low, high)
        active = head_ref[:, head : head + 1]
        grad = jnp.where(mine, grad_ref[:, low:high].astype(F32) * active, 0.0)
        balance = jnp.sum(grad * mixed_ref[:, low:high].astype(F32), axis=-1, keepdims=True)
        grad = grad.astype(BF16)
        scores = jnp.concatenate([against_cols(query, part) for part in key], axis=1) * FACTOR
        probs = jnp.where(allowed, jnp.exp(scores - lse_ref[:, head : head + 1]), 0.0)
        d_probs = jnp.concatenate([against_cols(grad, part) for part in value], axis=1)
        d_scores = (probs * (d_probs - balance)).astype(BF16)
        probs = probs.astype(BF16)
        d_query = 0.0
        for (window, at), part in zip(windows, key):
            piece = d_scores[:, at : at + part.shape[0]]
            d_query = d_query + dot(piece, part)
            sum_ref[window, low:high] += through_rows(piece, query) * FACTOR
            sum_ref[window, WIDTH + low : WIDTH + high] += through_rows(
                probs[:, at : at + part.shape[0]], grad
            )
        d_query = jnp.where(mine, d_query, 0.0)
        for k in range(low // LANES, high // LANES):
            at = k * LANES - low
            tiles[k] = tiles[k] + d_query[:, at : at + LANES]
    for k, tile in enumerate(tiles):
        d_joint_ref[rows, k * LANES : (k + 1) * LANES] = (tile * FACTOR).astype(BF16)

    @pl.when(step == pl.num_programs(0) - 1)
    def _():
        d_joint_ref[:, WIDTH:] = sum_ref[: TP * count].astype(BF16)
        d_before_ref[...] = sum_ref[TP * count : (TP + 1) * count].astype(BF16)
        d_after_ref[...] = sum_ref[(TP + 1) * count : (TP + 1) * count + AFTER].astype(BF16)


def kernel_params():
    return pltpu.CompilerParams(
        dimension_semantics=("arbitrary",), vmem_limit_bytes=48 * 1024 * 1024
    )


def block_specs(count):
    def rows(width):
        return pl.BlockSpec((count, width), lambda j, me: (j, 0))

    def whole(shape):
        return pl.BlockSpec(shape, lambda j, me: (0,) * len(shape))

    def around(kind):
        def before(j, me):
            return (jnp.maximum((j ^ me[2]) - 1, 0) ^ me[2], kind)

        def following(j, me):
            return ((jnp.minimum((j ^ me[2]) + 1, TP - 1) ^ me[2]) * (count // AFTER), kind)

        return [
            pl.BlockSpec((count, WIDTH), before),
            pl.BlockSpec((count, WIDTH), lambda j, me: (j, kind)),
            pl.BlockSpec((AFTER, WIDTH), following),
        ]

    fixed = [rows(WIDTH)] + around(1) + around(2)
    return rows, whole, fixed + [whole((count, 2 * WIDTH)), whole((AFTER, 2 * WIDTH))]


def attend(joint, halos, segq, segk, heads):
    span = segk.shape[2]
    count = joint.shape[0] // TP
    rows, whole, specs = block_specs(count)
    return pl.pallas_call(
        attend_kernel,
        grid_spec=pltpu.PrefetchScalarGridSpec(
            num_scalar_prefetch=1,
            grid=(TP,),
            in_specs=specs
            + [
                rows(1),
                pl.BlockSpec((1, 1, span), lambda j, me: (j, 0, 0)),
                rows(LANES),
            ],
            out_specs=[rows(WIDTH), rows(LANES)],
        ),
        out_shape=[
            jax.ShapeDtypeStruct((TP * count, WIDTH), BF16),
            jax.ShapeDtypeStruct((TP * count, LANES), F32),
        ],
        compiler_params=kernel_params(),
        cost_estimate=pl.CostEstimate(
            flops=8 * TP * count * span * LANES * LOCAL_HEADS,
            bytes_accessed=TP * count * WIDTH * 8,
            transcendentals=TP * count * span * LOCAL_HEADS,
        ),
        name="attend",
    )(here(), *[joint] * 7, *halos, segq, segk, heads)


def attend_back(joint, halos, grad, mixed, log_total, segq, segk, heads):
    span = segk.shape[2]
    count = joint.shape[0] // TP
    rows, whole, specs = block_specs(count)
    shapes = [(TP * count, 3 * WIDTH), (count, 2 * WIDTH), (AFTER, 2 * WIDTH)]
    return pl.pallas_call(
        attend_back_kernel,
        grid_spec=pltpu.PrefetchScalarGridSpec(
            num_scalar_prefetch=1,
            grid=(TP,),
            in_specs=specs
            + [
                rows(WIDTH),
                rows(WIDTH),
                rows(LANES),
                rows(1),
                pl.BlockSpec((1, 1, span), lambda j, me: (j, 0, 0)),
                rows(LANES),
            ],
            out_specs=[whole(shape) for shape in shapes],
            scratch_shapes=[pltpu.VMEM(((TP + 2) * count, 2 * WIDTH), F32)],
        ),
        out_shape=[jax.ShapeDtypeStruct(shape, BF16) for shape in shapes],
        compiler_params=kernel_params(),
        cost_estimate=pl.CostEstimate(
            flops=20 * TP * count * span * LANES * LOCAL_HEADS,
            bytes_accessed=TP * count * WIDTH * 20,
            transcendentals=TP * count * span * LOCAL_HEADS,
        ),
        name="attend_back",
    )(here(), *[joint] * 7, *halos, grad, mixed, log_total, segq, segk, heads)


def halos_of(joint):
    _, groups, _ = sizes()
    count = joint.shape[0] // TP
    if groups == 1:
        return [jnp.zeros((rows, 2 * WIDTH), joint.dtype) for rows in (count, AFTER)]
    group, member = place()
    column = jnp.int32(WIDTH)
    last = ((member ^ (TP - 1)) * count, column)
    if groups == 2:
        first = (member * count, column)
        start = [jnp.where(group == 0, x, y) for x, y in zip(last, first)]
        got = exchange(lax.dynamic_slice(joint, start, (count, 2 * WIDTH)), TP)
        return [got, got]
    last = lax.dynamic_slice(joint, last, (count, 2 * WIDTH))
    first = lax.dynamic_slice(joint, (member * count, column), (AFTER, 2 * WIDTH))
    return [shifted(last, TP), shifted(first, -TP)]


def halos_back(d_joint, d_before, d_after):
    _, groups, _ = sizes()
    if groups == 1:
        return d_joint
    group, member = place()
    count = d_joint.shape[0] // TP
    last, first = (member ^ (TP - 1)) * count, member * count
    if groups == 2:
        d_after = jnp.pad(d_after, ((0, count - AFTER), (0, 0)))
        got = exchange(jnp.where(group == 0, d_after, d_before), TP)
        pieces = [(got, jnp.where(group == 0, last, first))]
    else:
        pieces = [(shifted(d_before, -TP), last), (shifted(d_after, TP), first)]
    for piece, at in pieces:
        start = (at, jnp.int32(WIDTH))
        sums = lax.dynamic_slice(d_joint, start, piece.shape)
        sums = (sums.astype(F32) + piece.astype(F32)).astype(BF16)
        d_joint = lax.dynamic_update_slice(d_joint, sums, start)
    return d_joint


def normed(stream):
    center = stream - jnp.mean(stream, axis=-1, keepdims=True)
    scale = lax.rsqrt(jnp.mean(center * center, axis=-1, keepdims=True) + EPS)
    return center * scale, scale


def norm_back(grad, unit, scale):
    mean = jnp.mean(grad, axis=-1, keepdims=True)
    slope = jnp.mean(grad * unit, axis=-1, keepdims=True)
    return scale * (grad - mean - unit * slope)


def per_token(vectors, sides):
    return sides[0] * vectors[0][None, :] + sides[1] * vectors[1][None, :]


def per_crop(value, sides):
    return jnp.stack([jnp.sum(value * sides[0], axis=0), jnp.sum(value * sides[1], axis=0)])


def step_embed(stamps, breadth):
    halfway = breadth // 2
    frequency = jnp.exp(-math.log(10000.0) * jnp.arange(halfway, dtype=F32) / halfway)
    angles = stamps.astype(F32)[..., None] * frequency
    return jnp.concatenate([jnp.cos(angles), jnp.sin(angles)], axis=-1)


def segment_of(places, bounds):
    return jnp.sum((places[:, None] >= bounds[None, :]).astype(jnp.int32), axis=-1)


def layer_forward(stream, mod, w_joint, project_columns, open_reduce, masks, context, hold):
    head_tok, active, keeping = masks
    sides, living, segq, segk, slot_sides = context
    offset_one, stretch_one, gate_one, offset_two, stretch_two, gate_two = [
        per_token(mod[:, i], sides) for i in range(6)
    ]
    count = stream.shape[0]
    unit_one, _ = normed(stream)
    mine = (unit_one * (1.0 + stretch_one) + offset_one).astype(BF16)
    mine = hold("normed_one", mine)
    theirs, ours = exchange(mine, 2), near(mine)
    (joint,) = half_call(
        joint_body, 0, ours, [w_joint], [], [(3 * WIDTH, None)], False, "joint_near"
    )
    theirs = far(after(theirs, joint))
    (joint,) = half_call(
        joint_body, 1, theirs, [w_joint], [], [(3 * WIDTH, joint)], False, "joint_far"
    )
    normed_one = ours + theirs
    halos = halos_of(joint)
    w_project = project_matrix(after(project_columns, joint))
    halos = hold("halos", halos)
    mixed, log_total = attend(joint, halos, segq, segk, head_tok)
    mixed = hold("mixed", mixed)

    def branch_parts(rows, slots):
        return [dot(rows[j * count : (j + 1) * count], w_project).astype(BF16) for j in slots]

    away = pair_sum(branch_parts(mixed, (2, 3)))
    close = pair_sum(branch_parts(after(mixed, away), (0, 1)))
    branch = after(hold("branch", far_sum(away)), close) + close
    middle = stream + gate_one * branch * living
    unit_two, _ = normed(middle)
    mine = (unit_two * (1.0 + stretch_two) + offset_two).astype(BF16)
    theirs, ours = exchange(mine, 2), near(mine)
    w_expand, w_reduce = open_reduce(mine)
    matrices, tokens = [w_expand, w_reduce], [slot_sides, active]
    activated, slope, *parts = half_call(
        forward_body, 0, ours, matrices, tokens, [(LOCAL_FF, None)] * 2, True, "forward_near"
    )
    close = pair_sum(parts)
    theirs = far(after(theirs, activated))
    activated, slope, *parts = half_call(
        forward_body,
        1,
        theirs,
        matrices,
        tokens,
        [(LOCAL_FF, activated), (LOCAL_FF, slope)],
        True,
        "forward_far",
    )
    away = pair_sum(parts)
    feedout = hold("feedout", far_sum(away), away) + close
    result = middle + gate_two * feedout * keeping
    record = (
        stream,
        normed_one,
        joint,
        halos,
        mixed,
        log_total,
        branch,
        middle,
        ours + theirs,
        slope,
        activated,
        feedout,
    )
    return result, record, (w_joint, w_project, w_expand, w_reduce)


def layer_backward(adjoint, record, mod, weights, masks, context, last, hold):
    (
        stream,
        normed_one,
        joint,
        halos,
        mixed,
        log_total,
        branch,
        middle,
        normed_two,
        slope,
        activated,
        feedout,
    ) = record
    w_joint, w_project, w_expand, w_reduce = weights
    head_tok, active, keeping = masks
    sides, living, segq, segk, slot_sides = context
    offset_one, stretch_one, gate_one, offset_two, stretch_two, gate_two = [
        per_token(mod[:, i], sides) for i in range(6)
    ]
    count = stream.shape[0]
    fast = last and compact()
    mine = (adjoint * gate_two * keeping).astype(BF16)
    theirs, ours = exchange(mine, 2), near(mine)
    matrices = [w_expand, w_reduce]
    d_pre, *parts = half_call(
        backward_body, 0, ours, matrices, [slope], [(LOCAL_FF, None)], True, "backward_near"
    )
    close = pair_sum(parts)
    theirs = far(after(theirs, d_pre))
    d_pre, *parts = half_call(
        backward_body, 1, theirs, matrices, [slope], [(LOCAL_FF, d_pre)], True, "backward_far"
    )
    away = pair_sum(parts)
    d_feed = jnp.concatenate(ours + theirs, axis=0)
    g_reduce = through_rows(activated, after(d_feed, away)).astype(BF16)
    d_gate_two = per_crop(after(adjoint, away) * feedout * keeping, sides)
    unit_two, scale_two = normed(middle)
    d_normed_two = after(far_sum(away), g_reduce, d_gate_two) + close
    d_middle = adjoint + norm_back(d_normed_two * (1.0 + stretch_two), unit_two, scale_two)
    mine = (d_middle * gate_one * living).astype(BF16)
    theirs, ours = exchange(mine, 2), near(mine)
    rows = after(jnp.concatenate(normed_two, axis=0), mine)
    g_expand = through_rows(rows, d_pre).astype(BF16)
    forward_pieces = split_forward(g_expand, g_reduce, fast)
    d_offset_two = per_crop(after(d_normed_two, mine), sides)
    d_stretch_two = per_crop(after(d_normed_two, mine) * unit_two, sides)
    theirs = after(theirs, forward_pieces, d_offset_two, d_stretch_two)
    if fast:
        forward_sum = owner_sum(forward_pieces, 0, None)
    else:
        forward_sum = owner_sum_slow(forward_pieces)
    d_branch = jnp.concatenate(ours + far(theirs), axis=0)
    d_mixed = against_cols(d_branch, w_project).astype(BF16)
    g_project = split_project(through_rows(mixed, d_branch).astype(BF16))
    if fast:
        d_mixed = after(d_mixed, forward_sum)
        forward_sum = owner_sum(forward_pieces, 1, forward_sum)
    d_joint = halos_back(
        *attend_back(joint, halos, d_mixed, mixed, log_total, segq, segk, head_tok)
    )
    d_joint = hold("d_joint", d_joint)
    if fast:
        d_joint = after(d_joint, forward_sum)

    def normed_parts(rows, slots):
        return [against_cols(rows[j * count : (j + 1) * count], w_joint).astype(BF16) for j in slots]

    if last:
        g_joint = through_rows(jnp.concatenate(normed_one, axis=0), d_joint).astype(BF16)
        attention_pieces = split_attention(g_joint, g_project, fast)
        away = pair_sum(normed_parts(after(d_joint, attention_pieces), (2, 3)))
    else:
        away = pair_sum(normed_parts(d_joint, (2, 3)))
        rows = after(jnp.concatenate(normed_one, axis=0), away)
        g_joint = through_rows(rows, d_joint).astype(BF16)
        attention_pieces = split_attention(g_joint, g_project, fast)
    close = pair_sum(normed_parts(after(d_joint, away), (0, 1)))
    d_normed_one = after(far_sum(away), close, attention_pieces) + close
    if fast:
        attention_sum = None
        for step in range(4):
            attention_sum = owner_sum(attention_pieces, step, attention_sum)
        for step in (2, 3):
            forward_sum = owner_sum(forward_pieces, step, forward_sum, attention_pieces)
    else:
        attention_sum = owner_sum_slow(attention_pieces)
    unit_one, scale_one = normed(stream)
    d_stream = d_middle + norm_back(d_normed_one * (1.0 + stretch_one), unit_one, scale_one)
    d_gate_one = per_crop(d_middle * branch * living, sides)
    d_offset_one = per_crop(d_normed_one, sides)
    d_stretch_one = per_crop(d_normed_one * unit_one, sides)
    d_mod = jnp.stack(
        [d_offset_one, d_stretch_one, d_gate_one, d_offset_two, d_stretch_two, d_gate_two], axis=1
    )
    return d_stream, d_mod, attention_sum, forward_sum


def shards(
    hidden_in,
    lengths,
    timesteps,
    head_mask,
    group_mask,
    skip_mask,
    modulation_weight,
    joint_weight,
    project_weight,
    expand_weight,
    reduce_weight,
    cotangent,
):
    seq, groups, planes = sizes()
    block = hidden_in.shape[1]
    crops = lengths.shape[1]
    mine = lax.axis_index(SEQ)
    plane = lax.axis_index("dp")
    group, member = place()
    height = D // planes

    pack = pack_attention(joint_weight[0], project_weight[0])
    if compact():
        first = gather_planes(pack)
        forward_first = gather_planes(
            pack_forward(*after((expand_weight[0], reduce_weight[0]), pack), first)
        )
        first = first + [exchange(piece, TP) for piece in first]
    else:
        first = gather_slow(pack)
        forward_first = gather_slow(pack_forward(expand_weight[0], reduce_weight[0]))
    opened = [open_attention(first)]
    packs = []
    held = first[:4]
    for l in range(1, LAYERS):
        attention = pack_attention(*after((joint_weight[l], project_weight[l]), held))
        held = after((expand_weight[l], reduce_weight[l]), attention)
        packs.append((attention, pack_forward(*held)))
        held = packs[-1]

    stamps = jnp.zeros((planes, crops), jnp.int32)
    for step in range(planes):
        row = from_plane(timesteps[0], step) if step else timesteps[0]
        stamps = jnp.where(
            (jnp.arange(planes) == (plane - step) % planes)[:, None], row[None, :], stamps
        )
    stamps = stamps.reshape(planes * crops)
    embedded = jax.nn.silu(step_embed(stamps, D)).astype(BF16)
    condition = lax.dynamic_slice_in_dim(embedded, plane * height, height, axis=1)
    part = jnp.stack([dot(condition, modulation_weight[l]) for l in range(LAYERS)], axis=1)
    before = jnp.concatenate([jnp.zeros_like(part[:1]), part[:-1]])
    part = jnp.stack([before, part], axis=1)
    part = after(lax.all_to_all(part, EVERY, 0, 0, tiled=True), first[:4])
    part = jnp.sum(part.reshape((planes, seq) + part.shape[1:]), axis=0)
    mods = jnp.transpose(part, (2, 1, 0, 3)).reshape(LAYERS, 2, 6, D)

    bounds = jnp.cumsum(lengths[0])
    span = 2 * block + AFTER
    places = (group * TP - 1) * block + jnp.arange((TP + 1) * block + AFTER, dtype=jnp.int32)
    inside = (places >= 0) & (places < seq * block)
    segment = jnp.where(inside, segment_of(places, bounds), -1)
    segk = jnp.stack(
        [lax.dynamic_slice_in_dim(segment, (member ^ j) * block, span) for j in range(TP)]
    )[:, None, :]
    segq = segk[:, 0, block : 2 * block].reshape(TP * block, 1)
    own = segment_of(mine * block + jnp.arange(block, dtype=jnp.int32), bounds)[:, None]
    sides = [(own == mine - 1).astype(F32), ((own == mine) & (own < crops)).astype(F32)]
    living = (own < crops).astype(F32)
    onehot = (segq == jnp.arange(crops, dtype=jnp.int32)[None, :]).astype(BF16)
    blocks = jnp.stack([group * TP + (member ^ j) for j in range(TP)])
    firsts = jnp.repeat(blocks, block)[:, None]
    slot_sides = jnp.concatenate([segq == firsts - 1, (segq == firsts) & (segq < crops)], axis=1)
    context = (sides, living, segq, segk, slot_sides.astype(F32))
    rows = FF // (planes * seq)
    units = member * groups + jnp.arange(groups, dtype=jnp.int32)
    starts = (FF // planes) * jnp.arange(planes, dtype=jnp.int32)[None, :] + rows * units[:, None]
    hidden_here = (starts[:, :, None] + jnp.arange(rows, dtype=jnp.int32)).reshape(LOCAL_FF)
    spread = (hidden_here // (FF // GROUPS))[None, :] == jnp.arange(GROUPS)[:, None]
    masks = []
    for l in range(LAYERS):
        heads_on = lax.dynamic_slice_in_dim(head_mask[0, l], member * LOCAL_HEADS, LOCAL_HEADS, 1)
        heads_on = jnp.pad(heads_on.astype(BF16), ((0, 0), (0, LANES - LOCAL_HEADS)))
        groups_on = dot(group_mask[0, l].astype(BF16), spread.astype(BF16))
        groups_on = jnp.pad(groups_on, ((1, 0), (0, 0)))
        active = jnp.stack(
            [lax.dynamic_slice_in_dim(groups_on, blocks[j], 2) for j in range(TP)]
        )
        keeping = skip_mask[0, l].astype(F32)[:, None] * living
        masks.append((dot(onehot, heads_on), active, keeping))

    stream = hidden_in[0].astype(F32)
    records, weights, gathered = [], [], []
    for attention, forward in packs:
        gathered.append((gather_slow(attention), gather_slow(forward)))
    w_joint, project_columns = opened[0]
    for l in range(LAYERS):
        events, following = {}, None
        if l + 1 < LAYERS:
            following = open_attention(gathered[l][0])
            events["feedout"] = [following]
        if l == 0 and compact():
            others = [exchange(after(forward_first[0], w_joint), TP)]
            events["normed_one"] = [forward_first[0]]
            events["halos"] = [packs[0][0]]
            events["mixed"] = [others[0], packs[0][1]]

        def hold(name, value, *more, events=events, l=l):
            if l == 0 and compact() and name == "halos":
                others.extend(exchange(after(p, value), TP) for p in forward_first[1:])
                events["branch"] = others[1:3]
            return after(value, *more, *events.get(name, []))

        def open_here(mine, l=l):
            if l == 0:
                return open_forward(forward_first + others if compact() else forward_first)
            return open_forward(gathered[l - 1][1])

        stream, record, used = layer_forward(
            stream, mods[l], w_joint, project_columns, open_here, masks[l], context, hold
        )
        records.append(record)
        weights.append(used)
        if following is not None:
            w_joint, project_columns = following
    final_state = stream.astype(BF16)[None]
    adjoint = cotangent[0].astype(F32)
    grads, d_mods = [None] * LAYERS, [None] * LAYERS
    returned = []
    for l in reversed(range(LAYERS)):

        def hold(name, value, returned=tuple(returned)):
            return after(value, *returned)

        adjoint, d_mods[l], attention, forward = layer_backward(
            adjoint, records[l], mods[l], weights[l], masks[l], context, l == 0, hold
        )
        forward = tuple(return_forward(forward))
        grads[l] = return_attention(attention) + forward
        returned.append(forward)

    d_mod = jnp.stack(d_mods, axis=1)
    d_mod = d_mod[1] + shifted(d_mod[0], -1)
    d_mod = jnp.transpose(d_mod.reshape(LAYERS, seq, 6 * D // seq), (1, 0, 2))
    d_mod = jnp.broadcast_to(d_mod[None], (planes,) + d_mod.shape)
    d_mod = d_mod.reshape((planes * seq,) + d_mod.shape[2:])
    d_mod = lax.all_to_all(d_mod, EVERY, 0, 0, tiled=True)
    modulation_grad = jnp.stack(
        [
            lax.dot_general(
                condition.astype(F32),
                d_mod[:, l],
                (((0,), (0,)), ((), ())),
                precision=HIGH,
                preferred_element_type=F32,
            )
            for l in range(LAYERS)
        ]
    )
    joint_grad, project_grad, expand_grad, reduce_grad = [
        jnp.stack([grads[l][i] for l in range(LAYERS)]) for i in range(4)
    ]
    return (
        final_state,
        adjoint[None],
        modulation_grad,
        joint_grad,
        project_grad,
        expand_grad,
        reduce_grad,
    )


def solution(mesh):
    planes, seq = mesh.shape["dp"], mesh.shape["seq"]
    mesh = Mesh(mesh.devices.reshape(planes, seq // TP, TP), EVERY)
    in_specs = (
        P("dp", SEQ, None),
        P("dp", None),
        P("dp", None),
        P("dp", None, None, None),
        P("dp", None, None, None),
        P("dp", None, SEQ),
        P(None, "dp", SEQ),
        P(None, "dp", SEQ),
        P(None, "dp", SEQ),
        P(None, "dp", SEQ),
        P(None, "dp", SEQ),
        P("dp", SEQ, None),
    )
    out_specs = (
        P("dp", SEQ, None),
        P("dp", SEQ, None),
        P(None, "dp", SEQ),
        P(None, "dp", SEQ),
        P(None, "dp", SEQ),
        P(None, "dp", SEQ),
        P(None, "dp", SEQ),
    )
    return jax.shard_map(shards, mesh=mesh, in_specs=in_specs, out_specs=out_specs, check_vma=False)
```

time: 1020 us -> 900 us (0.88)
  local copies, waits for them, and re-layouts: 214 us -> 70.1 us
  Pallas kernels: 48.2 us -> 177 us
  other arithmetic: 128 us -> 75.6 us
  matrix products: 115 us -> 66.6 us
  waiting for transfers between devices: 290 us -> 335 us
  starting transfers between devices: 183 us -> 146 us
    pallas_call x4 -> x40, Pallas kernels: 48.2 us -> 177 us  [the longest x12 72.3 us: half_call(): pl.pallas_call(kernel, grid=(2,), in_specs=specs + [pl.BlockSpec(memory_s...]
    ppermute x102 -> x96, waiting for transfers between devices: 238 us -> 280 us  [the longest x68 228 us: exchange(): return lax.ppermute(value, SEQ, [(i, i ^ mask) for i in range(seq)])]
    ppermute x102 -> x96, starting transfers between devices: 139 us -> 103 us  [the longest x68 47.6 us: exchange(): return lax.ppermute(value, SEQ, [(i, i ^ mask) for i in range(seq)])]
    slice x42 -> x6, local copies, waits for them, and re-layouts: 36.8 us -> 6.7 us  [the longest x2 2.91 us: deal_joint(): joint[:, r * cols:(r + 1) * cols]]
    all_gather x3 -> x2, waiting for transfers between devices: 0.01 us -> 28.8 us  [gather_slow(): return [lax.all_gather(pack, OWNERS, axis=0, tiled=False)]]
    dot_general x14, matrix products: 39.5 us -> 11.2 us  [dot(): return jnp.dot(left, right, preferred_element_type=F32)]
    dynamic_update_slice x40 -> x0, local copies, waits for them, and re-layouts: 26.6 us -> none  [the longest x24 20 us: spread(): whole = lax.dynamic_update_index_in_dim(whole, got[mask], member ^ mask, 0)]
    all_to_all x10, waiting for transfers between devices: 51.1 us -> 26.6 us  [the longest x2 10.2 us: return_forward(): got = lax.all_to_all(chunks, SEQ, 0, 0, tiled=True)]
  transfers between devices with their start and end apart: 119 -> 110, of which waited for: 46 -> 46; matrix products, arithmetic and copies ran while one was open for 42% -> 18% of each run, Pallas kernels for 3% -> 19%
where the time goes in v2:
time: 900 us; the launch traced here: 888 us
  waiting for transfers between devices  335 us (37%)
  Pallas kernels  177 us (20%)
  starting transfers between devices  146 us (16%)
  other arithmetic  75.6 us (8%)
  local copies, waits for them, and re-layouts  70.1 us (8%)
  matrix products  66.6 us (7%)
  between operations  17.8 us (2%)
    ppermute x68, waiting for transfers between devices, exchange(): return lax.ppermute(value, SEQ, [(i, i ^ mask) for i in range(seq)])  228 us
    pallas_call x12, Pallas kernels, half_call(): pl.pallas_call(kernel, grid=(2,), in_specs=specs + [pl.BlockSpec(memory_s...  72.3 us
    ppermute x15, waiting for transfers between devices, from_plane(): lax.ppermute(value, 'dp', [(d, (d + back) % planes) for d in range(planes)])  51.5 us
    pallas_call x24, Pallas kernels, rearrange(): pl.pallas_call(body, in_specs=[pl.BlockSpec(memory_space=pltpu.SMEM)] + [...  50.8 us
    ppermute x68, starting transfers between devices, exchange(): return lax.ppermute(value, SEQ, [(i, i ^ mask) for i in range(seq)])  47.6 us
    unnamed x511, local copies, waits for them, and re-layouts  44.1 us
    pallas_call x2, Pallas kernels, attend_back(): pl.pallas_call(attend_back_kernel, grid_spec=pltpu.PrefetchScalarGridSpec...  31.9 us
    dot_general x8, matrix products, through_rows(): lax.dot_general(left, right, (((0,), (0,)), ((), ())), preferred_element_...  30.7 us
  transfers between devices with their start and end apart: 110, of which 46 were waited for; matrix products, arithmetic and copies ran while one was open for 18% of the time, Pallas kernels for 19%

profile of v2, /device:TPU:0, one launch (start us, length us, event | category | flops | bytes accessed | tf_op | source)
XLA Modules:
  0.0 888.4 jit_solution(18442426519119640249)
XLA Ops:
  41.4 5.5 all-to-all-done
  52.4 22.1 %collective-permute-done.7.refs_2_ = bf16[144,1152]{1,0:T(8,128)(2,1)S(1)} collective-permute-done((bf16[144,1152]{1,0:T(8,128)(2,1)S(1)}, bf16[144,1152]{1,0:T(8,128)(2,1)S(1)}, u32[]{:S(2)}, u32[]{:S(2)}) %collective-permute-start.7) | collective-permute-done | bytes 331808 | tf_op jit(solution)/shard_map/ppermute | solution.py:81
  88.4 5.2 collective-permute-done.14.refs_7_
  95.6 5.9 collective-permute-done.13.refs_6_
  140.4 6.9 all-to-all-done.2.got_ref
  164.6 4.7 collective-permute-done.16.refs_6_.refs_7_
  171.3 11.0 %attend.2 = (bf16[1024,384]{1,0:T(8,128)(2,1)S(1)}, f32[1024,128]{1,0:T(8,128)S(1)}) custom-call(s32[3]{0:T(128)S(1)} %pad_add_fusion.2.me_ref, bf16[1024,1152]{1,0:T(8,128)(2,1)S(1)} %joint_far.2.q_ref.refs_0_.refs_1_.refs_2_.refs_3_.refs_4_.refs_5_, bf16[1024,1152]{1,0:T(8,128)(2,1)S(1)} %joint_far.2.q_ref.refs_0_.refs_1_.refs_2_.refs_3_.refs_4_.refs_5_, ...), custom_call_target="tpu_custom_call" | custom-call | flops 2684354560 | bytes 3145728 | tf_op jit(solution)/shard_map/attend/pallas_call | solution.py:840
  190.6 15.8 %collective-permute-done.25.refs_2_ = bf16[288,1152]{1,0:T(8,128)(2,1)} collective-permute-done((bf16[288,1152]{1,0:T(8,128)(2,1)}, bf16[288,1152]{1,0:T(8,128)(2,1)}, u32[]{:S(2)}, u32[]{:S(2)}) %collective-permute-start.25) | collective-permute-done | bytes 663584 | tf_op jit(solution)/shard_map/ppermute | solution.py:81
  214.3 5.7 collective-permute-done.30.refs_3_
  226.1 14.4 %collective-permute-done.26.refs_6_ = bf16[288,1152]{1,0:T(8,128)(2,1)} collective-permute-done((bf16[288,1152]{1,0:T(8,128)(2,1)}, bf16[288,1152]{1,0:T(8,128)(2,1)}, u32[]{:S(2)}, u32[]{:S(2)}) %collective-permute-start.26) | collective-permute-done | bytes 663584 | tf_op jit(solution)/shard_map/ppermute | solution.py:69
  249.7 4.9 collective-permute-done.31.refs_7_
  254.6 5.6 open_forward.2
  260.3 8.8 forward_near.2
  271.1 8.8 forward_far.2
  287.1 5.7 all-gather.5.cloned.1.call-done
  309.2 11.7 %collective-permute-done.36.a_ref = bf16[256,1152]{1,0:T(8,128)(2,1)S(1)} collective-permute-done((bf16[256,1152]{1,0:T(8,128)(2,1)S(1)}, bf16[256,1152]{1,0:T(8,128)(2,1)S(1)}, u32[]{:S(2)}, u32[]{:S(2)}) %collective-permute-start.36) | collective-permute-done | bytes 589856 | tf_op jit(solution)/shard_map/ppermute | solution.py:69
  330.8 6.5 collective-permute-done.39.refs_6_.refs_7_
  338.4 11.5 %attend.3 = (bf16[1024,384]{1,0:T(8,128)(2,1)S(1)}, f32[1024,128]{1,0:T(8,128)S(1)}) custom-call(s32[3]{0:T(128)S(1)} %pad_add_fusion.2.me_ref, bf16[1024,1152]{1,0:T(8,128)(2,1)S(1)} %joint_far.3.q_ref.refs_0_.refs_1_.refs_2_.refs_3_.refs_4_.refs_5_, bf16[1024,1152]{1,0:T(8,128)(2,1)S(1)} %joint_far.3.q_ref.refs_0_.refs_1_.refs_2_.refs_3_.refs_4_.refs_5_, ...), custom_call_target="tpu_custom_call" | custom-call | flops 2684354560 | bytes 3145728 | tf_op jit(solution)/shard_map/attend/pallas_call | solution.py:840
  358.0 13.7 %collective-permute-done.41 = bf16[256,1152]{1,0:T(8,128)(2,1)S(1)} collective-permute-done((bf16[256,1152]{1,0:T(8,128)(2,1)S(1)}, bf16[256,1152]{1,0:T(8,128)(2,1)S(1)}, u32[]{:S(2)}, u32[]{:S(2)}) %collective-permute-start.41) | collective-permute-done | bytes 589856 | tf_op jit(solution)/shard_map/ppermute | solution.py:69
  378.8 23.1 %all-gather.7.cloned.1.call-done = bf16[2304,1152]{1,0:T(8,128)(2,1)} async-done(((bf16[288,1152]{1,0:T(8,128)(2,1)}), bf16[2304,1152]{1,0:T(8,128)(2,1)}) %all-gather.7.cloned.1.call-update) | async-done | bytes 5308432 | tf_op jit(solution)/shard_map/all_gather | solution.py:507
  408.4 8.6 forward_near.3
  419.1 8.6 forward_far.3
  427.9 6.8 backward_near.2
  440.3 6.8 backward_far.2
  448.6 5.7 collective-permute-done.47
  460.6 9.7 %collective-permute-done.53 = bf16[256,1152]{1,0:T(8,128)(2,1)S(1)} collective-permute-done((bf16[256,1152]{1,0:T(8,128)(2,1)S(1)}, bf16[256,1152]{1,0:T(8,128)(2,1)S(1)}, u32[]{:S(2)}, u32[]{:S(2)}) %collective-permute-start.53) | collective-permute-done | bytes 589856 | tf_op jit(solution)/shard_map/ppermute | solution.py:69
  484.7 12.2 %collective-permute-done.56 = bf16[256,1152]{1,0:T(8,128)(2,1)S(1)} collective-permute-done((bf16[256,1152]{1,0:T(8,128)(2,1)S(1)}, bf16[256,1152]{1,0:T(8,128)(2,1)S(1)}, u32[]{:S(2)}, u32[]{:S(2)}) %collective-permute-start.56) | collective-permute-done | bytes 589856 | tf_op jit(solution)/shard_map/ppermute | solution.py:69
  500.4 16.2 %attend_back.2 = (bf16[1024,1152]{1,0:T(8,128)(2,1)}, bf16[256,768]{1,0:T(8,128)(2,1)S(1)}, bf16[128,768]{1,0:T(8,128)(2,1)S(1)}) custom-call(s32[3]{0:T(128)S(1)} %pad_add_fusion.2.me_ref, bf16[1024,1152]{1,0:T(8,128)(2,1)} %copy-done.1, bf16[1024,1152]{1,0:T(8,128)(2,1)} %copy-done.1, bf16[1024,1152]{1,0:T(8,128)(2,1)} %copy-done.1, ...), custom_call_target="tpu_custom_call" | custom-call | flops 6710886400 | bytes 7864320 | tf_op jit(solution)/shard_map/attend_back/pallas_call | solution.py:872
  517.5 16.1 %collective-permute-done.58 = bf16[256,768]{1,0:T(8,128)(2,1)S(1)} collective-permute-done((bf16[256,768]{1,0:T(8,128)(2,1)S(1)}, bf16[256,768]{1,0:T(8,128)(2,1)S(1)}, u32[]{:S(2)}, u32[]{:S(2)}) %collective-permute-start.58) | collective-permute-done | bytes 393248 | tf_op jit(solution)/shard_map/ppermute | solution.py:69
  554.6 4.8 convolution_convert_fusion.3.joint_ref
  566.3 6.6 collective-permute-done.60
  581.8 7.0 backward_near.3
  589.7 5.9 collective-permute-done.62.a_ref
  597.6 7.6 backward_far.3
  614.0 4.9 convolution_convert_fusion.2.reduce_ref
  619.0 9.8 %collective-permute-done.66 = bf16[256,1152]{1,0:T(8,128)(2,1)S(1)} collective-permute-done((bf16[256,1152]{1,0:T(8,128)(2,1)S(1)}, bf16[256,1152]{1,0:T(8,128)(2,1)S(1)}, u32[]{:S(2)}, u32[]{:S(2)}) %collective-permute-start.66) | collective-permute-done | bytes 589856 | tf_op jit(solution)/shard_map/ppermute | solution.py:69
  634.8 4.8 convolution_convert_fusion.1.expand_ref
  650.5 18.9 %collective-permute-done.71 = bf16[288,1152]{1,0:T(8,128)(2,1)S(1)} collective-permute-done((bf16[288,1152]{1,0:T(8,128)(2,1)S(1)}, bf16[288,1152]{1,0:T(8,128)(2,1)S(1)}, u32[]{:S(2)}, u32[]{:S(2)}) %collective-permute-start.71) | collective-permute-done | bytes 663584 | tf_op jit(solution)/shard_map/ppermute | solution.py:69
  676.1 15.7 %attend_back.3 = (bf16[1024,1152]{1,0:T(8,128)(2,1)}, bf16[256,768]{1,0:T(8,128)(2,1)S(1)}, bf16[128,768]{1,0:T(8,128)(2,1)S(1)}) custom-call(s32[3]{0:T(128)S(1)} %pad_add_fusion.2.me_ref, bf16[1024,1152]{1,0:T(8,128)(2,1)} %copy-done, bf16[1024,1152]{1,0:T(8,128)(2,1)} %copy-done, bf16[1024,1152]{1,0:T(8,128)(2,1)} %copy-done, bf16[1024,1152]{1,0:T(8,128)(2,1)} %copy-done, ...), custom_call_target="tpu_custom_call" | custom-call | flops 6710886400 | bytes 7864320 | tf_op jit(solution)/shard_map/attend_back/pallas_call | solution.py:872
  706.3 17.9 %collective-permute-done.72 = bf16[256,768]{1,0:T(8,128)(2,1)S(1)} collective-permute-done((bf16[256,768]{1,0:T(8,128)(2,1)S(1)}, bf16[256,768]{1,0:T(8,128)(2,1)S(1)}, u32[]{:S(2)}, u32[]{:S(2)}) %collective-permute-start.72) | collective-permute-done | bytes 393248 | tf_op jit(solution)/shard_map/ppermute | solution.py:69
  732.4 7.2 convolution_convert_fusion.joint_ref
  774.1 5.8 collective-permute-done.83
  781.5 4.6 collective-permute-done.93
  788.7 11.5 %collective-permute-done.80 = bf16[144,1152]{1,0:T(8,128)(2,1)S(1)} collective-permute-done((bf16[144,1152]{1,0:T(8,128)(2,1)S(1)}, bf16[144,1152]{1,0:T(8,128)(2,1)S(1)}, u32[]{:S(2)}, u32[]{:S(2)}) %collective-permute-start.80) | collective-permute-done | bytes 331808 | tf_op jit(solution)/shard_map/ppermute | solution.py:69
  806.4 10.1 %collective-permute-done.76 = bf16[256,1152]{1,0:T(8,128)(2,1)S(1)} collective-permute-done((bf16[256,1152]{1,0:T(8,128)(2,1)S(1)}, bf16[256,1152]{1,0:T(8,128)(2,1)S(1)}, u32[]{:S(2)}, u32[]{:S(2)}) %collective-permute-start.76) | collective-permute-done | bytes 589856 | tf_op jit(solution)/shard_map/ppermute | solution.py:69
  827.4 6.4 all-to-all-start.8
  837.6 4.7 collective-permute-start.91
  865.0 10.2 %all-to-all-done.9.got_ref = bf16[8,144,432]{2,1,0:T(8,128)(2,1)S(1)} async-done(((bf16[8,144,432]{2,1,0:T(8,128)(2,1)}), bf16[8,144,432]{2,1,0:T(8,128)(2,1)S(1)}, u32[]{:S(2)}, u32[]{:S(2)}) %all-to-all-start.9) | async-done | bytes 995360 | tf_op jit(solution)/shard_map/all_to_all | solution.py:592
  (942 shorter events, 418.2 us)
Async XLA Ops:
  38.3 36.2 %collective-permute-start.7 = (bf16[144,1152]{1,0:T(8,128)(2,1)S(1)}, bf16[144,1152]{1,0:T(8,128)(2,1)S(1)}, u32[]{:S(2)}, u32[]{:S(2)}) collective-permute-start(bf16[144,1152]{1,0:T(8,128)(2,1)S(1)} %pack_attention.2.refs_0_), channel_id=1, source_target_pairs={{0,16},{8,24},{16,0},{24,8},{1,17},{9,25},{17,1},{25,9},{2,18},{10... | collective-permute-start | bytes 995336 | tf_op jit(solution)/shard_map/ppermute | solution.py:81
  38.3 36.2 %collective-permute-start.6 = (bf16[144,1152]{1,0:T(8,128)(2,1)S(1)}, bf16[144,1152]{1,0:T(8,128)(2,1)S(1)}, u32[]{:S(2)}, u32[]{:S(2)}) collective-permute-start(bf16[144,1152]{1,0:T(8,128)(2,1)S(1)} %pack_attention.2.refs_0_), channel_id=1, source_target_pairs={{0,8},{8,16},{16,24},{24,0},{1,9},{9,17},{17,25},{25,1},{2,10},{10... | collective-permute-start | bytes 995336 | tf_op jit(solution)/shard_map/ppermute | solution.py:81
  46.9 32.3 %all-to-all-start.1 = ((bf16[8,144,432]{2,1,0:T(8,128)(2,1)}), bf16[8,144,432]{2,1,0:T(8,128)(2,1)S(1)}, u32[]{:S(2)}, u32[]{:S(2)}) async-start(bf16[8,144,432]{2,1,0:T(8,128)(2,1)} %pack_forward.2), calls=%async_computation.1 | async-start | bytes 2359296 | tf_op jit(solution)/shard_map/all_to_all | solution.py:498
  50.5 34.3 %collective-permute-start.11 = (bf16[144,1152]{1,0:T(8,128)(2,1)S(1)}, bf16[144,1152]{1,0:T(8,128)(2,1)}, u32[]{:S(2)}, u32[]{:S(2)}) collective-permute-start(bf16[144,1152]{1,0:T(8,128)(2,1)S(1)} %pack_attention.2.refs_0_), channel_id=1, source_target_pairs={{0,4},{1,5},{2,6},{3,7},{4,0},{5,1},{6,2},{7,3},{8,12},{9,13},{10,... | collective-permute-start | bytes 995336 | tf_op jit(solution)/shard_map/ppermute | solution.py:69
  81.0 33.8 %collective-permute-start.10 = (bf16[256,1152]{1,0:T(8,128)(2,1)S(1)}, bf16[256,1152]{1,0:T(8,128)(2,1)S(1)}, u32[]{:S(2)}, u32[]{:S(2)}) collective-permute-start(bf16[256,1152]{1,0:T(8,128)(2,1)S(1)} %fusion.27.a_ref), channel_id=1, source_target_pairs={{0,1},{1,0},{2,3},{3,2},{4,5},{5,4},{6,7},{7,6},{8,9},{9,8},{10,11... | collective-permute-start | bytes 1769480 | tf_op jit(solution)/shard_map/ppermute | solution.py:69
  81.0 37.9 %collective-permute-start.9 = (bf16[256,1152]{1,0:T(8,128)(2,1)S(1)}, bf16[256,1152]{1,0:T(8,128)(2,1)}, u32[]{:S(2)}, u32[]{:S(2)}) collective-permute-start(bf16[256,1152]{1,0:T(8,128)(2,1)S(1)} %fusion.27.a_ref), channel_id=1, source_target_pairs={{0,2},{1,3},{2,0},{3,1},{4,6},{5,7},{6,4},{7,5},{8,10},{9,11},{10,... | collective-permute-start | bytes 1769480 | tf_op jit(solution)/shard_map/ppermute | solution.py:69
  84.8 23.0 %collective-permute-start.12 = (bf16[144,1152]{1,0:T(8,128)(2,1)}, bf16[144,1152]{1,0:T(8,128)(2,1)S(1)}, u32[]{:S(2)}, u32[]{:S(2)}) collective-permute-start(bf16[144,1152]{1,0:T(8,128)(2,1)} %copy-done.82), channel_id=1, source_target_pairs={{0,4},{1,5},{2,6},{3,7},{4,0},{5,1},{6,2},{7,3},{8,12},{9,13},{10,... | collective-permute-start | bytes 995336 | tf_op jit(solution)/shard_map/ppermute | solution.py:69
  93.6 28.9 %collective-permute-start.19 = (bf16[288,144]{1,0:T(8,128)(2,1)}, bf16[288,144]{1,0:T(8,128)(2,1)}, u32[]{:S(2)}, u32[]{:S(2)}) collective-permute-start(bf16[288,144]{1,0:T(8,128)(2,1)} %get-tuple-element.414), channel_id=1, source_target_pairs={{0,1},{1,6},{2,0},{3,5},{4,3},{5,4},{6,2},{7,7},{8,9},{9,14},{10,8... | collective-permute-start | bytes 248840 | tf_op jit(solution)/shard_map/ppermute | solution.py:136
  101.4 21.1 %collective-permute-start.18 = (bf16[288,144]{1,0:T(8,128)(2,1)}, bf16[288,144]{1,0:T(8,128)(2,1)}, u32[]{:S(2)}, u32[]{:S(2)}) collective-permute-start(bf16[288,144]{1,0:T(8,128)(2,1)} %get-tuple-element.415), channel_id=1, source_target_pairs={{0,4},{1,2},{2,7},{3,1},{4,6},{5,0},{6,5},{7,3},{8,12},{9,10},{10,... | collective-permute-start | bytes 248840 | tf_op jit(solution)/shard_map/ppermute | solution.py:136
  126.7 20.6 %all-to-all-start.2 = ((bf16[8,144,432]{2,1,0:T(8,128)(2,1)}), bf16[8,144,432]{2,1,0:T(8,128)(2,1)S(1)}, u32[]{:S(2)}, u32[]{:S(2)}) async-start(bf16[8,144,432]{2,1,0:T(8,128)(2,1)} %copy-done.11), calls=%async_computation.2 | async-start | bytes 2359296 | tf_op jit(solution)/shard_map/all_to_all | solution.py:498
  131.8 51.4 %collective-permute-start.20 = (bf16[288,1152]{1,0:T(8,128)(2,1)}, bf16[288,1152]{1,0:T(8,128)(2,1)}, u32[]{:S(2)}, u32[]{:S(2)}) collective-permute-start(bf16[288,1152]{1,0:T(8,128)(2,1)} %copy-done.22), channel_id=1, source_target_pairs={{0,4},{1,5},{2,6},{3,7},{4,0},{5,1},{6,2},{7,3},{8,12},{9,13},{10,... | collective-permute-start | bytes 1990664 | tf_op jit(solution)/shard_map/ppermute | solution.py:69
  139.8 29.5 %collective-permute-start.16 = (bf16[256,768]{1,0:T(8,128)(2,1)}, bf16[256,768]{1,0:T(8,128)(2,1)}, u32[]{:S(2)}, u32[]{:S(2)}) collective-permute-start(bf16[256,768]{1,0:T(8,128)(2,1)} %constant_dynamic-slice_fusion.1), channel_id=1, source_target_pairs={{0,4},{1,5},{2,6},{3,7},{4,0},{5,1},{6,2},{7,3},{8,12},{9,13},{10,... | collective-permute-start | bytes 1179656 | tf_op jit(solution)/shard_map/ppermute | solution.py:69
  147.4 35.9 %all-to-all-start.3 = ((bf16[4,288,288]{2,1,0:T(8,128)(2,1)}), bf16[4,288,288]{2,1,0:T(8,128)(2,1)}, u32[]{:S(2)}, u32[]{:S(2)}) async-start(bf16[4,288,288]{2,1,0:T(8,128)(2,1)} %copy-done.49), calls=%async_computation.3 | async-start | bytes 1769472 | tf_op jit(solution)/shard_map/all_to_all | solution.py:523
  151.6 141.2 %all-gather.5.cloned.1.call-start = ((), (), s32[]{:S(2)}) async-start(), calls=%async_computation.14 | async-start | bytes 2985984 | tf_op jit(solution)/shard_map/all_gather | solution.py:507
  158.9 47.4 %collective-permute-start.25 = (bf16[288,1152]{1,0:T(8,128)(2,1)}, bf16[288,1152]{1,0:T(8,128)(2,1)}, u32[]{:S(2)}, u32[]{:S(2)}) collective-permute-start(bf16[288,1152]{1,0:T(8,128)(2,1)} %copy-done.22), channel_id=1, source_target_pairs={{0,16},{8,24},{16,0},{24,8},{1,17},{9,25},{17,1},{25,9},{2,18},{10... | collective-permute-start | bytes 1990664 | tf_op jit(solution)/shard_map/ppermute | solution.py:81
  161.4 44.9 %collective-permute-start.23 = (bf16[288,1152]{1,0:T(8,128)(2,1)}, bf16[288,1152]{1,0:T(8,128)(2,1)}, u32[]{:S(2)}, u32[]{:S(2)}) collective-permute-start(bf16[288,1152]{1,0:T(8,128)(2,1)} %copy-done.22), channel_id=1, source_target_pairs={{0,8},{8,16},{16,24},{24,0},{1,9},{9,17},{17,25},{25,1},{2,10},{10... | collective-permute-start | bytes 1990664 | tf_op jit(solution)/shard_map/ppermute | solution.py:81
  186.3 22.0 %collective-permute-start.21 = (bf16[256,1152]{1,0:T(8,128)(2,1)}, bf16[256,1152]{1,0:T(8,128)(2,1)}, u32[]{:S(2)}, u32[]{:S(2)}) collective-permute-start(bf16[256,1152]{1,0:T(8,128)(2,1)} %convolution_convert_fusion.22), channel_id=1, source_target_pairs={{0,1},{1,0},{2,3},{3,2},{4,5},{5,4},{6,7},{7,6},{8,9},{9,8},{10,11... | collective-permute-start | bytes 1769480 | tf_op jit(solution)/shard_map/ppermute | solution.py:69
  186.9 33.1 %collective-permute-start.30 = (bf16[288,1152]{1,0:T(8,128)(2,1)S(1)}, bf16[288,1152]{1,0:T(8,128)(2,1)}, u32[]{:S(2)}, u32[]{:S(2)}) collective-permute-start(bf16[288,1152]{1,0:T(8,128)(2,1)S(1)} %copy-done.23), channel_id=1, source_target_pairs={{0,24},{8,0},{16,8},{24,16},{1,25},{9,1},{17,9},{25,17},{2,26},{10... | collective-permute-start | bytes 1990664 | tf_op jit(solution)/shard_map/ppermute | solution.py:81
  207.0 33.6 %collective-permute-start.26 = (bf16[288,1152]{1,0:T(8,128)(2,1)}, bf16[288,1152]{1,0:T(8,128)(2,1)}, u32[]{:S(2)}, u32[]{:S(2)}) collective-permute-start(bf16[288,1152]{1,0:T(8,128)(2,1)} %collective-permute-done.25.refs_2_), channel_id=1, source_target_pairs={{0,4},{1,5},{2,6},{3,7},{4,0},{5,1},{6,2},{7,3},{8,12},{9,13},{10,... | collective-permute-start | bytes 1990664 | tf_op jit(solution)/shard_map/ppermute | solution.py:69
  214.0 26.6 %collective-permute-start.27 = (bf16[256,1152]{1,0:T(8,128)(2,1)}, bf16[256,1152]{1,0:T(8,128)(2,1)}, u32[]{:S(2)}, u32[]{:S(2)}) collective-permute-start(bf16[256,1152]{1,0:T(8,128)(2,1)} %convolution_convert_fusion.20), channel_id=1, source_target_pairs={{0,1},{1,0},{2,3},{3,2},{4,5},{5,4},{6,7},{7,6},{8,9},{9,8},{10,11... | collective-permute-start | bytes 1769480 | tf_op jit(solution)/shard_map/ppermute | solution.py:69
  214.0 187.9 %all-gather.7.cloned.1.call-start = ((), (), s32[]{:S(2)}) async-start(), calls=%async_computation.15 | async-start | bytes 5971968 | tf_op jit(solution)/shard_map/all_gather | solution.py:507
  220.0 34.6 %collective-permute-start.31 = (bf16[288,1152]{1,0:T(8,128)(2,1)}, bf16[288,1152]{1,0:T(8,128)(2,1)}, u32[]{:S(2)}, u32[]{:S(2)}) collective-permute-start(bf16[288,1152]{1,0:T(8,128)(2,1)} %collective-permute-done.30.refs_3_), channel_id=1, source_target_pairs={{0,4},{1,5},{2,6},{3,7},{4,0},{5,1},{6,2},{7,3},{8,12},{9,13},{10,... | collective-permute-start | bytes 1990664 | tf_op jit(solution)/shard_map/ppermute | solution.py:69
  245.9 23.1 %collective-permute-start.28 = (bf16[256,1152]{1,0:T(8,128)(2,1)S(1)}, bf16[256,1152]{1,0:T(8,128)(2,1)S(1)}, u32[]{:S(2)}, u32[]{:S(2)}) collective-permute-start(bf16[256,1152]{1,0:T(8,128)(2,1)S(1)} %add_convert_fusion.7.a_ref), channel_id=1, source_target_pairs={{0,2},{1,3},{2,0},{3,1},{4,6},{5,7},{6,4},{7,5},{8,10},{9,11},{10,... | collective-permute-start | bytes 1769480 | tf_op jit(solution)/shard_map/ppermute | solution.py:69
  326.1 25.4 %all-to-all-start.4 = ((bf16[4,288,288]{2,1,0:T(8,128)(2,1)}), bf16[4,288,288]{2,1,0:T(8,128)(2,1)}, u32[]{:S(2)}, u32[]{:S(2)}) async-start(bf16[4,288,288]{2,1,0:T(8,128)(2,1)} %copy-done.50), calls=%async_computation.4 | async-start | bytes 1769472 | tf_op jit(solution)/shard_map/all_to_all | solution.py:523
  330.3 362.6 %reduce-scatter.3.cloned.1.call-start = ((), (), s32[]{:S(2)}) async-start(), calls=%async_computation.12 | async-start | bytes 5971968 | tf_op jit(solution)/shard_map/reduce_scatter | solution.py:572
  376.9 31.5 %collective-permute-start.44 = (bf16[256,1152]{1,0:T(8,128)(2,1)S(1)}, bf16[256,1152]{1,0:T(8,128)(2,1)}, u32[]{:S(2)}, u32[]{:S(2)}) collective-permute-start(bf16[256,1152]{1,0:T(8,128)(2,1)S(1)} %get-tuple-element.447.a_ref), channel_id=1, source_target_pairs={{0,1},{1,0},{2,3},{3,2},{4,5},{5,4},{6,7},{7,6},{8,9},{9,8},{10,11... | collective-permute-start | bytes 1769480 | tf_op jit(solution)/shard_map/ppermute | solution.py:69
  377.0 40.1 %collective-permute-start.43 = (bf16[256,1152]{1,0:T(8,128)(2,1)S(1)}, bf16[256,1152]{1,0:T(8,128)(2,1)S(1)}, u32[]{:S(2)}, u32[]{:S(2)}) collective-permute-start(bf16[256,1152]{1,0:T(8,128)(2,1)S(1)} %get-tuple-element.447.a_ref), channel_id=1, source_target_pairs={{0,2},{1,3},{2,0},{3,1},{4,6},{5,7},{6,4},{7,5},{8,10},{9,11},{10,... | collective-permute-start | bytes 1769480 | tf_op jit(solution)/shard_map/ppermute | solution.py:69
  436.2 34.1 %collective-permute-start.48 = (bf16[256,1152]{1,0:T(8,128)(2,1)S(1)}, bf16[256,1152]{1,0:T(8,128)(2,1)}, u32[]{:S(2)}, u32[]{:S(2)}) collective-permute-start(bf16[256,1152]{1,0:T(8,128)(2,1)S(1)} %get-tuple-element.189), channel_id=1, source_target_pairs={{0,1},{1,0},{2,3},{3,2},{4,5},{5,4},{6,7},{7,6},{8,9},{9,8},{10,11... | collective-permute-start | bytes 1769480 | tf_op jit(solution)/shard_map/ppermute | solution.py:69
  436.4 33.9 %collective-permute-start.54 = (bf16[256,1152]{1,0:T(8,128)(2,1)S(1)}, bf16[256,1152]{1,0:T(8,128)(2,1)}, u32[]{:S(2)}, u32[]{:S(2)}) collective-permute-start(bf16[256,1152]{1,0:T(8,128)(2,1)S(1)} %get-tuple-element.200), channel_id=1, source_target_pairs={{0,1},{1,0},{2,3},{3,2},{4,5},{5,4},{6,7},{7,6},{8,9},{9,8},{10,11... | collective-permute-start | bytes 1769480 | tf_op jit(solution)/shard_map/ppermute | solution.py:69
  547.5 208.0 %reduce-scatter.5.cloned.1.call-start = ((), (), s32[]{:S(2)}) async-start(), calls=%async_computation.13 | async-start | bytes 2985984 | tf_op jit(solution)/shard_map/reduce_scatter | solution.py:572
  550.9 22.0 %collective-permute-start.60 = (bf16[256,1152]{1,0:T(8,128)(2,1)}, bf16[256,1152]{1,0:T(8,128)(2,1)}, u32[]{:S(2)}, u32[]{:S(2)}) collective-permute-start(bf16[256,1152]{1,0:T(8,128)(2,1)} %convert_add_fusion.2), channel_id=1, source_target_pairs={{0,2},{1,3},{2,0},{3,1},{4,6},{5,7},{6,4},{7,5},{8,10},{9,11},{10,... | collective-permute-start | bytes 1769480 | tf_op jit(solution)/shard_map/ppermute | solution.py:69
  644.9 24.5 %collective-permute-start.71 = (bf16[288,1152]{1,0:T(8,128)(2,1)S(1)}, bf16[288,1152]{1,0:T(8,128)(2,1)S(1)}, u32[]{:S(2)}, u32[]{:S(2)}) collective-permute-start(bf16[288,1152]{1,0:T(8,128)(2,1)S(1)} %get-tuple-element.229), channel_id=1, source_target_pairs={{0,4},{1,5},{2,6},{3,7},{4,0},{5,1},{6,2},{7,3},{8,12},{9,13},{10,... | collective-permute-start | bytes 1990664 | tf_op jit(solution)/shard_map/ppermute | solution.py:69
  645.7 28.8 %collective-permute-start.68 = (bf16[256,1152]{1,0:T(8,128)(2,1)S(1)}, bf16[256,1152]{1,0:T(8,128)(2,1)S(1)}, u32[]{:S(2)}, u32[]{:S(2)}) collective-permute-start(bf16[256,1152]{1,0:T(8,128)(2,1)S(1)} %get-tuple-element.386), channel_id=1, source_target_pairs={{0,1},{1,0},{2,3},{3,2},{4,5},{5,4},{6,7},{7,6},{8,9},{9,8},{10,11... | collective-permute-start | bytes 1769480 | tf_op jit(solution)/shard_map/ppermute | solution.py:69
  647.9 26.6 %collective-permute-start.70 = (bf16[256,1152]{1,0:T(8,128)(2,1)S(1)}, bf16[256,1152]{1,0:T(8,128)(2,1)S(1)}, u32[]{:S(2)}, u32[]{:S(2)}) collective-permute-start(bf16[256,1152]{1,0:T(8,128)(2,1)S(1)} %collective-permute-done.69), channel_id=1, source_target_pairs={{0,1},{1,0},{2,3},{3,2},{4,5},{5,4},{6,7},{7,6},{8,9},{9,8},{10,11... | collective-permute-start | bytes 1769480 | tf_op jit(solution)/shard_map/ppermute | solution.py:69
  649.7 54.2 %collective-permute-start.73 = (bf16[288,1152]{1,0:T(8,128)(2,1)}, bf16[288,1152]{1,0:T(8,128)(2,1)}, u32[]{:S(2)}, u32[]{:S(2)}) collective-permute-start(bf16[288,1152]{1,0:T(8,128)(2,1)} %get-tuple-element.230), channel_id=1, source_target_pairs={{0,4},{1,5},{2,6},{3,7},{4,0},{5,1},{6,2},{7,3},{8,12},{9,13},{10,... | collective-permute-start | bytes 1990664 | tf_op jit(solution)/shard_map/ppermute | solution.py:69
  670.5 33.4 %collective-permute-start.74 = (bf16[288,1152]{1,0:T(8,128)(2,1)}, bf16[288,1152]{1,0:T(8,128)(2,1)}, u32[]{:S(2)}, u32[]{:S(2)}) collective-permute-start(bf16[288,1152]{1,0:T(8,128)(2,1)} %add_convert_fusion.3), channel_id=1, source_target_pairs={{0,8},{8,16},{16,24},{24,0},{1,9},{9,17},{17,25},{25,1},{2,10},{10... | collective-permute-start | bytes 1990664 | tf_op jit(solution)/shard_map/ppermute | solution.py:81
  696.1 30.1 %all-to-all-start.6 = ((bf16[8,144,432]{2,1,0:T(8,128)(2,1)}), bf16[8,144,432]{2,1,0:T(8,128)(2,1)S(1)}, u32[]{:S(2)}, u32[]{:S(2)}) async-start(bf16[8,144,432]{2,1,0:T(8,128)(2,1)} %pack_return.2), calls=%async_computation.7 | async-start | bytes 2359296 | tf_op jit(solution)/shard_map/all_to_all | solution.py:592
  701.9 22.3 %collective-permute-start.72 = (bf16[256,768]{1,0:T(8,128)(2,1)S(1)}, bf16[256,768]{1,0:T(8,128)(2,1)S(1)}, u32[]{:S(2)}, u32[]{:S(2)}) collective-permute-start(bf16[256,768]{1,0:T(8,128)(2,1)S(1)} %pad_select_fusion), channel_id=1, source_target_pairs={{0,4},{1,5},{2,6},{3,7},{4,0},{5,1},{6,2},{7,3},{8,12},{9,13},{10,... | collective-permute-start | bytes 1179656 | tf_op jit(solution)/shard_map/ppermute | solution.py:69
  753.5 27.9 %collective-permute-start.94 = (bf16[288,1152]{1,0:T(8,128)(2,1)}, bf16[288,1152]{1,0:T(8,128)(2,1)}, u32[]{:S(2)}, u32[]{:S(2)}) collective-permute-start(bf16[288,1152]{1,0:T(8,128)(2,1)} %add_convert_fusion.2), channel_id=1, source_target_pairs={{0,8},{8,16},{16,24},{24,0},{1,9},{9,17},{17,25},{25,1},{2,10},{10... | collective-permute-start | bytes 1990664 | tf_op jit(solution)/shard_map/ppermute | solution.py:81
  758.1 93.7 %collective-permute-start.89 = (bf16[288,144]{1,0:T(8,128)(2,1)}, bf16[288,144]{1,0:T(8,128)(2,1)}, u32[]{:S(2)}, u32[]{:S(2)}) collective-permute-start(bf16[288,144]{1,0:T(8,128)(2,1)} %get-tuple-element.258), channel_id=1, source_target_pairs={{0,0},{5,1},{3,2},{4,3},{2,4},{7,5},{1,6},{6,7},{8,8},{13,9},{11,1... | collective-permute-start | bytes 248840 | tf_op jit(solution)/shard_map/ppermute | solution.py:143
  761.7 24.4 %collective-permute-start.93 = (bf16[288,1152]{1,0:T(8,128)(2,1)}, bf16[288,1152]{1,0:T(8,128)(2,1)S(1)}, u32[]{:S(2)}, u32[]{:S(2)}) collective-permute-start(bf16[288,1152]{1,0:T(8,128)(2,1)} %copy-done.85), channel_id=1, source_target_pairs={{0,4},{1,5},{2,6},{3,7},{4,0},{5,1},{6,2},{7,3},{8,12},{9,13},{10,... | collective-permute-start | bytes 1990664 | tf_op jit(solution)/shard_map/ppermute | solution.py:69
  771.9 61.9 %collective-permute-start.79 = (bf16[144,1152]{1,0:T(8,128)(2,1)}, bf16[144,1152]{1,0:T(8,128)(2,1)}, u32[]{:S(2)}, u32[]{:S(2)}) collective-permute-start(bf16[144,1152]{1,0:T(8,128)(2,1)} %get-tuple-element.251), channel_id=1, source_target_pairs={{0,4},{1,5},{2,6},{3,7},{4,0},{5,1},{6,2},{7,3},{8,12},{9,13},{10,... | collective-permute-start | bytes 995336 | tf_op jit(solution)/shard_map/ppermute | solution.py:69
  781.4 22.4 %collective-permute-start.77 = (bf16[256,1152]{1,0:T(8,128)(2,1)S(1)}, bf16[256,1152]{1,0:T(8,128)(2,1)S(1)}, u32[]{:S(2)}, u32[]{:S(2)}) collective-permute-start(bf16[256,1152]{1,0:T(8,128)(2,1)S(1)} %convolution_convert_fusion.8), channel_id=1, source_target_pairs={{0,1},{1,0},{2,3},{3,2},{4,5},{5,4},{6,7},{7,6},{8,9},{9,8},{10,11... | collective-permute-start | bytes 1769480 | tf_op jit(solution)/shard_map/ppermute | solution.py:69
  800.1 44.4 %collective-permute-start.92 = (bf16[288,1152]{1,0:T(8,128)(2,1)}, bf16[288,1152]{1,0:T(8,128)(2,1)}, u32[]{:S(2)}, u32[]{:S(2)}) collective-permute-start(bf16[288,1152]{1,0:T(8,128)(2,1)} %get-tuple-element.263), channel_id=1, source_target_pairs={{0,4},{1,5},{2,6},{3,7},{4,0},{5,1},{6,2},{7,3},{8,12},{9,13},{10,... | collective-permute-start | bytes 1990664 | tf_op jit(solution)/shard_map/ppermute | solution.py:69
  803.8 42.0 %collective-permute-start.95 = (bf16[288,1152]{1,0:T(8,128)(2,1)}, bf16[288,1152]{1,0:T(8,128)(2,1)}, u32[]{:S(2)}, u32[]{:S(2)}) collective-permute-start(bf16[288,1152]{1,0:T(8,128)(2,1)} %add_convert_fusion.1), channel_id=1, source_target_pairs={{0,8},{8,16},{16,24},{24,0},{1,9},{9,17},{17,25},{25,1},{2,10},{10... | collective-permute-start | bytes 1990664 | tf_op jit(solution)/shard_map/ppermute | solution.py:81
  827.4 27.4 %all-to-all-start.8 = ((f32[32,2,864]{2,1,0:T(2,128)}), f32[32,2,864]{2,1,0:T(2,128)S(1)}, u32[]{:S(2)}, u32[]{:S(2)}) async-start(f32[32,2,864]{2,1,0:T(2,128)} %bitcast.69), calls=%async_computation.9 | async-start | bytes 458752 | tf_op jit(solution)/shard_map/all_to_all | solution.py:1287
  833.9 25.6 %collective-permute-start.90 = (bf16[288,144]{1,0:T(8,128)(2,1)S(1)}, bf16[288,144]{1,0:T(8,128)(2,1)}, u32[]{:S(2)}, u32[]{:S(2)}) collective-permute-start(bf16[288,144]{1,0:T(8,128)(2,1)S(1)} %copy-done.95), channel_id=1, source_target_pairs={{4,0},{2,1},{7,2},{1,3},{6,4},{0,5},{5,6},{3,7},{12,8},{10,9},{15,... | collective-permute-start | bytes 248840 | tf_op jit(solution)/shard_map/ppermute | solution.py:143
  837.6 21.9 %collective-permute-start.91 = (bf16[288,144]{1,0:T(8,128)(2,1)S(1)}, bf16[288,144]{1,0:T(8,128)(2,1)}, u32[]{:S(2)}, u32[]{:S(2)}) collective-permute-start(bf16[288,144]{1,0:T(8,128)(2,1)S(1)} %get-tuple-element.260), channel_id=1, source_target_pairs={{1,0},{6,1},{0,2},{5,3},{3,4},{4,5},{2,6},{7,7},{9,8},{14,9},{8,10... | collective-permute-start | bytes 248840 | tf_op jit(solution)/shard_map/ppermute | solution.py:143
  (313 other events, 3025.3 us)
Sparse Core Ops, SparseCore 0:
  214.1 78.6 all-gather.4
  295.0 106.8 all-gather.6
  483.3 114.9 reduce-scatter.2
  610.4 88.0 reduce-scatter.4

commit v3 on v2

--- a/solution.py
+++ b/solution.py
@@ -981,7 +981,7 @@
     (joint,) = half_call(
         joint_body, 0, ours, [w_joint], [], [(3 * WIDTH, None)], False, "joint_near"
     )
-    theirs = far(after(theirs, joint))
+    theirs = far(hold("far_one", theirs, joint))
     (joint,) = half_call(
         joint_body, 1, theirs, [w_joint], [], [(3 * WIDTH, joint)], False, "joint_far"
     )
@@ -1008,7 +1008,7 @@
         forward_body, 0, ours, matrices, tokens, [(LOCAL_FF, None)] * 2, True, "forward_near"
     )
     close = pair_sum(parts)
-    theirs = far(after(theirs, activated))
+    theirs = far(hold("far_two", theirs, activated))
     activated, slope, *parts = half_call(
         forward_body,
         1,
@@ -1061,7 +1061,7 @@
         per_token(mod[:, i], sides) for i in range(6)
     ]
     count = stream.shape[0]
-    fast = last and compact()
+    fast = compact()
     mine = (adjoint * gate_two * keeping).astype(BF16)
     theirs, ours = exchange(mine, 2), near(mine)
     matrices = [w_expand, w_reduce]
@@ -1069,7 +1069,7 @@
         backward_body, 0, ours, matrices, [slope], [(LOCAL_FF, None)], True, "backward_near"
     )
     close = pair_sum(parts)
-    theirs = far(after(theirs, d_pre))
+    theirs = far(hold("far_feed", theirs, d_pre))
     d_pre, *parts = half_call(
         backward_body, 1, theirs, matrices, [slope], [(LOCAL_FF, d_pre)], True, "backward_far"
     )
@@ -1078,32 +1078,25 @@
     g_reduce = through_rows(activated, after(d_feed, away)).astype(BF16)
     d_gate_two = per_crop(after(adjoint, away) * feedout * keeping, sides)
     unit_two, scale_two = normed(middle)
-    d_normed_two = after(far_sum(away), g_reduce, d_gate_two) + close
+    d_normed_two = hold("d_normed_two", far_sum(away), g_reduce, d_gate_two) + close
     d_middle = adjoint + norm_back(d_normed_two * (1.0 + stretch_two), unit_two, scale_two)
     mine = (d_middle * gate_one * living).astype(BF16)
     theirs, ours = exchange(mine, 2), near(mine)
-    rows = after(jnp.concatenate(normed_two, axis=0), mine)
+    rows = after(jnp.concatenate(normed_two, axis=0), ours)
     g_expand = through_rows(rows, d_pre).astype(BF16)
-    forward_pieces = split_forward(g_expand, g_reduce, fast)
+    forward_pieces = split_forward(g_expand, g_reduce, False)
     d_offset_two = per_crop(after(d_normed_two, mine), sides)
     d_stretch_two = per_crop(after(d_normed_two, mine) * unit_two, sides)
-    theirs = after(theirs, forward_pieces, d_offset_two, d_stretch_two)
-    if fast:
-        forward_sum = owner_sum(forward_pieces, 0, None)
-    else:
-        forward_sum = owner_sum_slow(forward_pieces)
+    theirs = hold("d_branch", theirs, forward_pieces, d_offset_two, d_stretch_two)
+    forward_sum = owner_sum_slow(forward_pieces)
     d_branch = jnp.concatenate(ours + far(theirs), axis=0)
     d_mixed = against_cols(d_branch, w_project).astype(BF16)
     g_project = split_project(through_rows(mixed, d_branch).astype(BF16))
-    if fast:
-        d_mixed = after(d_mixed, forward_sum)
-        forward_sum = owner_sum(forward_pieces, 1, forward_sum)
+    d_mixed = hold("d_mixed", d_mixed)
     d_joint = halos_back(
         *attend_back(joint, halos, d_mixed, mixed, log_total, segq, segk, head_tok)
     )
     d_joint = hold("d_joint", d_joint)
-    if fast:
-        d_joint = after(d_joint, forward_sum)
 
     def normed_parts(rows, slots):
         return [against_cols(rows[j * count : (j + 1) * count], w_joint).astype(BF16) for j in slots]
@@ -1119,14 +1112,6 @@
         attention_pieces = split_attention(g_joint, g_project, fast)
     close = pair_sum(normed_parts(after(d_joint, away), (0, 1)))
     d_normed_one = after(far_sum(away), close, attention_pieces) + close
-    if fast:
-        attention_sum = None
-        for step in range(4):
-            attention_sum = owner_sum(attention_pieces, step, attention_sum)
-        for step in (2, 3):
-            forward_sum = owner_sum(forward_pieces, step, forward_sum, attention_pieces)
-    else:
-        attention_sum = owner_sum_slow(attention_pieces)
     unit_one, scale_one = normed(stream)
     d_stream = d_middle + norm_back(d_normed_one * (1.0 + stretch_one), unit_one, scale_one)
     d_gate_one = per_crop(d_middle * branch * living, sides)
@@ -1135,7 +1120,7 @@
     d_mod = jnp.stack(
         [d_offset_one, d_stretch_one, d_gate_one, d_offset_two, d_stretch_two, d_gate_two], axis=1
     )
-    return d_stream, d_mod, attention_sum, forward_sum
+    return d_stream, d_mod, attention_pieces, forward_sum
 
 
 def shards(
@@ -1166,18 +1151,21 @@
         forward_first = gather_planes(
             pack_forward(*after((expand_weight[0], reduce_weight[0]), pack), first)
         )
-        first = first + [exchange(piece, TP) for piece in first]
+        for k in range(4):
+            first.append(exchange(after(first[k], first[-1]) if k else first[0], TP))
+        mod_events, normed_events = [first[1], first[4]], [forward_first[0], first[5]]
     else:
         first = gather_slow(pack)
         forward_first = gather_slow(pack_forward(expand_weight[0], reduce_weight[0]))
-    opened = [open_attention(first)]
+        mod_events, normed_events = [], []
+    opened = open_attention(first)
     packs = []
-    held = first[:4]
+    held = opened
     for l in range(1, LAYERS):
-        attention = pack_attention(*after((joint_weight[l], project_weight[l]), held))
-        held = after((expand_weight[l], reduce_weight[l]), attention)
-        packs.append((attention, pack_forward(*held)))
-        held = packs[-1]
+        forward = pack_forward(*after((expand_weight[l], reduce_weight[l]), held))
+        attention = pack_attention(*after((joint_weight[l], project_weight[l]), forward))
+        packs.append((attention, forward))
+        held = attention
 
     stamps = jnp.zeros((planes, crops), jnp.int32)
     for step in range(planes):
@@ -1191,7 +1179,7 @@
     part = jnp.stack([dot(condition, modulation_weight[l]) for l in range(LAYERS)], axis=1)
     before = jnp.concatenate([jnp.zeros_like(part[:1]), part[:-1]])
     part = jnp.stack([before, part], axis=1)
-    part = after(lax.all_to_all(part, EVERY, 0, 0, tiled=True), first[:4])
+    part = after(lax.all_to_all(part, EVERY, 0, 0, tiled=True), mod_events)
     part = jnp.sum(part.reshape((planes, seq) + part.shape[1:]), axis=0)
     mods = jnp.transpose(part, (2, 1, 0, 3)).reshape(LAYERS, 2, 6, D)
 
@@ -1230,54 +1218,88 @@
         masks.append((dot(onehot, heads_on), active, keeping))
 
     stream = hidden_in[0].astype(F32)
-    records, weights, gathered = [], [], []
-    for attention, forward in packs:
-        gathered.append((gather_slow(attention), gather_slow(forward)))
-    w_joint, project_columns = opened[0]
+    records, weights = [], []
+    w_joint, project_columns = opened
+    forward_slow = [gather_slow(forward) for _, forward in packs]
     for l in range(LAYERS):
-        events, following = {}, None
+        events, pieces, others = {}, [], []
         if l + 1 < LAYERS:
-            following = open_attention(gathered[l][0])
-            events["feedout"] = [following]
+            attention, forward = packs[l]
+            events["halos"], events["mixed"] = [forward], [attention]
+            pieces = gather_planes(attention) if compact() else gather_slow(attention)
         if l == 0 and compact():
-            others = [exchange(after(forward_first[0], w_joint), TP)]
-            events["normed_one"] = [forward_first[0]]
-            events["halos"] = [packs[0][0]]
-            events["mixed"] = [others[0], packs[0][1]]
-
-        def hold(name, value, *more, events=events, l=l):
+            first_others = [exchange(after(forward_first[0], w_joint), TP)]
+            events["normed_one"] = normed_events
+            events["far_one"] = [forward_first[1]]
+            events["halos"] = events["halos"] + [forward_first[2]]
+            events["mixed"] = events["mixed"] + [forward_first[3], first_others[0]]
+
+        def hold(name, value, *more, events=events, l=l, pieces=pieces, others=others):
             if l == 0 and compact() and name == "halos":
-                others.extend(exchange(after(p, value), TP) for p in forward_first[1:])
-                events["branch"] = others[1:3]
+                first_others.extend(exchange(after(p, value), TP) for p in forward_first[1:])
+                events["branch"] = first_others[1:3]
+            if l + 1 < LAYERS and name == "branch" and compact():
+                events["branch"] = events.get("branch", []) + pieces[1:2]
+            if l + 1 < LAYERS and name == "far_two":
+                if compact():
+                    events["far_two"] = pieces[2:]
+                    for k in range(4):
+                        others.append(exchange(after(pieces[k], *others[-1:]), TP))
+                following.append(open_attention(pieces + others))
+                events["feedout"] = following
             return after(value, *more, *events.get(name, []))
 
         def open_here(mine, l=l):
             if l == 0:
-                return open_forward(forward_first + others if compact() else forward_first)
-            return open_forward(gathered[l - 1][1])
-
+                return open_forward(forward_first + first_others if compact() else forward_first)
+            return open_forward(forward_slow[l - 1])
+
+        following = []
         stream, record, used = layer_forward(
             stream, mods[l], w_joint, project_columns, open_here, masks[l], context, hold
         )
         records.append(record)
         weights.append(used)
-        if following is not None:
-            w_joint, project_columns = following
+        if following:
+            w_joint, project_columns = following[0]
     final_state = stream.astype(BF16)[None]
     adjoint = cotangent[0].astype(F32)
     grads, d_mods = [None] * LAYERS, [None] * LAYERS
-    returned = []
+    waiting = None
     for l in reversed(range(LAYERS)):
-
-        def hold(name, value, returned=tuple(returned)):
-            return after(value, *returned)
-
-        adjoint, d_mods[l], attention, forward = layer_backward(
+        state = {}
+
+        def hold(name, value, *more, waiting=waiting, state=state):
+            events = []
+            if waiting is not None:
+                above, pieces, forward_sum = waiting
+                steps = ["far_feed", "d_normed_two", "d_branch", "d_mixed"]
+                if compact() and name in steps:
+                    step = steps.index(name)
+                    state["sum"] = owner_sum(pieces, step, state.get("sum"))
+                    events.append(state["sum"])
+                if name == "d_branch":
+                    state["forward"] = tuple(return_forward(forward_sum))
+                    events.append(state["forward"])
+                if name == "d_joint":
+                    owned = state["sum"] if compact() else owner_sum_slow(pieces)
+                    state["attention"] = return_attention(owned)
+                    grads[above] = state["attention"] + state["forward"]
+                    events.append(state["attention"])
+            return after(value, *more, *events)
+
+        adjoint, d_mods[l], pieces, forward_sum = layer_backward(
             adjoint, records[l], mods[l], weights[l], masks[l], context, l == 0, hold
         )
-        forward = tuple(return_forward(forward))
-        grads[l] = return_attention(attention) + forward
-        returned.append(forward)
+        waiting = (l, pieces, forward_sum)
+    _, pieces, forward_sum = waiting
+    if compact():
+        owned = None
+        for step in range(4):
+            owned = owner_sum(pieces, step, owned)
+    else:
+        owned = owner_sum_slow(pieces)
+    grads[0] = return_attention(owned) + tuple(return_forward(forward_sum))
 
     d_mod = jnp.stack(d_mods, axis=1)
     d_mod = d_mod[1] + shifted(d_mod[0], -1)

time: 900 us -> 841 us (0.934)
  waiting for transfers between devices: 335 us -> 281 us
  other arithmetic: 75.6 us -> 64.2 us
  local copies, waits for them, and re-layouts: 70.1 us -> 80.4 us
    all_gather x2 -> x1, waiting for transfers between devices: 28.8 us -> 0.01 us  [gather_slow(): return [lax.all_gather(pack, OWNERS, axis=0, tiled=False)]]
    ppermute x15 -> x18, waiting for transfers between devices: 51.5 us -> 32.6 us  [from_plane(): lax.ppermute(value, 'dp', [(d, (d + back) % planes) for d in range(planes)])]
    ppermute x68 -> x72, waiting for transfers between devices: 228 us -> 212 us  [exchange(): return lax.ppermute(value, SEQ, [(i, i ^ mask) for i in range(seq)])]
    unnamed x511 -> x531, local copies, waits for them, and re-layouts: 44.1 us -> 57.8 us
    ppermute x15 -> x18, starting transfers between devices: 26.2 us -> 24.9 us  [from_plane(): lax.ppermute(value, 'dp', [(d, (d + back) % planes) for d in range(planes)])]
    ppermute x68 -> x72, starting transfers between devices: 47.6 us -> 46.8 us  [exchange(): return lax.ppermute(value, SEQ, [(i, i ^ mask) for i in range(seq)])]
  transfers between devices with their start and end apart: 110 -> 116, of which waited for: 46 -> 47; matrix products, arithmetic and copies ran while one was open for 18% -> 18% of each run, Pallas kernels for 19% -> 19%
where the time goes in v3:
time: 841 us; the launch traced here: 829 us
  waiting for transfers between devices  281 us (33%)
  Pallas kernels  176 us (21%)
  starting transfers between devices  144 us (17%)
  local copies, waits for them, and re-layouts  80.4 us (10%)
  matrix products  64.8 us (8%)
  other arithmetic  64.2 us (8%)
  between operations  18.1 us (2%)
    ppermute x72, waiting for transfers between devices, exchange(): return lax.ppermute(value, SEQ, [(i, i ^ mask) for i in range(seq)])  212 us
    pallas_call x12, Pallas kernels, half_call(): pl.pallas_call(kernel, grid=(2,), in_specs=specs + [pl.BlockSpec(memory_s...  72.4 us
    unnamed x531, local copies, waits for them, and re-layouts  57.8 us
    pallas_call x24, Pallas kernels, rearrange(): pl.pallas_call(body, in_specs=[pl.BlockSpec(memory_space=pltpu.SMEM)] + [...  49.8 us
    ppermute x72, starting transfers between devices, exchange(): return lax.ppermute(value, SEQ, [(i, i ^ mask) for i in range(seq)])  46.8 us
    dot_general x8, matrix products, through_rows(): lax.dot_general(left, right, (((0,), (0,)), ((), ())), preferred_element_...  32.6 us
    ppermute x18, waiting for transfers between devices, from_plane(): lax.ppermute(value, 'dp', [(d, (d + back) % planes) for d in range(planes)])  32.6 us
    pallas_call x2, Pallas kernels, attend_back(): pl.pallas_call(attend_back_kernel, grid_spec=pltpu.PrefetchScalarGridSpec...  31.7 us
  transfers between devices with their start and end apart: 116, of which 47 were waited for; matrix products, arithmetic and copies ran while one was open for 18% of the time, Pallas kernels for 19%

profile of v3, /device:TPU:0, one launch (start us, length us, event | category | flops | bytes accessed | tf_op | source)
XLA Modules:
  0.0 829.1 jit_solution(12019819897854505569)
XLA Ops:
  26.5 5.5 all-to-all-start
  40.2 6.6 collective-permute-done.7.refs_4_
  46.8 4.6 collective-permute-done.6.refs_1_
  55.3 5.2 all-to-all-done
  91.0 5.5 collective-permute-done.14.refs_7_
  143.7 6.8 collective-permute-done.20.b_ref
  160.0 6.5 collective-permute-done.18.refs_2_
  167.9 11.0 %attend.2 = (bf16[1024,384]{1,0:T(8,128)(2,1)S(1)}, f32[1024,128]{1,0:T(8,128)S(1)}) custom-call(s32[3]{0:T(128)S(1)} %copy-done.71, bf16[1024,1152]{1,0:T(8,128)(2,1)S(1)} %joint_far.2.q_ref.refs_0_.refs_1_.refs_2_.refs_3_.refs_4_.refs_5_, bf16[1024,1152]{1,0:T(8,128)(2,1)S(1)} %joint_far.2.q_ref.refs_0_.refs_1_.refs_2_.refs_3_.refs_4_.refs_5_, ...), custom_call_target="tpu_custom_call" | custom-call | flops 2684354560 | bytes 3145728 | tf_op jit(solution)/shard_map/attend/pallas_call | solution.py:840
  199.2 9.7 %collective-permute-done.25 = bf16[256,1152]{1,0:T(8,128)(2,1)} collective-permute-done((bf16[256,1152]{1,0:T(8,128)(2,1)}, bf16[256,1152]{1,0:T(8,128)(2,1)}, u32[]{:S(2)}, u32[]{:S(2)}) %collective-permute-start.25) | collective-permute-done | bytes 589856 | tf_op jit(solution)/shard_map/ppermute | solution.py:69
  210.4 9.8 %collective-permute-done.27.refs_6_ = bf16[288,1152]{1,0:T(8,128)(2,1)S(1)} collective-permute-done((bf16[288,1152]{1,0:T(8,128)(2,1)}, bf16[288,1152]{1,0:T(8,128)(2,1)S(1)}, u32[]{:S(2)}, u32[]{:S(2)}) %collective-permute-start.27) | collective-permute-done | bytes 663584 | tf_op jit(solution)/shard_map/ppermute | solution.py:69
  235.8 5.3 open_forward.2
  241.2 8.6 %forward_near.2 = (bf16[1024,1152]{1,0:T(8,128)(2,1)S(1)}, bf16[1024,1152]{1,0:T(8,128)(2,1)}, bf16[256,1152]{1,0:T(8,128)(2,1)S(1)}, bf16[256,1152]{1,0:T(8,128)(2,1)S(1)}) custom-call(bf16[256,1152]{1,0:T(8,128)(2,1)S(1)} %add_convert_fusion.3.a_ref, bf16[256,1152]{1,0:T(8,128)(2,1)} %collective-permute-done.31.b_ref, ...), custom_call_target="tpu_custom_call" | custom-call | flops 2717908992 | bytes 5308416 | tf_op jit(solution)/shard_map/forward_near/pallas_call | solution.py:626
  255.8 8.8 %forward_far.2 = (bf16[1024,1152]{1,0:T(8,128)(2,1)S(1)}, bf16[1024,1152]{1,0:T(8,128)(2,1)}, bf16[256,1152]{1,0:T(8,128)(2,1)S(1)}, bf16[256,1152]{1,0:T(8,128)(2,1)}) custom-call(bf16[256,1152]{1,0:T(8,128)(2,1)S(1)} %collective-permute-done.30.a_ref, ...), custom_call_target="tpu_custom_call", output_to_operand_aliasing={{0}: (6, {}), {1}: (7, {})} | custom-call | flops 2717908992 | bytes 5308416 | tf_op jit(solution)/shard_map/forward_far/pallas_call | solution.py:626
  268.1 10.7 %collective-permute-done.39.refs_5_ = bf16[144,1152]{1,0:T(8,128)(2,1)S(1)} collective-permute-done((bf16[144,1152]{1,0:T(8,128)(2,1)S(1)}, bf16[144,1152]{1,0:T(8,128)(2,1)S(1)}, u32[]{:S(2)}, u32[]{:S(2)}) %collective-permute-start.39) | collective-permute-done | bytes 331808 | tf_op jit(solution)/shard_map/ppermute | solution.py:69
  281.2 11.0 %collective-permute-done.40.refs_6_ = bf16[144,1152]{1,0:T(8,128)(2,1)S(1)} collective-permute-done((bf16[144,1152]{1,0:T(8,128)(2,1)}, bf16[144,1152]{1,0:T(8,128)(2,1)S(1)}, u32[]{:S(2)}, u32[]{:S(2)}) %collective-permute-start.40) | collective-permute-done | bytes 331808 | tf_op jit(solution)/shard_map/ppermute | solution.py:69
  294.6 7.7 collective-permute-done.41.refs_7_
  315.8 11.7 %collective-permute-done.43.a_ref = bf16[256,1152]{1,0:T(8,128)(2,1)S(1)} collective-permute-done((bf16[256,1152]{1,0:T(8,128)(2,1)S(1)}, bf16[256,1152]{1,0:T(8,128)(2,1)S(1)}, u32[]{:S(2)}, u32[]{:S(2)}) %collective-permute-start.43) | collective-permute-done | bytes 589856 | tf_op jit(solution)/shard_map/ppermute | solution.py:69
  337.4 9.4 %collective-permute-done.46.refs_6_.refs_7_ = bf16[256,768]{1,0:T(8,128)(2,1)} collective-permute-done((bf16[256,768]{1,0:T(8,128)(2,1)}, bf16[256,768]{1,0:T(8,128)(2,1)}, u32[]{:S(2)}, u32[]{:S(2)}) %collective-permute-start.46) | collective-permute-done | bytes 393248 | tf_op jit(solution)/shard_map/ppermute | solution.py:69
  347.9 11.2 %attend.3 = (bf16[1024,384]{1,0:T(8,128)(2,1)S(1)}, f32[1024,128]{1,0:T(8,128)S(1)}) custom-call(s32[3]{0:T(128)S(1)} %copy-done.72, bf16[1024,1152]{1,0:T(8,128)(2,1)S(1)} %joint_far.3.q_ref.refs_0_.refs_1_.refs_2_.refs_3_.refs_4_.refs_5_, bf16[1024,1152]{1,0:T(8,128)(2,1)S(1)} %joint_far.3.q_ref.refs_0_.refs_1_.refs_2_.refs_3_.refs_4_.refs_5_, ...), custom_call_target="tpu_custom_call" | custom-call | flops 2684354560 | bytes 3145728 | tf_op jit(solution)/shard_map/attend/pallas_call | solution.py:840
  367.6 13.4 %collective-permute-done.48 = bf16[256,1152]{1,0:T(8,128)(2,1)S(1)} collective-permute-done((bf16[256,1152]{1,0:T(8,128)(2,1)S(1)}, bf16[256,1152]{1,0:T(8,128)(2,1)S(1)}, u32[]{:S(2)}, u32[]{:S(2)}) %collective-permute-start.48) | collective-permute-done | bytes 589856 | tf_op jit(solution)/shard_map/ppermute | solution.py:69
  394.8 8.6 %forward_near.3 = (bf16[1024,1152]{1,0:T(8,128)(2,1)S(1)}, bf16[1024,1152]{1,0:T(8,128)(2,1)}, bf16[256,1152]{1,0:T(8,128)(2,1)S(1)}, bf16[256,1152]{1,0:T(8,128)(2,1)S(1)}) custom-call(bf16[256,1152]{1,0:T(8,128)(2,1)S(1)} %get-tuple-element.453.a_ref, bf16[256,1152]{1,0:T(8,128)(2,1)} %collective-permute-done.51.b_ref, bf16[1152,1152]{1,0:T(8,128)(2,1)} %copy-done.8, ...), custom_call_target="tpu_custom_call" | custom-call | flops 2717908992 | bytes 5308416 | tf_op jit(solution)/shard_map/forward_near/pallas_call | solution.py:626
  405.4 8.3 %forward_far.3 = (bf16[1024,1152]{1,0:T(8,128)(2,1)S(1)}, bf16[1024,1152]{1,0:T(8,128)(2,1)}, bf16[256,1152]{1,0:T(8,128)(2,1)S(1)}, bf16[256,1152]{1,0:T(8,128)(2,1)S(1)}) custom-call(bf16[256,1152]{1,0:T(8,128)(2,1)S(1)} %collective-permute-done.50.a_ref, ...), custom_call_target="tpu_custom_call", output_to_operand_aliasing={{0}: (6, {}), {1}: (7, {})} | custom-call | flops 2717908992 | bytes 5308416 | tf_op jit(solution)/shard_map/forward_far/pallas_call | solution.py:626
  414.0 7.1 backward_near.2
  423.2 6.7 backward_far.2
  431.2 6.0 collective-permute-done.54
  441.4 10.6 %collective-permute-done.60 = bf16[256,1152]{1,0:T(8,128)(2,1)S(1)} collective-permute-done((bf16[256,1152]{1,0:T(8,128)(2,1)S(1)}, bf16[256,1152]{1,0:T(8,128)(2,1)S(1)}, u32[]{:S(2)}, u32[]{:S(2)}) %collective-permute-start.60) | collective-permute-done | bytes 589856 | tf_op jit(solution)/shard_map/ppermute | solution.py:69
  466.5 7.1 collective-permute-done.63
  477.1 15.7 %attend_back.2 = (bf16[1024,1152]{1,0:T(8,128)(2,1)}, bf16[256,768]{1,0:T(8,128)(2,1)S(1)}, bf16[128,768]{1,0:T(8,128)(2,1)S(1)}) custom-call(s32[3]{0:T(128)S(1)} %copy-done.72, bf16[1024,1152]{1,0:T(8,128)(2,1)} %copy-done.1, bf16[1024,1152]{1,0:T(8,128)(2,1)} %copy-done.1, bf16[1024,1152]{1,0:T(8,128)(2,1)} %copy-done.1, bf16[1024,1152]{1,0:T(8,128)(2,1)} %copy-done.1, ...), custom_call_target="tpu_custom_call" | custom-call | flops 6710886400 | bytes 7864320 | tf_op jit(solution)/shard_map/attend_back/pallas_call | solution.py:872
  494.2 13.0 %collective-permute-done.65 = bf16[256,768]{1,0:T(8,128)(2,1)} collective-permute-done((bf16[256,768]{1,0:T(8,128)(2,1)}, bf16[256,768]{1,0:T(8,128)(2,1)}, u32[]{:S(2)}, u32[]{:S(2)}) %collective-permute-start.65) | collective-permute-done | bytes 393248 | tf_op jit(solution)/shard_map/ppermute | solution.py:69
  529.4 4.8 convolution_convert_fusion.3.joint_ref
  541.1 6.5 collective-permute-done.67
  555.8 6.8 backward_near.3
  562.6 7.0 collective-permute-done.69.a_ref
  573.1 7.1 backward_far.3
  585.0 4.8 convolution_convert_fusion.2.reduce_ref
  589.8 9.7 %collective-permute-done.74 = bf16[256,1152]{1,0:T(8,128)(2,1)S(1)} collective-permute-done((bf16[256,1152]{1,0:T(8,128)(2,1)S(1)}, bf16[256,1152]{1,0:T(8,128)(2,1)S(1)}, u32[]{:S(2)}, u32[]{:S(2)}) %collective-permute-start.74) | collective-permute-done | bytes 589856 | tf_op jit(solution)/shard_map/ppermute | solution.py:69
  623.2 5.8 convolution_convert_fusion.1.expand_ref
  638.7 8.5 %collective-permute-done.79 = bf16[256,1152]{1,0:T(8,128)(2,1)} collective-permute-done((bf16[256,1152]{1,0:T(8,128)(2,1)S(1)}, bf16[256,1152]{1,0:T(8,128)(2,1)}, u32[]{:S(2)}, u32[]{:S(2)}) %collective-permute-start.79) | collective-permute-done | bytes 589856 | tf_op jit(solution)/shard_map/ppermute | solution.py:69
  655.2 16.0 %attend_back.3 = (bf16[1024,1152]{1,0:T(8,128)(2,1)}, bf16[256,768]{1,0:T(8,128)(2,1)S(1)}, bf16[128,768]{1,0:T(8,128)(2,1)S(1)}) custom-call(s32[3]{0:T(128)S(1)} %copy-done.72, bf16[1024,1152]{1,0:T(8,128)(2,1)} %copy-done, bf16[1024,1152]{1,0:T(8,128)(2,1)} %copy-done, bf16[1024,1152]{1,0:T(8,128)(2,1)} %copy-done, bf16[1024,1152]{1,0:T(8,128)(2,1)} %copy-done, ...), custom_call_target="tpu_custom_call" | custom-call | flops 6710886400 | bytes 7864320 | tf_op jit(solution)/shard_map/attend_back/pallas_call | solution.py:872
  680.7 6.7 collective-permute-done.85
  689.2 7.0 convolution_convert_fusion.joint_ref
  707.4 8.7 %collective-permute-done.93 = bf16[144,1152]{1,0:T(8,128)(2,1)S(1)} collective-permute-done((bf16[144,1152]{1,0:T(8,128)(2,1)S(1)}, bf16[144,1152]{1,0:T(8,128)(2,1)S(1)}, u32[]{:S(2)}, u32[]{:S(2)}) %collective-permute-start.93) | collective-permute-done | bytes 331808 | tf_op jit(solution)/shard_map/ppermute | solution.py:69
  718.3 17.7 %collective-permute-done.92 = bf16[144,1152]{1,0:T(8,128)(2,1)S(1)} collective-permute-done((bf16[144,1152]{1,0:T(8,128)(2,1)S(1)}, bf16[144,1152]{1,0:T(8,128)(2,1)S(1)}, u32[]{:S(2)}, u32[]{:S(2)}) %collective-permute-start.92) | collective-permute-done | bytes 331808 | tf_op jit(solution)/shard_map/ppermute | solution.py:69
  742.0 5.6 collective-permute-done.95
  762.3 8.2 all-to-all-start.8
  770.5 8.6 %collective-permute-done.96 = bf16[144,1152]{1,0:T(8,128)(2,1)S(1)} collective-permute-done((bf16[144,1152]{1,0:T(8,128)(2,1)S(1)}, bf16[144,1152]{1,0:T(8,128)(2,1)S(1)}, u32[]{:S(2)}, u32[]{:S(2)}) %collective-permute-start.96) | collective-permute-done | bytes 331808 | tf_op jit(solution)/shard_map/ppermute | solution.py:81
  792.7 6.0 all-to-all-start.9
  805.3 10.3 %all-to-all-done.9.got_ref = bf16[8,144,432]{2,1,0:T(8,128)(2,1)S(1)} async-done(((bf16[8,144,432]{2,1,0:T(8,128)(2,1)}), bf16[8,144,432]{2,1,0:T(8,128)(2,1)S(1)}, u32[]{:S(2)}, u32[]{:S(2)}) %all-to-all-start.9) | async-done | bytes 995360 | tf_op jit(solution)/shard_map/all_to_all | solution.py:592
  (973 shorter events, 403.0 us)
Async XLA Ops:
  26.5 34.0 %all-to-all-start = ((f32[32,2,2,864]{3,2,1,0:T(2,128)}), f32[32,2,2,864]{3,2,1,0:T(2,128)}, u32[]{:S(2)}, u32[]{:S(2)}) async-start(f32[32,2,2,864]{3,2,1,0:T(2,128)} %copy.123), calls=%async_computation | async-start | bytes 917504 | tf_op jit(solution)/shard_map/all_to_all | solution.py:1182
  37.7 29.0 %collective-permute-start.8 = (bf16[144,1152]{1,0:T(8,128)(2,1)S(1)}, bf16[144,1152]{1,0:T(8,128)(2,1)S(1)}, u32[]{:S(2)}, u32[]{:S(2)}) collective-permute-start(bf16[144,1152]{1,0:T(8,128)(2,1)S(1)} %pack_attention.2.refs_0_), channel_id=1, source_target_pairs={{0,16},{8,24},{16,0},{24,8},{1,17},{9,25},{17,1},{25,9},{2,18},{10... | collective-permute-start | bytes 995336 | tf_op jit(solution)/shard_map/ppermute | solution.py:81
  60.5 20.4 %all-to-all-start.1 = ((bf16[8,144,432]{2,1,0:T(8,128)(2,1)}), bf16[8,144,432]{2,1,0:T(8,128)(2,1)S(1)}, u32[]{:S(2)}, u32[]{:S(2)}) async-start(bf16[8,144,432]{2,1,0:T(8,128)(2,1)} %pack_forward.2), calls=%async_computation.1 | async-start | bytes 2359296 | tf_op jit(solution)/shard_map/all_to_all | solution.py:498
  66.7 20.3 %collective-permute-start.13 = (bf16[144,1152]{1,0:T(8,128)(2,1)S(1)}, bf16[144,1152]{1,0:T(8,128)(2,1)}, u32[]{:S(2)}, u32[]{:S(2)}) collective-permute-start(bf16[144,1152]{1,0:T(8,128)(2,1)S(1)} %collective-permute-done.8.refs_2_), channel_id=1, source_target_pairs={{0,4},{1,5},{2,6},{3,7},{4,0},{5,1},{6,2},{7,3},{8,12},{9,13},{10,... | collective-permute-start | bytes 995336 | tf_op jit(solution)/shard_map/ppermute | solution.py:69
  82.6 24.1 %collective-permute-start.12 = (bf16[256,1152]{1,0:T(8,128)(2,1)}, bf16[256,1152]{1,0:T(8,128)(2,1)S(1)}, u32[]{:S(2)}, u32[]{:S(2)}) collective-permute-start(bf16[256,1152]{1,0:T(8,128)(2,1)} %fusion.29.a_ref), channel_id=1, source_target_pairs={{0,1},{1,0},{2,3},{3,2},{4,5},{5,4},{6,7},{7,6},{8,9},{9,8},{10,11... | collective-permute-start | bytes 1769480 | tf_op jit(solution)/shard_map/ppermute | solution.py:69
  82.6 31.0 %collective-permute-start.11 = (bf16[256,1152]{1,0:T(8,128)(2,1)}, bf16[256,1152]{1,0:T(8,128)(2,1)}, u32[]{:S(2)}, u32[]{:S(2)}) collective-permute-start(bf16[256,1152]{1,0:T(8,128)(2,1)} %fusion.29.a_ref), channel_id=1, source_target_pairs={{0,2},{1,3},{2,0},{3,1},{4,6},{5,7},{6,4},{7,5},{8,10},{9,11},{10,... | collective-permute-start | bytes 1769480 | tf_op jit(solution)/shard_map/ppermute | solution.py:69
  83.1 30.5 %collective-permute-start.15 = (bf16[288,1152]{1,0:T(8,128)(2,1)}, bf16[288,1152]{1,0:T(8,128)(2,1)}, u32[]{:S(2)}, u32[]{:S(2)}) collective-permute-start(bf16[288,1152]{1,0:T(8,128)(2,1)} %unpack_forward.2.refs_0_), channel_id=1, source_target_pairs={{0,8},{8,16},{16,24},{24,0},{1,9},{9,17},{17,25},{25,1},{2,10},{10... | collective-permute-start | bytes 1990664 | tf_op jit(solution)/shard_map/ppermute | solution.py:81
  103.2 27.3 %all-to-all-start.2 = ((bf16[8,144,432]{2,1,0:T(8,128)(2,1)}), bf16[8,144,432]{2,1,0:T(8,128)(2,1)S(1)}, u32[]{:S(2)}, u32[]{:S(2)}) async-start(bf16[8,144,432]{2,1,0:T(8,128)(2,1)} %pack_forward.3), calls=%async_computation.2 | async-start | bytes 2359296 | tf_op jit(solution)/shard_map/all_to_all | solution.py:498
  119.0 61.7 %collective-permute-start.22 = (bf16[288,1152]{1,0:T(8,128)(2,1)}, bf16[288,1152]{1,0:T(8,128)(2,1)}, u32[]{:S(2)}, u32[]{:S(2)}) collective-permute-start(bf16[288,1152]{1,0:T(8,128)(2,1)} %unpack_forward.2.refs_0_), channel_id=1, source_target_pairs={{0,24},{8,0},{16,8},{24,16},{1,25},{9,1},{17,9},{25,17},{2,26},{10... | collective-permute-start | bytes 1990664 | tf_op jit(solution)/shard_map/ppermute | solution.py:81
  119.3 47.2 %collective-permute-start.18 = (bf16[288,1152]{1,0:T(8,128)(2,1)}, bf16[288,1152]{1,0:T(8,128)(2,1)}, u32[]{:S(2)}, u32[]{:S(2)}) collective-permute-start(bf16[288,1152]{1,0:T(8,128)(2,1)} %unpack_forward.2.refs_0_), channel_id=1, source_target_pairs={{0,16},{8,24},{16,0},{24,8},{1,17},{9,25},{17,1},{25,9},{2,18},{10... | collective-permute-start | bytes 1990664 | tf_op jit(solution)/shard_map/ppermute | solution.py:81
  122.6 58.1 %collective-permute-start.23 = (bf16[288,1152]{1,0:T(8,128)(2,1)}, bf16[288,1152]{1,0:T(8,128)(2,1)}, u32[]{:S(2)}, u32[]{:S(2)}) collective-permute-start(bf16[288,1152]{1,0:T(8,128)(2,1)} %unpack_forward.2.refs_0_), channel_id=1, source_target_pairs={{0,4},{1,5},{2,6},{3,7},{4,0},{5,1},{6,2},{7,3},{8,12},{9,13},{10,... | collective-permute-start | bytes 1990664 | tf_op jit(solution)/shard_map/ppermute | solution.py:69
  130.2 36.3 %collective-permute-start.17 = (bf16[256,768]{1,0:T(8,128)(2,1)}, bf16[256,768]{1,0:T(8,128)(2,1)}, u32[]{:S(2)}, u32[]{:S(2)}) collective-permute-start(bf16[256,768]{1,0:T(8,128)(2,1)} %constant_dynamic-slice_fusion.1), channel_id=1, source_target_pairs={{0,4},{1,5},{2,6},{3,7},{4,0},{5,1},{6,2},{7,3},{8,12},{9,13},{10,... | collective-permute-start | bytes 1179656 | tf_op jit(solution)/shard_map/ppermute | solution.py:69
  136.2 44.5 %all-to-all-start.3 = ((bf16[4,288,288]{2,1,0:T(8,128)(2,1)}), bf16[4,288,288]{2,1,0:T(8,128)(2,1)}, u32[]{:S(2)}, u32[]{:S(2)}) async-start(bf16[4,288,288]{2,1,0:T(8,128)(2,1)} %copy-done.47), calls=%async_computation.3 | async-start | bytes 1769472 | tf_op jit(solution)/shard_map/all_to_all | solution.py:523
  140.8 247.6 %all-gather.3.cloned.1.call-start = ((), (), s32[]{:S(2)}) async-start(), calls=%async_computation.14 | async-start | bytes 5971968 | tf_op jit(solution)/shard_map/all_gather | solution.py:507
  188.0 22.4 %collective-permute-start.26 = (bf16[288,1152]{1,0:T(8,128)(2,1)}, bf16[288,1152]{1,0:T(8,128)(2,1)S(1)}, u32[]{:S(2)}, u32[]{:S(2)}) collective-permute-start(bf16[288,1152]{1,0:T(8,128)(2,1)} %collective-permute-done.15.refs_1_), channel_id=1, source_target_pairs={{0,4},{1,5},{2,6},{3,7},{4,0},{5,1},{6,2},{7,3},{8,12},{9,13},{10,... | collective-permute-start | bytes 1990664 | tf_op jit(solution)/shard_map/ppermute | solution.py:69
  188.8 31.4 %collective-permute-start.27 = (bf16[288,1152]{1,0:T(8,128)(2,1)}, bf16[288,1152]{1,0:T(8,128)(2,1)S(1)}, u32[]{:S(2)}, u32[]{:S(2)}) collective-permute-start(bf16[288,1152]{1,0:T(8,128)(2,1)} %collective-permute-done.18.refs_2_), channel_id=1, source_target_pairs={{0,4},{1,5},{2,6},{3,7},{4,0},{5,1},{6,2},{7,3},{8,12},{9,13},{10,... | collective-permute-start | bytes 1990664 | tf_op jit(solution)/shard_map/ppermute | solution.py:69
  196.4 23.9 %collective-permute-start.29 = (bf16[256,1152]{1,0:T(8,128)(2,1)}, bf16[256,1152]{1,0:T(8,128)(2,1)}, u32[]{:S(2)}, u32[]{:S(2)}) collective-permute-start(bf16[256,1152]{1,0:T(8,128)(2,1)} %convolution_convert_fusion.20), channel_id=1, source_target_pairs={{0,1},{1,0},{2,3},{3,2},{4,5},{5,4},{6,7},{7,6},{8,9},{9,8},{10,11... | collective-permute-start | bytes 1769480 | tf_op jit(solution)/shard_map/ppermute | solution.py:69
  208.9 24.8 %collective-permute-start.32 = (bf16[288,1152]{1,0:T(8,128)(2,1)}, bf16[288,1152]{1,0:T(8,128)(2,1)}, u32[]{:S(2)}, u32[]{:S(2)}) collective-permute-start(bf16[288,1152]{1,0:T(8,128)(2,1)} %collective-permute-done.22.refs_3_), channel_id=1, source_target_pairs={{0,4},{1,5},{2,6},{3,7},{4,0},{5,1},{6,2},{7,3},{8,12},{9,13},{10,... | collective-permute-start | bytes 1990664 | tf_op jit(solution)/shard_map/ppermute | solution.py:69
  225.3 28.5 %collective-permute-start.30 = (bf16[256,1152]{1,0:T(8,128)(2,1)S(1)}, bf16[256,1152]{1,0:T(8,128)(2,1)S(1)}, u32[]{:S(2)}, u32[]{:S(2)}) collective-permute-start(bf16[256,1152]{1,0:T(8,128)(2,1)S(1)} %add_convert_fusion.3.a_ref), channel_id=1, source_target_pairs={{0,2},{1,3},{2,0},{3,1},{4,6},{5,7},{6,4},{7,5},{8,10},{9,11},{10,... | collective-permute-start | bytes 1769480 | tf_op jit(solution)/shard_map/ppermute | solution.py:69
  227.9 22.6 %collective-permute-start.34 = (bf16[144,1152]{1,0:T(8,128)(2,1)S(1)}, bf16[144,1152]{1,0:T(8,128)(2,1)S(1)}, u32[]{:S(2)}, u32[]{:S(2)}) collective-permute-start(bf16[144,1152]{1,0:T(8,128)(2,1)S(1)} %copy-done.44), channel_id=1, source_target_pairs={{0,24},{8,0},{16,8},{24,16},{1,25},{9,1},{17,9},{25,17},{2,26},{10... | collective-permute-start | bytes 995336 | tf_op jit(solution)/shard_map/ppermute | solution.py:81
  229.9 24.0 %collective-permute-start.33 = (bf16[144,1152]{1,0:T(8,128)(2,1)S(1)}, bf16[144,1152]{1,0:T(8,128)(2,1)}, u32[]{:S(2)}, u32[]{:S(2)}) collective-permute-start(bf16[144,1152]{1,0:T(8,128)(2,1)S(1)} %copy-done.44), channel_id=1, source_target_pairs={{0,16},{8,24},{16,0},{24,8},{1,17},{9,25},{17,1},{25,9},{2,18},{10... | collective-permute-start | bytes 995336 | tf_op jit(solution)/shard_map/ppermute | solution.py:81
  281.2 24.4 %collective-permute-start.37 = (bf16[256,1152]{1,0:T(8,128)(2,1)}, bf16[256,1152]{1,0:T(8,128)(2,1)}, u32[]{:S(2)}, u32[]{:S(2)}) collective-permute-start(bf16[256,1152]{1,0:T(8,128)(2,1)} %fusion.106), channel_id=1, source_target_pairs={{0,2},{1,3},{2,0},{3,1},{4,6},{5,7},{6,4},{7,5},{8,10},{9,11},{10,... | collective-permute-start | bytes 1769480 | tf_op jit(solution)/shard_map/ppermute | solution.py:69
  281.2 26.2 %collective-permute-start.42 = (bf16[256,1152]{1,0:T(8,128)(2,1)}, bf16[256,1152]{1,0:T(8,128)(2,1)}, u32[]{:S(2)}, u32[]{:S(2)}) collective-permute-start(bf16[256,1152]{1,0:T(8,128)(2,1)} %copy-done.97), channel_id=1, source_target_pairs={{0,1},{1,0},{2,3},{3,2},{4,5},{5,4},{6,7},{7,6},{8,9},{9,8},{10,11... | collective-permute-start | bytes 1769480 | tf_op jit(solution)/shard_map/ppermute | solution.py:69
  332.7 28.1 %all-to-all-start.4 = ((bf16[4,288,288]{2,1,0:T(8,128)(2,1)}), bf16[4,288,288]{2,1,0:T(8,128)(2,1)}, u32[]{:S(2)}, u32[]{:S(2)}) async-start(bf16[4,288,288]{2,1,0:T(8,128)(2,1)} %copy-done.48), calls=%async_computation.4 | async-start | bytes 1769472 | tf_op jit(solution)/shard_map/all_to_all | solution.py:523
  336.9 274.9 %reduce-scatter.3.cloned.1.call-start = ((), (), s32[]{:S(2)}) async-start(), calls=%async_computation.12 | async-start | bytes 5971968 | tf_op jit(solution)/shard_map/reduce_scatter | solution.py:572
  430.4 21.7 %collective-permute-start.55 = (bf16[256,1152]{1,0:T(8,128)(2,1)S(1)}, bf16[256,1152]{1,0:T(8,128)(2,1)S(1)}, u32[]{:S(2)}, u32[]{:S(2)}) collective-permute-start(bf16[256,1152]{1,0:T(8,128)(2,1)S(1)} %get-tuple-element.198), channel_id=1, source_target_pairs={{0,1},{1,0},{2,3},{3,2},{4,5},{5,4},{6,7},{7,6},{8,9},{9,8},{10,11... | collective-permute-start | bytes 1769480 | tf_op jit(solution)/shard_map/ppermute | solution.py:69
  430.6 21.5 %collective-permute-start.61 = (bf16[256,1152]{1,0:T(8,128)(2,1)S(1)}, bf16[256,1152]{1,0:T(8,128)(2,1)S(1)}, u32[]{:S(2)}, u32[]{:S(2)}) collective-permute-start(bf16[256,1152]{1,0:T(8,128)(2,1)S(1)} %get-tuple-element.209), channel_id=1, source_target_pairs={{0,1},{1,0},{2,3},{3,2},{4,5},{5,4},{6,7},{7,6},{8,9},{9,8},{10,11... | collective-permute-start | bytes 1769480 | tf_op jit(solution)/shard_map/ppermute | solution.py:69
  525.6 22.1 %collective-permute-start.67 = (bf16[256,1152]{1,0:T(8,128)(2,1)}, bf16[256,1152]{1,0:T(8,128)(2,1)}, u32[]{:S(2)}, u32[]{:S(2)}) collective-permute-start(bf16[256,1152]{1,0:T(8,128)(2,1)} %fusion.7), channel_id=1, source_target_pairs={{0,2},{1,3},{2,0},{3,1},{4,6},{5,7},{6,4},{7,5},{8,10},{9,11},{10,... | collective-permute-start | bytes 1769480 | tf_op jit(solution)/shard_map/ppermute | solution.py:69
  529.4 19.5 %collective-permute-start.68 = (bf16[256,1152]{1,0:T(8,128)(2,1)}, bf16[256,1152]{1,0:T(8,128)(2,1)}, u32[]{:S(2)}, u32[]{:S(2)}) collective-permute-start(bf16[256,1152]{1,0:T(8,128)(2,1)} %convolution_convert_fusion.12), channel_id=1, source_target_pairs={{0,1},{1,0},{2,3},{3,2},{4,5},{5,4},{6,7},{7,6},{8,9},{9,8},{10,11... | collective-permute-start | bytes 1769480 | tf_op jit(solution)/shard_map/ppermute | solution.py:69
  571.6 47.2 %collective-permute-start.80 = (bf16[144,1152]{1,0:T(8,128)(2,1)}, bf16[144,1152]{1,0:T(8,128)(2,1)}, u32[]{:S(2)}, u32[]{:S(2)}) collective-permute-start(bf16[144,1152]{1,0:T(8,128)(2,1)} %get-tuple-element.226), channel_id=1, source_target_pairs={{0,4},{1,5},{2,6},{3,7},{4,0},{5,1},{6,2},{7,3},{8,12},{9,13},{10,... | collective-permute-start | bytes 995336 | tf_op jit(solution)/shard_map/ppermute | solution.py:69
  583.1 35.6 %collective-permute-start.81 = (bf16[144,1152]{1,0:T(8,128)(2,1)}, bf16[144,1152]{1,0:T(8,128)(2,1)}, u32[]{:S(2)}, u32[]{:S(2)}) collective-permute-start(bf16[144,1152]{1,0:T(8,128)(2,1)} %add_convert_fusion.12), channel_id=1, source_target_pairs={{0,8},{8,16},{16,24},{24,0},{1,9},{9,17},{17,25},{25,1},{2,10},{10... | collective-permute-start | bytes 995336 | tf_op jit(solution)/shard_map/ppermute | solution.py:81
  603.7 19.5 %collective-permute-start.78 = (bf16[256,1152]{1,0:T(8,128)(2,1)S(1)}, bf16[256,1152]{1,0:T(8,128)(2,1)}, u32[]{:S(2)}, u32[]{:S(2)}) collective-permute-start(bf16[256,1152]{1,0:T(8,128)(2,1)S(1)} %get-tuple-element.392), channel_id=1, source_target_pairs={{0,1},{1,0},{2,3},{3,2},{4,5},{5,4},{6,7},{7,6},{8,9},{9,8},{10,11... | collective-permute-start | bytes 1769480 | tf_op jit(solution)/shard_map/ppermute | solution.py:69
  606.8 41.7 %collective-permute-start.83 = (bf16[144,1152]{1,0:T(8,128)(2,1)}, bf16[144,1152]{1,0:T(8,128)(2,1)}, u32[]{:S(2)}, u32[]{:S(2)}) collective-permute-start(bf16[144,1152]{1,0:T(8,128)(2,1)} %get-tuple-element.227), channel_id=1, source_target_pairs={{0,4},{1,5},{2,6},{3,7},{4,0},{5,1},{6,2},{7,3},{8,12},{9,13},{10,... | collective-permute-start | bytes 995336 | tf_op jit(solution)/shard_map/ppermute | solution.py:69
  615.0 20.9 %all-to-all-start.6 = ((bf16[8,144,432]{2,1,0:T(8,128)(2,1)}), bf16[8,144,432]{2,1,0:T(8,128)(2,1)S(1)}, u32[]{:S(2)}, u32[]{:S(2)}) async-start(bf16[8,144,432]{2,1,0:T(8,128)(2,1)} %pack_return.2), calls=%async_computation.7 | async-start | bytes 2359296 | tf_op jit(solution)/shard_map/all_to_all | solution.py:592
  618.7 167.4 %reduce-scatter.5.cloned.1.call-start = ((), (), s32[]{:S(2)}) async-start(), calls=%async_computation.13 | async-start | bytes 5971968 | tf_op jit(solution)/shard_map/reduce_scatter | solution.py:572
  620.7 27.8 %collective-permute-start.84 = (bf16[144,1152]{1,0:T(8,128)(2,1)}, bf16[144,1152]{1,0:T(8,128)(2,1)}, u32[]{:S(2)}, u32[]{:S(2)}) collective-permute-start(bf16[144,1152]{1,0:T(8,128)(2,1)} %add_convert_fusion.11), channel_id=1, source_target_pairs={{0,8},{8,16},{16,24},{24,0},{1,9},{9,17},{17,25},{25,1},{2,10},{10... | collective-permute-start | bytes 995336 | tf_op jit(solution)/shard_map/ppermute | solution.py:81
  621.2 26.0 %collective-permute-start.79 = (bf16[256,1152]{1,0:T(8,128)(2,1)S(1)}, bf16[256,1152]{1,0:T(8,128)(2,1)}, u32[]{:S(2)}, u32[]{:S(2)}) collective-permute-start(bf16[256,1152]{1,0:T(8,128)(2,1)S(1)} %get-tuple-element.392), channel_id=1, source_target_pairs={{0,2},{1,3},{2,0},{3,1},{4,6},{5,7},{6,4},{7,5},{8,10},{9,11},{10,... | collective-permute-start | bytes 1769480 | tf_op jit(solution)/shard_map/ppermute | solution.py:69
  676.8 19.4 %all-to-all-start.7 = ((bf16[4,288,288]{2,1,0:T(8,128)(2,1)}), bf16[4,288,288]{2,1,0:T(8,128)(2,1)S(1)}, u32[]{:S(2)}, u32[]{:S(2)}) async-start(bf16[4,288,288]{2,1,0:T(8,128)(2,1)} %split_project.3), calls=%async_computation.8 | async-start | bytes 1769472 | tf_op jit(solution)/shard_map/all_to_all | solution.py:546
  705.3 34.2 %collective-permute-start.91 = (bf16[144,1152]{1,0:T(8,128)(2,1)S(1)}, bf16[144,1152]{1,0:T(8,128)(2,1)S(1)}, u32[]{:S(2)}, u32[]{:S(2)}) collective-permute-start(bf16[144,1152]{1,0:T(8,128)(2,1)S(1)} %get-tuple-element.259), channel_id=1, source_target_pairs={{0,4},{1,5},{2,6},{3,7},{4,0},{5,1},{6,2},{7,3},{8,12},{9,13},{10,... | collective-permute-start | bytes 995336 | tf_op jit(solution)/shard_map/ppermute | solution.py:69
  705.6 30.4 %collective-permute-start.92 = (bf16[144,1152]{1,0:T(8,128)(2,1)S(1)}, bf16[144,1152]{1,0:T(8,128)(2,1)S(1)}, u32[]{:S(2)}, u32[]{:S(2)}) collective-permute-start(bf16[144,1152]{1,0:T(8,128)(2,1)S(1)} %get-tuple-element.258), channel_id=1, source_target_pairs={{0,4},{1,5},{2,6},{3,7},{4,0},{5,1},{6,2},{7,3},{8,12},{9,13},{10,... | collective-permute-start | bytes 995336 | tf_op jit(solution)/shard_map/ppermute | solution.py:69
  716.1 19.8 %collective-permute-start.94 = (bf16[144,1152]{1,0:T(8,128)(2,1)S(1)}, bf16[144,1152]{1,0:T(8,128)(2,1)S(1)}, u32[]{:S(2)}, u32[]{:S(2)}) collective-permute-start(bf16[144,1152]{1,0:T(8,128)(2,1)S(1)} %add_convert_fusion.9), channel_id=1, source_target_pairs={{0,8},{8,16},{16,24},{24,0},{1,9},{9,17},{17,25},{25,1},{2,10},{10... | collective-permute-start | bytes 995336 | tf_op jit(solution)/shard_map/ppermute | solution.py:81
  717.3 32.4 %collective-permute-start.87 = (bf16[256,1152]{1,0:T(8,128)(2,1)S(1)}, bf16[256,1152]{1,0:T(8,128)(2,1)S(1)}, u32[]{:S(2)}, u32[]{:S(2)}) collective-permute-start(bf16[256,1152]{1,0:T(8,128)(2,1)S(1)} %fusion.3), channel_id=1, source_target_pairs={{0,2},{1,3},{2,0},{3,1},{4,6},{5,7},{6,4},{7,5},{8,10},{9,11},{10,... | collective-permute-start | bytes 1769480 | tf_op jit(solution)/shard_map/ppermute | solution.py:69
  738.1 51.1 %collective-permute-start.100 = (bf16[288,144]{1,0:T(8,128)(2,1)S(1)}, bf16[288,144]{1,0:T(8,128)(2,1)}, u32[]{:S(2)}, u32[]{:S(2)}) collective-permute-start(bf16[288,144]{1,0:T(8,128)(2,1)S(1)} %copy-done.107), channel_id=1, source_target_pairs={{0,0},{5,1},{3,2},{4,3},{2,4},{7,5},{1,6},{6,7},{8,8},{13,9},{11,1... | collective-permute-start | bytes 248840 | tf_op jit(solution)/shard_map/ppermute | solution.py:143
  739.5 60.3 %collective-permute-start.101 = (bf16[288,144]{1,0:T(8,128)(2,1)S(1)}, bf16[288,144]{1,0:T(8,128)(2,1)}, u32[]{:S(2)}, u32[]{:S(2)}) collective-permute-start(bf16[288,144]{1,0:T(8,128)(2,1)S(1)} %copy-done.105), channel_id=1, source_target_pairs={{4,0},{2,1},{7,2},{1,3},{6,4},{0,5},{5,6},{3,7},{12,8},{10,9},{15,... | collective-permute-start | bytes 248840 | tf_op jit(solution)/shard_map/ppermute | solution.py:143
  747.6 52.2 %collective-permute-start.102 = (bf16[288,144]{1,0:T(8,128)(2,1)S(1)}, bf16[288,144]{1,0:T(8,128)(2,1)}, u32[]{:S(2)}, u32[]{:S(2)}) collective-permute-start(bf16[288,144]{1,0:T(8,128)(2,1)S(1)} %copy-done.103), channel_id=1, source_target_pairs={{1,0},{6,1},{0,2},{5,3},{3,4},{4,5},{2,6},{7,7},{9,8},{14,9},{8,10... | collective-permute-start | bytes 248840 | tf_op jit(solution)/shard_map/ppermute | solution.py:143
  749.7 20.8 %collective-permute-start.90 = (bf16[144,1152]{1,0:T(8,128)(2,1)}, bf16[144,1152]{1,0:T(8,128)(2,1)}, u32[]{:S(2)}, u32[]{:S(2)}) collective-permute-start(bf16[144,1152]{1,0:T(8,128)(2,1)} %get-tuple-element.260), channel_id=1, source_target_pairs={{0,4},{1,5},{2,6},{3,7},{4,0},{5,1},{6,2},{7,3},{8,12},{9,13},{10,... | collective-permute-start | bytes 995336 | tf_op jit(solution)/shard_map/ppermute | solution.py:69
  762.3 30.5 %all-to-all-start.8 = ((f32[32,2,864]{2,1,0:T(2,128)}), f32[32,2,864]{2,1,0:T(2,128)S(1)}, u32[]{:S(2)}, u32[]{:S(2)}) async-start(f32[32,2,864]{2,1,0:T(2,128)} %bitcast.68), calls=%async_computation.9 | async-start | bytes 458752 | tf_op jit(solution)/shard_map/all_to_all | solution.py:1309
  792.7 22.8 %all-to-all-start.9 = ((bf16[8,144,432]{2,1,0:T(8,128)(2,1)}), bf16[8,144,432]{2,1,0:T(8,128)(2,1)S(1)}, u32[]{:S(2)}, u32[]{:S(2)}) async-start(bf16[8,144,432]{2,1,0:T(8,128)(2,1)} %pack_return.3), calls=%async_computation.11 | async-start | bytes 2359296 | tf_op jit(solution)/shard_map/all_to_all | solution.py:592
  (329 other events, 2779.8 us)
Sparse Core Ops, SparseCore 0:
  268.2 91.4 all-gather.2
  494.3 117.5 reduce-scatter.2
  651.6 122.6 reduce-scatter.4

commit v4 on v3

--- a/solution.py
+++ b/solution.py
@@ -131,10 +131,14 @@
 def deal_joint(joint):
     seq, groups, _ = sizes()
     pairs, _ = kinds_table(seq, groups)
-    cols = joint.shape[1] // 3
-    return [
-        lax.ppermute(joint[:, r * cols : (r + 1) * cols], SEQ, pairs[r]) for r in range(3)
+    cols = joint.shape[2] // 3
+    sent = [
+        jnp.concatenate(
+            [joint[l, :, r * cols : (r + 1) * cols] for l in range(LAYERS)], axis=1
+        )
+        for r in range(3)
     ]
+    return [lax.ppermute(part, SEQ, pairs[r]) for r, part in enumerate(sent)]
 
 
 def return_joint(parts):
@@ -149,10 +153,18 @@
     return jnp.where(which == 0, first, jnp.where(which == 1, second, third))
 
 
-def pack_attention_any(got, project):
+def pack_attention_any(got, projects):
     kinds = my_kinds()
-    sent = [jnp.where(kinds[0] == k, got[0], jnp.where(kinds[1] == k, got[1], got[2])) for k in range(3)]
-    return jnp.concatenate(sent + [project], axis=1)
+    cols = projects[0].shape[1]
+    packs = []
+    for l, project in enumerate(projects):
+        parts = [part[:, l * cols : (l + 1) * cols] for part in got]
+        sent = [
+            jnp.where(kinds[0] == k, parts[0], jnp.where(kinds[1] == k, parts[1], parts[2]))
+            for k in range(3)
+        ]
+        packs.append(jnp.concatenate(sent + [project], axis=1))
+    return packs
 
 
 def open_attention_any(stack):
@@ -295,16 +307,19 @@
     return (3 * source + r) // 8
 
 
-def pack_attention_kernel(me_ref, a_ref, b_ref, c_ref, project_ref, out_ref):
-    cols = a_ref.shape[1]
+def pack_attention_kernel(me_ref, a_ref, b_ref, c_ref, *refs):
+    cols = refs[0].shape[1]
     first, second = kind_sent(me_ref, 0), kind_sent(me_ref, 1)
-    for half in range(2):
-        rows = slice(half * cols, (half + 1) * cols)
-        a, b, c = a_ref[rows], b_ref[rows], c_ref[rows]
-        parts = [jnp.where(first == k, a, jnp.where(second == k, b, c)) for k in range(3)]
-        out_ref[:, half * 4 * cols : (half + 1) * 4 * cols] = side_by_side(
-            parts + [project_ref[rows]]
-        )
+    for l in range(LAYERS):
+        project_ref, out_ref = refs[l], refs[LAYERS + l]
+        at = slice(l * cols, (l + 1) * cols)
+        for half in range(2):
+            rows = slice(half * cols, (half + 1) * cols)
+            a, b, c = a_ref[rows, at], b_ref[rows, at], c_ref[rows, at]
+            parts = [jnp.where(first == k, a, jnp.where(second == k, b, c)) for k in range(3)]
+            out_ref[:, half * 4 * cols : (half + 1) * 4 * cols] = side_by_side(
+                parts + [project_ref[rows]]
+            )
 
 
 def by_plane(me_ref, refs):
@@ -481,11 +496,12 @@
 
 def pack_attention(joint, project):
     got = deal_joint(joint)
+    projects = [project[l] for l in range(LAYERS)]
     if not compact():
-        return pack_attention_any(got, project)
-    cols = project.shape[1]
-    outs = [((cols, 8 * cols), BF16)]
-    return rearrange(pack_attention_kernel, [*got, project], outs, "pack_attention")[0]
+        return pack_attention_any(got, projects)
+    cols = project.shape[2]
+    outs = [((cols, 8 * cols), BF16)] * LAYERS
+    return rearrange(pack_attention_kernel, [*got, *projects], outs, "pack_attention")
 
 
 def pack_forward(expand, reduce, *events):
@@ -636,6 +652,32 @@
         ),
         name=name,
     )(*operands, *kept)
+
+
+def slot_products(product, half, tokens, matrix, name, slots=TP):
+    count = tokens.shape[0] // slots
+
+    def kernel(rows_ref, matrix_ref, a_ref, b_ref):
+        value = product(rows_ref[...], matrix_ref[...])
+        put_partial(pl.program_id(0) == 0, value, a_ref, b_ref)
+
+    return pl.pallas_call(
+        kernel,
+        grid=(2,),
+        in_specs=[
+            pl.BlockSpec((count, tokens.shape[1]), lambda i: (2 * half + i, 0)),
+            pl.BlockSpec(matrix.shape, lambda i: (0, 0)),
+        ],
+        out_specs=[pl.BlockSpec((count, D), lambda i: (0, 0))] * 2,
+        out_shape=[jax.ShapeDtypeStruct((count, D), BF16)] * 2,
+        compiler_params=kernel_params(),
+        cost_estimate=pl.CostEstimate(
+            flops=4 * count * math.prod(matrix.shape),
+            bytes_accessed=2 * math.prod(matrix.shape),
+            transcendentals=0,
+        ),
+        name=name,
+    )(tokens, matrix)
 
 
 def put_partial(mine, value, a_ref, b_ref):
@@ -706,14 +748,10 @@
     return prev, here_ref[:, low:high], following
 
 
-def attend_kernel(
-    me_ref,
-    q_ref,
-    *refs,
-):
+def attend_kernel(base, me_ref, q_ref, *refs):
     keys, values, halos = refs[0:3], refs[3:6], refs[6:8]
     segq_ref, segk_ref, head_ref, mixed_ref, lse_ref = refs[8:]
-    block = pl.program_id(0) ^ me_ref[2]
+    block = (base + pl.program_id(0)) ^ me_ref[2]
     count = q_ref.shape[0]
     allowed = segq_ref[...] == segk_ref[0]
     tiles = [jnp.zeros((count, LANES), F32) for _ in range(WIDTH // LANES)]
@@ -809,23 +847,24 @@
     )
 
 
-def block_specs(count):
+def block_specs(count, base=0):
     def rows(width):
-        return pl.BlockSpec((count, width), lambda j, me: (j, 0))
+        return pl.BlockSpec((count, width), lambda j, me: (base + j, 0))
 
     def whole(shape):
         return pl.BlockSpec(shape, lambda j, me: (0,) * len(shape))
 
     def around(kind):
         def before(j, me):
-            return (jnp.maximum((j ^ me[2]) - 1, 0) ^ me[2], kind)
+            return (jnp.maximum(((base + j) ^ me[2]) - 1, 0) ^ me[2], kind)
 
         def following(j, me):
-            return ((jnp.minimum((j ^ me[2]) + 1, TP - 1) ^ me[2]) * (count // AFTER), kind)
+            slot = jnp.minimum(((base + j) ^ me[2]) + 1, TP - 1) ^ me[2]
+            return (slot * (count // AFTER), kind)
 
         return [
             pl.BlockSpec((count, WIDTH), before),
-            pl.BlockSpec((count, WIDTH), lambda j, me: (j, kind)),
+            pl.BlockSpec((count, WIDTH), lambda j, me: (base + j, kind)),
             pl.BlockSpec((AFTER, WIDTH), following),
         ]
 
@@ -833,32 +872,35 @@
     return rows, whole, fixed + [whole((count, 2 * WIDTH)), whole((AFTER, 2 * WIDTH))]
 
 
-def attend(joint, halos, segq, segk, heads):
+def attend(joint, halos, segq, segk, heads, base, slots):
     span = segk.shape[2]
     count = joint.shape[0] // TP
-    rows, whole, specs = block_specs(count)
+    rows, whole, specs = block_specs(count, base)
     return pl.pallas_call(
-        attend_kernel,
+        functools.partial(attend_kernel, base),
         grid_spec=pltpu.PrefetchScalarGridSpec(
             num_scalar_prefetch=1,
-            grid=(TP,),
+            grid=(slots,),
             in_specs=specs
             + [
                 rows(1),
-                pl.BlockSpec((1, 1, span), lambda j, me: (j, 0, 0)),
+                pl.BlockSpec((1, 1, span), lambda j, me: (base + j, 0, 0)),
                 rows(LANES),
             ],
-            out_specs=[rows(WIDTH), rows(LANES)],
+            out_specs=[
+                pl.BlockSpec((count, WIDTH), lambda j, me: (j, 0)),
+                pl.BlockSpec((count, LANES), lambda j, me: (j, 0)),
+            ],
         ),
         out_shape=[
-            jax.ShapeDtypeStruct((TP * count, WIDTH), BF16),
-            jax.ShapeDtypeStruct((TP * count, LANES), F32),
+            jax.ShapeDtypeStruct((slots * count, WIDTH), BF16),
+            jax.ShapeDtypeStruct((slots * count, LANES), F32),
         ],
         compiler_params=kernel_params(),
         cost_estimate=pl.CostEstimate(
-            flops=8 * TP * count * span * LANES * LOCAL_HEADS,
-            bytes_accessed=TP * count * WIDTH * 8,
-            transcendentals=TP * count * span * LOCAL_HEADS,
+            flops=8 * slots * count * span * LANES * LOCAL_HEADS,
+            bytes_accessed=slots * count * WIDTH * 8,
+            transcendentals=slots * count * span * LOCAL_HEADS,
         ),
         name="attend",
     )(here(), *[joint] * 7, *halos, segq, segk, heads)
@@ -967,7 +1009,9 @@
     return jnp.sum((places[:, None] >= bounds[None, :]).astype(jnp.int32), axis=-1)
 
 
-def layer_forward(stream, mod, w_joint, project_columns, open_reduce, masks, context, hold):
+def layer_forward(
+    stream, mod, w_joint, project_columns, open_reduce, masks, context, hold, split
+):
     head_tok, active, keeping = masks
     sides, living, segq, segk, slot_sides = context
     offset_one, stretch_one, gate_one, offset_two, stretch_two, gate_two = [
@@ -989,14 +1033,20 @@
     halos = halos_of(joint)
     w_project = project_matrix(after(project_columns, joint))
     halos = hold("halos", halos)
-    mixed, log_total = attend(joint, halos, segq, segk, head_tok)
-    mixed = hold("mixed", mixed)
-
-    def branch_parts(rows, slots):
-        return [dot(rows[j * count : (j + 1) * count], w_project).astype(BF16) for j in slots]
-
-    away = pair_sum(branch_parts(mixed, (2, 3)))
-    close = pair_sum(branch_parts(after(mixed, away), (0, 1)))
+    if split:
+        far_rows, total_far = attend(joint, halos, segq, segk, head_tok, 2, 2)
+        away = pair_sum(slot_products(dot, 0, far_rows, w_project, "branch_far", 2))
+        held = after(halos, away)
+        near_rows, total_near = attend(joint, held, segq, segk, head_tok, 0, 2)
+        near_rows = hold("mixed", near_rows)
+        close = pair_sum(slot_products(dot, 0, near_rows, w_project, "branch_near", 2))
+        mixed = jnp.concatenate([near_rows, far_rows], axis=0)
+        log_total = jnp.concatenate([total_near, total_far], axis=0)
+    else:
+        mixed, log_total = attend(joint, halos, segq, segk, head_tok, 0, TP)
+        mixed = hold("mixed", mixed)
+        away = pair_sum(slot_products(dot, 1, mixed, w_project, "branch_far"))
+        close = pair_sum(slot_products(dot, 0, after(mixed, away), w_project, "branch_near"))
     branch = after(hold("branch", far_sum(away)), close) + close
     middle = stream + gate_one * branch * living
     unit_two, _ = normed(middle)
@@ -1098,19 +1148,19 @@
     )
     d_joint = hold("d_joint", d_joint)
 
-    def normed_parts(rows, slots):
-        return [against_cols(rows[j * count : (j + 1) * count], w_joint).astype(BF16) for j in slots]
+    def normed_parts(rows, half):
+        return slot_products(against_cols, half, rows, w_joint, "d_normed")
 
     if last:
         g_joint = through_rows(jnp.concatenate(normed_one, axis=0), d_joint).astype(BF16)
         attention_pieces = split_attention(g_joint, g_project, fast)
-        away = pair_sum(normed_parts(after(d_joint, attention_pieces), (2, 3)))
+        away = pair_sum(normed_parts(after(d_joint, attention_pieces), 1))
     else:
-        away = pair_sum(normed_parts(d_joint, (2, 3)))
+        away = pair_sum(normed_parts(d_joint, 1))
         rows = after(jnp.concatenate(normed_one, axis=0), away)
         g_joint = through_rows(rows, d_joint).astype(BF16)
         attention_pieces = split_attention(g_joint, g_project, fast)
-    close = pair_sum(normed_parts(after(d_joint, away), (0, 1)))
+    close = pair_sum(normed_parts(after(d_joint, away), 0))
     d_normed_one = after(far_sum(away), close, attention_pieces) + close
     unit_one, scale_one = normed(stream)
     d_stream = d_middle + norm_back(d_normed_one * (1.0 + stretch_one), unit_one, scale_one)
@@ -1145,27 +1195,19 @@
     group, member = place()
     height = D // planes
 
-    pack = pack_attention(joint_weight[0], project_weight[0])
+    attention_packs = pack_attention(joint_weight, project_weight)
     if compact():
-        first = gather_planes(pack)
-        forward_first = gather_planes(
-            pack_forward(*after((expand_weight[0], reduce_weight[0]), pack), first)
-        )
+        first = gather_planes(attention_packs[0])
+        held = after((expand_weight[0], reduce_weight[0]), attention_packs[0])
+        forward_first = gather_planes(pack_forward(*held, first))
         for k in range(4):
             first.append(exchange(after(first[k], first[-1]) if k else first[0], TP))
         mod_events, normed_events = [first[1], first[4]], [forward_first[0], first[5]]
     else:
-        first = gather_slow(pack)
+        first = gather_slow(attention_packs[0])
         forward_first = gather_slow(pack_forward(expand_weight[0], reduce_weight[0]))
         mod_events, normed_events = [], []
-    opened = open_attention(first)
-    packs = []
-    held = opened
-    for l in range(1, LAYERS):
-        forward = pack_forward(*after((expand_weight[l], reduce_weight[l]), held))
-        attention = pack_attention(*after((joint_weight[l], project_weight[l]), forward))
-        packs.append((attention, forward))
-        held = attention
+    w_joint, project_columns = open_attention(first)
 
     stamps = jnp.zeros((planes, crops), jnp.int32)
     for step in range(planes):
@@ -1219,34 +1261,36 @@
 
     stream = hidden_in[0].astype(F32)
     records, weights = [], []
-    w_joint, project_columns = opened
-    forward_slow = [gather_slow(forward) for _, forward in packs]
+    forward_slow = []
     for l in range(LAYERS):
-        events, pieces, others = {}, [], []
+        events, pieces = {}, []
         if l + 1 < LAYERS:
-            attention, forward = packs[l]
-            events["halos"], events["mixed"] = [forward], [attention]
-            pieces = gather_planes(attention) if compact() else gather_slow(attention)
+            pack = after(attention_packs[l + 1], w_joint)
+            pieces = gather_planes(pack) if compact() else gather_slow(pack)
         if l == 0 and compact():
             first_others = [exchange(after(forward_first[0], w_joint), TP)]
             events["normed_one"] = normed_events
             events["far_one"] = [forward_first[1]]
-            events["halos"] = events["halos"] + [forward_first[2]]
-            events["mixed"] = events["mixed"] + [forward_first[3], first_others[0]]
-
-        def hold(name, value, *more, events=events, l=l, pieces=pieces, others=others):
+            events["halos"] = [forward_first[2]]
+            events["mixed"] = [forward_first[3], first_others[0]]
+
+        def hold(name, value, *more, events=events, l=l, pieces=pieces):
             if l == 0 and compact() and name == "halos":
                 first_others.extend(exchange(after(p, value), TP) for p in forward_first[1:])
                 events["branch"] = first_others[1:3]
-            if l + 1 < LAYERS and name == "branch" and compact():
-                events["branch"] = events.get("branch", []) + pieces[1:2]
-            if l + 1 < LAYERS and name == "far_two":
-                if compact():
-                    events["far_two"] = pieces[2:]
-                    for k in range(4):
-                        others.append(exchange(after(pieces[k], *others[-1:]), TP))
-                following.append(open_attention(pieces + others))
-                events["feedout"] = following
+            if l + 1 < LAYERS:
+                if name == "halos":
+                    held = after((expand_weight[l + 1], reduce_weight[l + 1]), value)
+                    forward = pack_forward(*held)
+                    forward_slow.append(gather_slow(forward))
+                    events["mixed"] = events.get("mixed", []) + [forward]
+                if name == "branch" and compact():
+                    events["branch"] = events.get("branch", []) + pieces[1:2]
+                    pieces.extend([exchange(piece, TP) for piece in pieces])
+                    events["far_two"] = pieces[2:6]
+                if name == "far_two":
+                    following.append(open_attention(pieces))
+                    events["feedout"] = following
             return after(value, *more, *events.get(name, []))
 
         def open_here(mine, l=l):
@@ -1256,7 +1300,7 @@
 
         following = []
         stream, record, used = layer_forward(
-            stream, mods[l], w_joint, project_columns, open_here, masks[l], context, hold
+            stream, mods[l], w_joint, project_columns, open_here, masks[l], context, hold, l > 0
         )
         records.append(record)
         weights.append(used)

time: 841 us -> 830 us (0.987)
  matrix products: 64.8 us -> 39.8 us
  starting transfers between devices: 144 us -> 165 us
  waiting for transfers between devices: 281 us -> 264 us
  Pallas kernels: 176 us -> 189 us
    ppermute x72, waiting for transfers between devices: 212 us -> 171 us  [exchange(): return lax.ppermute(value, SEQ, [(i, i ^ mask) for i in range(seq)])]
    ppermute x18, starting transfers between devices: 24.9 us -> 49.3 us  [from_plane(): lax.ppermute(value, 'dp', [(d, (d + back) % planes) for d in range(planes)])]
    ppermute x18, waiting for transfers between devices: 32.6 us -> 56.9 us  [from_plane(): lax.ppermute(value, 'dp', [(d, (d + back) % planes) for d in range(planes)])]
    pallas_call x2 -> x11, Pallas kernels: 22.3 us -> 39.1 us  [the longest x3 22.7 us: attend(): pl.pallas_call(functools.partial(attend_kernel, base), grid_spec=pltpu.Pr...]
    dot_general x10 -> x2, matrix products: 20.2 us -> 5.4 us  [against_cols(): lax.dot_general(left, right, (((1,), (1,)), ((), ())), preferred_element_...]
    dot_general x14 -> x6, matrix products: 10.7 us -> 1.31 us  [dot(): return jnp.dot(left, right, preferred_element_type=F32)]
    ppermute x6 -> x3, waiting for transfers between devices: 8.53 us -> 0.01 us  [deal_joint(): return [lax.ppermute(part, SEQ, pairs[r]) for r, part in enumerate(sent)]]
    unnamed x531 -> x501, local copies, waits for them, and re-layouts: 57.8 us -> 56 us
  transfers between devices with their start and end apart: 116 -> 113, of which waited for: 47 -> 46; matrix products, arithmetic and copies ran while one was open for 18% -> 14% of each run, Pallas kernels for 19% -> 21%
where the time goes in v4:
time: 830 us; the launch traced here: 818 us
  waiting for transfers between devices  264 us (32%)
  Pallas kernels  189 us (23%)
  starting transfers between devices  165 us (20%)
  local copies, waits for them, and re-layouts  73.4 us (9%)
  other arithmetic  69.3 us (8%)
  matrix products  39.8 us (5%)
  between operations  18 us (2%)
    ppermute x72, waiting for transfers between devices, exchange(): return lax.ppermute(value, SEQ, [(i, i ^ mask) for i in range(seq)])  171 us
    pallas_call x12, Pallas kernels, half_call(): pl.pallas_call(kernel, grid=(2,), in_specs=specs + [pl.BlockSpec(memory_s...  69.8 us
    ppermute x18, waiting for transfers between devices, from_plane(): lax.ppermute(value, 'dp', [(d, (d + back) % planes) for d in range(planes)])  56.9 us
    unnamed x501, local copies, waits for them, and re-layouts  56 us
    ppermute x72, starting transfers between devices, exchange(): return lax.ppermute(value, SEQ, [(i, i ^ mask) for i in range(seq)])  49.6 us
    ppermute x18, starting transfers between devices, from_plane(): lax.ppermute(value, 'dp', [(d, (d + back) % planes) for d in range(planes)])  49.3 us
    pallas_call x23, Pallas kernels, rearrange(): pl.pallas_call(body, in_specs=[pl.BlockSpec(memory_space=pltpu.SMEM)] + [...  49.3 us
    dot_general x8, matrix products, through_rows(): lax.dot_general(left, right, (((0,), (0,)), ((), ())), preferred_element_...  31.9 us
  transfers between devices with their start and end apart: 113, of which 46 were waited for; matrix products, arithmetic and copies ran while one was open for 14% of the time, Pallas kernels for 21%

profile of v4, /device:TPU:0, one launch (start us, length us, event | category | flops | bytes accessed | tf_op | source)
XLA Modules:
  0.0 818.3 jit_solution(9172837739771870627)
XLA Ops:
  7.2 5.1 collective-permute-start
  27.1 4.7 all-to-all-start
  42.0 9.4 %collective-permute-done.6.refs_1_ = bf16[144,1152]{1,0:T(8,128)(2,1)S(1)} collective-permute-done((bf16[144,1152]{1,0:T(8,128)(2,1)S(1)}, bf16[144,1152]{1,0:T(8,128)(2,1)S(1)}, u32[]{:S(2)}, u32[]{:S(2)}) %collective-permute-start.6) | collective-permute-done | bytes 331808 | tf_op jit(solution)/shard_map/ppermute | solution.py:81
  55.2 5.2 all-to-all-done
  74.7 6.2 all-to-all-done.1.got_ref
  87.3 9.2 %collective-permute-done.14.refs_7_ = bf16[144,1152]{1,0:T(8,128)(2,1)S(1)} collective-permute-done((bf16[144,1152]{1,0:T(8,128)(2,1)}, bf16[144,1152]{1,0:T(8,128)(2,1)S(1)}, u32[]{:S(2)}, u32[]{:S(2)}) %collective-permute-start.14) | collective-permute-done | bytes 331808 | tf_op jit(solution)/shard_map/ppermute | solution.py:69
  123.4 6.3 collective-permute-done.17.refs_6_.refs_7_
  141.7 11.9 %collective-permute-done.18.refs_2_ = bf16[288,1152]{1,0:T(8,128)(2,1)} collective-permute-done((bf16[288,1152]{1,0:T(8,128)(2,1)}, bf16[288,1152]{1,0:T(8,128)(2,1)}, u32[]{:S(2)}, u32[]{:S(2)}) %collective-permute-start.18) | collective-permute-done | bytes 663584 | tf_op jit(solution)/shard_map/ppermute | solution.py:81
  154.6 10.1 %attend.3 = (bf16[1024,384]{1,0:T(8,128)(2,1)S(1)}, f32[1024,128]{1,0:T(8,128)S(1)}) custom-call(s32[3]{0:T(128)S(1)} %pad_add_fusion.2.me_ref, bf16[1024,1152]{1,0:T(8,128)(2,1)S(1)} %joint_far.2.q_ref.refs_0_.refs_1_.refs_2_.refs_3_.refs_4_.refs_5_, bf16[1024,1152]{1,0:T(8,128)(2,1)S(1)} %joint_far.2.q_ref.refs_0_.refs_1_.refs_2_.refs_3_.refs_4_.refs_5_, ...), custom_call_target="tpu_custom_call" | custom-call | flops 2684354560 | bytes 3145728 | tf_op jit(solution)/shard_map/attend/pallas_call | solution.py:879
  183.6 11.6 %collective-permute-start.25 = (bf16[144,1152]{1,0:T(8,128)(2,1)S(1)}, bf16[144,1152]{1,0:T(8,128)(2,1)S(1)}, u32[]{:S(2)}, u32[]{:S(2)}) collective-permute-start(bf16[144,1152]{1,0:T(8,128)(2,1)S(1)} %copy-done.98), channel_id=1, source_target_pairs={{0,8},{8,16},{16,24},{24,0},{1,9},{9,17},{17,25},{25,1},{2,10},{10... | collective-permute-start | bytes 995336 | tf_op jit(solution)/shard_map/ppermute | solution.py:81
  200.1 5.9 collective-permute-done.25.refs_1_
  214.7 12.8 %collective-permute-start.31 = (bf16[144,1152]{1,0:T(8,128)(2,1)S(1)}, bf16[144,1152]{1,0:T(8,128)(2,1)}, u32[]{:S(2)}, u32[]{:S(2)}) collective-permute-start(bf16[144,1152]{1,0:T(8,128)(2,1)S(1)} %copy-done.98), channel_id=1, source_target_pairs={{0,24},{8,0},{16,8},{24,16},{1,25},{9,1},{17,9},{25,17},{2,26},{10... | collective-permute-start | bytes 995336 | tf_op jit(solution)/shard_map/ppermute | solution.py:81
  233.8 5.3 open_forward.2
  239.1 8.7 %forward_near.2 = (bf16[1024,1152]{1,0:T(8,128)(2,1)S(1)}, bf16[1024,1152]{1,0:T(8,128)(2,1)}, bf16[256,1152]{1,0:T(8,128)(2,1)S(1)}, bf16[256,1152]{1,0:T(8,128)(2,1)}) custom-call(bf16[256,1152]{1,0:T(8,128)(2,1)S(1)} %add_convert_fusion.3.a_ref, bf16[256,1152]{1,0:T(8,128)(2,1)S(1)} %copy-done.78, bf16[1152,1152]{1,0:T(8,128)(2,1)} %get-tuple-element.189.refs_0_, ...), custom_call_target="tpu_custom_call" | custom-call | flops 2717908992 | bytes 5308416 | tf_op jit(solution)/shard_map/forward_near/pallas_call | solution.py:642
  253.2 8.4 %forward_far.2 = (bf16[1024,1152]{1,0:T(8,128)(2,1)S(1)}, bf16[1024,1152]{1,0:T(8,128)(2,1)}, bf16[256,1152]{1,0:T(8,128)(2,1)S(1)}, bf16[256,1152]{1,0:T(8,128)(2,1)S(1)}) custom-call(bf16[256,1152]{1,0:T(8,128)(2,1)S(1)} %collective-permute-done.27.a_ref, ...), custom_call_target="tpu_custom_call", output_to_operand_aliasing={{0}: (6, {}), {1}: (7, {})} | custom-call | flops 2717908992 | bytes 5308416 | tf_op jit(solution)/shard_map/forward_far/pallas_call | solution.py:642
  270.0 9.8 %collective-permute-done.37.refs_6_ = bf16[144,1152]{1,0:T(8,128)(2,1)S(1)} collective-permute-done((bf16[144,1152]{1,0:T(8,128)(2,1)}, bf16[144,1152]{1,0:T(8,128)(2,1)S(1)}, u32[]{:S(2)}, u32[]{:S(2)}) %collective-permute-start.37) | collective-permute-done | bytes 331808 | tf_op jit(solution)/shard_map/ppermute | solution.py:69
  279.9 6.9 collective-permute-done.38.refs_7_
  301.2 11.7 %collective-permute-done.40.a_ref = bf16[256,1152]{1,0:T(8,128)(2,1)S(1)} collective-permute-done((bf16[256,1152]{1,0:T(8,128)(2,1)S(1)}, bf16[256,1152]{1,0:T(8,128)(2,1)S(1)}, u32[]{:S(2)}, u32[]{:S(2)}) %collective-permute-start.40) | collective-permute-done | bytes 589856 | tf_op jit(solution)/shard_map/ppermute | solution.py:69
  323.1 8.9 %collective-permute-done.43.refs_6_.refs_7_ = bf16[256,768]{1,0:T(8,128)(2,1)} collective-permute-done((bf16[256,768]{1,0:T(8,128)(2,1)}, bf16[256,768]{1,0:T(8,128)(2,1)}, u32[]{:S(2)}, u32[]{:S(2)}) %collective-permute-start.43) | collective-permute-done | bytes 393248 | tf_op jit(solution)/shard_map/ppermute | solution.py:69
  331.9 6.3 attend.4
  342.7 6.3 attend.5
  352.0 12.8 %collective-permute-done.45 = bf16[256,1152]{1,0:T(8,128)(2,1)S(1)} collective-permute-done((bf16[256,1152]{1,0:T(8,128)(2,1)S(1)}, bf16[256,1152]{1,0:T(8,128)(2,1)S(1)}, u32[]{:S(2)}, u32[]{:S(2)}) %collective-permute-start.45) | collective-permute-done | bytes 589856 | tf_op jit(solution)/shard_map/ppermute | solution.py:69
  376.8 8.7 %forward_near.3 = (bf16[1024,1152]{1,0:T(8,128)(2,1)S(1)}, bf16[1024,1152]{1,0:T(8,128)(2,1)}, bf16[256,1152]{1,0:T(8,128)(2,1)S(1)}, bf16[256,1152]{1,0:T(8,128)(2,1)S(1)}) custom-call(bf16[256,1152]{1,0:T(8,128)(2,1)S(1)} %get-tuple-element.477.a_ref, bf16[256,1152]{1,0:T(8,128)(2,1)S(1)} %collective-permute-done.48.b_ref, bf16[1152,1152]{1,0:T(8,128)(2,1)} %copy-done.7, ...), custom_call_target="tpu_custom_call" | custom-call | flops 2717908992 | bytes 5308416 | tf_op jit(solution)/shard_map/forward_near/pallas_call | solution.py:642
  387.5 8.4 %forward_far.3 = (bf16[1024,1152]{1,0:T(8,128)(2,1)S(1)}, bf16[1024,1152]{1,0:T(8,128)(2,1)}, bf16[256,1152]{1,0:T(8,128)(2,1)S(1)}, bf16[256,1152]{1,0:T(8,128)(2,1)S(1)}) custom-call(bf16[256,1152]{1,0:T(8,128)(2,1)S(1)} %collective-permute-done.47.a_ref, ...), custom_call_target="tpu_custom_call", output_to_operand_aliasing={{0}: (6, {}), {1}: (7, {})} | custom-call | flops 2717908992 | bytes 5308416 | tf_op jit(solution)/shard_map/forward_far/pallas_call | solution.py:642
  395.9 6.8 backward_near.2
  404.9 7.2 backward_far.2
  416.1 13.7 %collective-permute-done.51 = bf16[256,1152]{1,0:T(8,128)(2,1)S(1)} collective-permute-done((bf16[256,1152]{1,0:T(8,128)(2,1)S(1)}, bf16[256,1152]{1,0:T(8,128)(2,1)S(1)}, u32[]{:S(2)}, u32[]{:S(2)}) %collective-permute-start.51) | collective-permute-done | bytes 589856 | tf_op jit(solution)/shard_map/ppermute | solution.py:69
  433.2 8.6 %collective-permute-done.57 = bf16[256,1152]{1,0:T(8,128)(2,1)S(1)} collective-permute-done((bf16[256,1152]{1,0:T(8,128)(2,1)S(1)}, bf16[256,1152]{1,0:T(8,128)(2,1)S(1)}, u32[]{:S(2)}, u32[]{:S(2)}) %collective-permute-start.57) | collective-permute-done | bytes 589856 | tf_op jit(solution)/shard_map/ppermute | solution.py:69
  457.1 6.8 collective-permute-done.60
  469.3 15.9 %attend_back.2 = (bf16[1024,1152]{1,0:T(8,128)(2,1)}, bf16[256,768]{1,0:T(8,128)(2,1)S(1)}, bf16[128,768]{1,0:T(8,128)(2,1)S(1)}) custom-call(s32[3]{0:T(128)S(1)} %pad_add_fusion.2.me_ref, bf16[1024,1152]{1,0:T(8,128)(2,1)} %copy-done, bf16[1024,1152]{1,0:T(8,128)(2,1)} %copy-done, bf16[1024,1152]{1,0:T(8,128)(2,1)} %copy-done, bf16[1024,1152]{1,0:T(8,128)(2,1)} %copy-done, ...), custom_call_target="tpu_custom_call" | custom-call | flops 6710886400 | bytes 7864320 | tf_op jit(solution)/shard_map/attend_back/pallas_call | solution.py:914
  486.6 13.0 %collective-permute-done.62 = bf16[256,768]{1,0:T(8,128)(2,1)} collective-permute-done((bf16[256,768]{1,0:T(8,128)(2,1)}, bf16[256,768]{1,0:T(8,128)(2,1)}, u32[]{:S(2)}, u32[]{:S(2)}) %collective-permute-start.62) | collective-permute-done | bytes 393248 | tf_op jit(solution)/shard_map/ppermute | solution.py:69
  536.1 6.8 collective-permute-done.64
  557.1 6.8 backward_near.3
  567.2 6.7 backward_far.3
  580.4 4.8 convolution_convert_fusion.2.reduce_ref
  585.2 9.7 %collective-permute-done.71 = bf16[256,1152]{1,0:T(8,128)(2,1)S(1)} collective-permute-done((bf16[256,1152]{1,0:T(8,128)(2,1)S(1)}, bf16[256,1152]{1,0:T(8,128)(2,1)S(1)}, u32[]{:S(2)}, u32[]{:S(2)}) %collective-permute-start.71) | collective-permute-done | bytes 589856 | tf_op jit(solution)/shard_map/ppermute | solution.py:69
  600.3 12.4 %reduce-scatter.3.cloned.1.call-done = bf16[1,288,1152]{2,1,0:T(8,128)(2,1)} async-done(((bf16[8,288,1152]{2,1,0:T(8,128)(2,1)}), bf16[1,288,1152]{2,1,0:T(8,128)(2,1)}) %reduce-scatter.3.cloned.1.call-update) | async-done | bytes 663568 | tf_op jit(solution)/shard_map/reduce_scatter | solution.py:588
  627.8 5.9 convolution_convert_fusion.1.expand_ref
  639.5 10.1 %collective-permute-done.76 = bf16[256,1152]{1,0:T(8,128)(2,1)} collective-permute-done((bf16[256,1152]{1,0:T(8,128)(2,1)}, bf16[256,1152]{1,0:T(8,128)(2,1)}, u32[]{:S(2)}, u32[]{:S(2)}) %collective-permute-start.76) | collective-permute-done | bytes 589856 | tf_op jit(solution)/shard_map/ppermute | solution.py:69
  649.6 7.0 multiply_reduce_fusion.1
  660.7 15.4 %attend_back.3 = (bf16[1024,1152]{1,0:T(8,128)(2,1)}, bf16[256,768]{1,0:T(8,128)(2,1)S(1)}, bf16[128,768]{1,0:T(8,128)(2,1)S(1)}) custom-call(s32[3]{0:T(128)S(1)} %pad_add_fusion.2.me_ref, bf16[1024,1152]{1,0:T(8,128)(2,1)} %copy-done.1, bf16[1024,1152]{1,0:T(8,128)(2,1)} %copy-done.1, bf16[1024,1152]{1,0:T(8,128)(2,1)} %copy-done.1, ...), custom_call_target="tpu_custom_call" | custom-call | flops 6710886400 | bytes 7864320 | tf_op jit(solution)/shard_map/attend_back/pallas_call | solution.py:914
  686.8 5.9 collective-permute-done.82
  694.7 6.5 convolution_convert_fusion.joint_ref
  708.2 8.6 %collective-permute-done.90 = bf16[144,1152]{1,0:T(8,128)(2,1)S(1)} collective-permute-done((bf16[144,1152]{1,0:T(8,128)(2,1)S(1)}, bf16[144,1152]{1,0:T(8,128)(2,1)S(1)}, u32[]{:S(2)}, u32[]{:S(2)}) %collective-permute-start.90) | collective-permute-done | bytes 331808 | tf_op jit(solution)/shard_map/ppermute | solution.py:69
  727.7 5.7 collective-permute-done.91
  736.2 14.7 %collective-permute-done.92 = bf16[144,1152]{1,0:T(8,128)(2,1)S(1)} collective-permute-done((bf16[144,1152]{1,0:T(8,128)(2,1)S(1)}, bf16[144,1152]{1,0:T(8,128)(2,1)S(1)}, u32[]{:S(2)}, u32[]{:S(2)}) %collective-permute-start.92) | collective-permute-done | bytes 331808 | tf_op jit(solution)/shard_map/ppermute | solution.py:81
  761.6 7.5 all-to-all-start.8
  794.5 10.2 %all-to-all-done.9.got_ref = bf16[8,144,432]{2,1,0:T(8,128)(2,1)S(1)} async-done(((bf16[8,144,432]{2,1,0:T(8,128)(2,1)}), bf16[8,144,432]{2,1,0:T(8,128)(2,1)S(1)}, u32[]{:S(2)}, u32[]{:S(2)}) %all-to-all-start.9) | async-done | bytes 995360 | tf_op jit(solution)/shard_map/all_to_all | solution.py:608
  (937 shorter events, 382.8 us)
Async XLA Ops:
  27.1 33.3 %all-to-all-start = ((f32[32,2,2,864]{3,2,1,0:T(2,128)}), f32[32,2,2,864]{3,2,1,0:T(2,128)}, u32[]{:S(2)}, u32[]{:S(2)}) async-start(f32[32,2,2,864]{3,2,1,0:T(2,128)} %copy.128), calls=%async_computation | async-start | bytes 917504 | tf_op jit(solution)/shard_map/all_to_all | solution.py:1224
  39.5 27.2 %collective-permute-start.8 = (bf16[144,1152]{1,0:T(8,128)(2,1)S(1)}, bf16[144,1152]{1,0:T(8,128)(2,1)}, u32[]{:S(2)}, u32[]{:S(2)}) collective-permute-start(bf16[144,1152]{1,0:T(8,128)(2,1)S(1)} %get-tuple-element.157.refs_0_), channel_id=1, source_target_pairs={{0,16},{8,24},{16,0},{24,8},{1,17},{9,25},{17,1},{25,9},{2,18},{10... | collective-permute-start | bytes 995336 | tf_op jit(solution)/shard_map/ppermute | solution.py:81
  60.4 20.4 %all-to-all-start.1 = ((bf16[8,144,432]{2,1,0:T(8,128)(2,1)}), bf16[8,144,432]{2,1,0:T(8,128)(2,1)S(1)}, u32[]{:S(2)}, u32[]{:S(2)}) async-start(bf16[8,144,432]{2,1,0:T(8,128)(2,1)} %pack_forward.2), calls=%async_computation.1 | async-start | bytes 2359296 | tf_op jit(solution)/shard_map/all_to_all | solution.py:514
  66.8 20.2 %collective-permute-start.13 = (bf16[144,1152]{1,0:T(8,128)(2,1)}, bf16[144,1152]{1,0:T(8,128)(2,1)}, u32[]{:S(2)}, u32[]{:S(2)}) collective-permute-start(bf16[144,1152]{1,0:T(8,128)(2,1)} %collective-permute-done.8.refs_2_), channel_id=1, source_target_pairs={{0,4},{1,5},{2,6},{3,7},{4,0},{5,1},{6,2},{7,3},{8,12},{9,13},{10,... | collective-permute-start | bytes 995336 | tf_op jit(solution)/shard_map/ppermute | solution.py:69
  81.8 19.9 %collective-permute-start.12 = (bf16[256,1152]{1,0:T(8,128)(2,1)S(1)}, bf16[256,1152]{1,0:T(8,128)(2,1)S(1)}, u32[]{:S(2)}, u32[]{:S(2)}) collective-permute-start(bf16[256,1152]{1,0:T(8,128)(2,1)S(1)} %fusion.16.a_ref), channel_id=1, source_target_pairs={{0,1},{1,0},{2,3},{3,2},{4,5},{5,4},{6,7},{7,6},{8,9},{9,8},{10,11... | collective-permute-start | bytes 1769480 | tf_op jit(solution)/shard_map/ppermute | solution.py:69
  81.9 21.9 %collective-permute-start.15 = (bf16[288,1152]{1,0:T(8,128)(2,1)S(1)}, bf16[288,1152]{1,0:T(8,128)(2,1)S(1)}, u32[]{:S(2)}, u32[]{:S(2)}) collective-permute-start(bf16[288,1152]{1,0:T(8,128)(2,1)S(1)} %unpack_forward.2.refs_0_), channel_id=1, source_target_pairs={{0,8},{8,16},{16,24},{24,0},{1,9},{9,17},{17,25},{25,1},{2,10},{10... | collective-permute-start | bytes 1990664 | tf_op jit(solution)/shard_map/ppermute | solution.py:81
  83.6 20.2 %collective-permute-start.11 = (bf16[256,1152]{1,0:T(8,128)(2,1)S(1)}, bf16[256,1152]{1,0:T(8,128)(2,1)S(1)}, u32[]{:S(2)}, u32[]{:S(2)}) collective-permute-start(bf16[256,1152]{1,0:T(8,128)(2,1)S(1)} %fusion.16.a_ref), channel_id=1, source_target_pairs={{0,2},{1,3},{2,0},{3,1},{4,6},{5,7},{6,4},{7,5},{8,10},{9,11},{10,... | collective-permute-start | bytes 1769480 | tf_op jit(solution)/shard_map/ppermute | solution.py:69
  114.4 19.0 %all-to-all-start.3 = ((bf16[4,288,288]{2,1,0:T(8,128)(2,1)}), bf16[4,288,288]{2,1,0:T(8,128)(2,1)S(1)}, u32[]{:S(2)}, u32[]{:S(2)}) async-start(bf16[4,288,288]{2,1,0:T(8,128)(2,1)} %copy-done.56), calls=%async_computation.3 | async-start | bytes 1769472 | tf_op jit(solution)/shard_map/all_to_all | solution.py:539
  119.4 34.1 %collective-permute-start.18 = (bf16[288,1152]{1,0:T(8,128)(2,1)}, bf16[288,1152]{1,0:T(8,128)(2,1)}, u32[]{:S(2)}, u32[]{:S(2)}) collective-permute-start(bf16[288,1152]{1,0:T(8,128)(2,1)} %copy-done.21), channel_id=1, source_target_pairs={{0,16},{8,24},{16,0},{24,8},{1,17},{9,25},{17,1},{25,9},{2,18},{10... | collective-permute-start | bytes 1990664 | tf_op jit(solution)/shard_map/ppermute | solution.py:81
  134.4 32.9 %all-to-all-start.2 = ((bf16[8,144,432]{2,1,0:T(8,128)(2,1)}), bf16[8,144,432]{2,1,0:T(8,128)(2,1)}, u32[]{:S(2)}, u32[]{:S(2)}) async-start(bf16[8,144,432]{2,1,0:T(8,128)(2,1)} %pack_forward.3), calls=%async_computation.2 | async-start | bytes 2359296 | tf_op jit(solution)/shard_map/all_to_all | solution.py:514
  138.6 231.6 %all-gather.3.cloned.1.call-start = ((), (), s32[]{:S(2)}) async-start(), calls=%async_computation.14 | async-start | bytes 5971968 | tf_op jit(solution)/shard_map/all_gather | solution.py:523
  139.0 31.1 %collective-permute-start.19 = (bf16[288,1152]{1,0:T(8,128)(2,1)}, bf16[288,1152]{1,0:T(8,128)(2,1)}, u32[]{:S(2)}, u32[]{:S(2)}) collective-permute-start(bf16[288,1152]{1,0:T(8,128)(2,1)} %copy-done.21), channel_id=1, source_target_pairs={{0,24},{8,0},{16,8},{24,16},{1,25},{9,1},{17,9},{25,17},{2,26},{10... | collective-permute-start | bytes 1990664 | tf_op jit(solution)/shard_map/ppermute | solution.py:81
  139.3 30.8 %collective-permute-start.20 = (bf16[288,1152]{1,0:T(8,128)(2,1)}, bf16[288,1152]{1,0:T(8,128)(2,1)}, u32[]{:S(2)}, u32[]{:S(2)}) collective-permute-start(bf16[288,1152]{1,0:T(8,128)(2,1)} %copy-done.21), channel_id=1, source_target_pairs={{0,4},{1,5},{2,6},{3,7},{4,0},{5,1},{6,2},{7,3},{8,12},{9,13},{10,... | collective-permute-start | bytes 1990664 | tf_op jit(solution)/shard_map/ppermute | solution.py:69
  174.4 31.6 %collective-permute-start.24 = (bf16[288,1152]{1,0:T(8,128)(2,1)}, bf16[288,1152]{1,0:T(8,128)(2,1)}, u32[]{:S(2)}, u32[]{:S(2)}) collective-permute-start(bf16[288,1152]{1,0:T(8,128)(2,1)} %collective-permute-done.18.refs_2_), channel_id=1, source_target_pairs={{0,4},{1,5},{2,6},{3,7},{4,0},{5,1},{6,2},{7,3},{8,12},{9,13},{10,... | collective-permute-start | bytes 1990664 | tf_op jit(solution)/shard_map/ppermute | solution.py:69
  175.6 31.1 %collective-permute-start.23 = (bf16[288,1152]{1,0:T(8,128)(2,1)S(1)}, bf16[288,1152]{1,0:T(8,128)(2,1)}, u32[]{:S(2)}, u32[]{:S(2)}) collective-permute-start(bf16[288,1152]{1,0:T(8,128)(2,1)S(1)} %copy-done.67), channel_id=1, source_target_pairs={{0,4},{1,5},{2,6},{3,7},{4,0},{5,1},{6,2},{7,3},{8,12},{9,13},{10,... | collective-permute-start | bytes 1990664 | tf_op jit(solution)/shard_map/ppermute | solution.py:69
  179.5 27.2 %collective-permute-start.26 = (bf16[256,1152]{1,0:T(8,128)(2,1)}, bf16[256,1152]{1,0:T(8,128)(2,1)}, u32[]{:S(2)}, u32[]{:S(2)}) collective-permute-start(bf16[256,1152]{1,0:T(8,128)(2,1)} %get-tuple-element.186), channel_id=1, source_target_pairs={{0,1},{1,0},{2,3},{3,2},{4,5},{5,4},{6,7},{7,6},{8,9},{9,8},{10,11... | collective-permute-start | bytes 1769480 | tf_op jit(solution)/shard_map/ppermute | solution.py:69
  183.6 22.3 %collective-permute-start.25 = (bf16[144,1152]{1,0:T(8,128)(2,1)S(1)}, bf16[144,1152]{1,0:T(8,128)(2,1)S(1)}, u32[]{:S(2)}, u32[]{:S(2)}) collective-permute-start(bf16[144,1152]{1,0:T(8,128)(2,1)S(1)} %copy-done.98), channel_id=1, source_target_pairs={{0,8},{8,16},{16,24},{24,0},{1,9},{9,17},{17,25},{25,1},{2,10},{10... | collective-permute-start | bytes 995336 | tf_op jit(solution)/shard_map/ppermute | solution.py:81
  197.6 29.9 %collective-permute-start.29 = (bf16[288,1152]{1,0:T(8,128)(2,1)}, bf16[288,1152]{1,0:T(8,128)(2,1)S(1)}, u32[]{:S(2)}, u32[]{:S(2)}) collective-permute-start(bf16[288,1152]{1,0:T(8,128)(2,1)} %collective-permute-done.19.refs_3_), channel_id=1, source_target_pairs={{0,4},{1,5},{2,6},{3,7},{4,0},{5,1},{6,2},{7,3},{8,12},{9,13},{10,... | collective-permute-start | bytes 1990664 | tf_op jit(solution)/shard_map/ppermute | solution.py:69
  209.9 19.8 %collective-permute-start.28 = (bf16[256,1152]{1,0:T(8,128)(2,1)S(1)}, bf16[256,1152]{1,0:T(8,128)(2,1)S(1)}, u32[]{:S(2)}, u32[]{:S(2)}) collective-permute-start(bf16[256,1152]{1,0:T(8,128)(2,1)S(1)} %add_convert_fusion.3.a_ref), channel_id=1, source_target_pairs={{0,1},{1,0},{2,3},{3,2},{4,5},{5,4},{6,7},{7,6},{8,9},{9,8},{10,11... | collective-permute-start | bytes 1769480 | tf_op jit(solution)/shard_map/ppermute | solution.py:69
  210.8 38.4 %collective-permute-start.27 = (bf16[256,1152]{1,0:T(8,128)(2,1)S(1)}, bf16[256,1152]{1,0:T(8,128)(2,1)S(1)}, u32[]{:S(2)}, u32[]{:S(2)}) collective-permute-start(bf16[256,1152]{1,0:T(8,128)(2,1)S(1)} %add_convert_fusion.3.a_ref), channel_id=1, source_target_pairs={{0,2},{1,3},{2,0},{3,1},{4,6},{5,7},{6,4},{7,5},{8,10},{9,11},{10,... | collective-permute-start | bytes 1769480 | tf_op jit(solution)/shard_map/ppermute | solution.py:69
  212.5 36.7 %collective-permute-start.30 = (bf16[144,1152]{1,0:T(8,128)(2,1)S(1)}, bf16[144,1152]{1,0:T(8,128)(2,1)}, u32[]{:S(2)}, u32[]{:S(2)}) collective-permute-start(bf16[144,1152]{1,0:T(8,128)(2,1)S(1)} %copy-done.98), channel_id=1, source_target_pairs={{0,16},{8,24},{16,0},{24,8},{1,17},{9,25},{17,1},{25,9},{2,18},{10... | collective-permute-start | bytes 995336 | tf_op jit(solution)/shard_map/ppermute | solution.py:81
  214.7 34.5 %collective-permute-start.31 = (bf16[144,1152]{1,0:T(8,128)(2,1)S(1)}, bf16[144,1152]{1,0:T(8,128)(2,1)}, u32[]{:S(2)}, u32[]{:S(2)}) collective-permute-start(bf16[144,1152]{1,0:T(8,128)(2,1)S(1)} %copy-done.98), channel_id=1, source_target_pairs={{0,24},{8,0},{16,8},{24,16},{1,25},{9,1},{17,9},{25,17},{2,26},{10... | collective-permute-start | bytes 995336 | tf_op jit(solution)/shard_map/ppermute | solution.py:81
  228.3 20.9 %collective-permute-start.32 = (bf16[144,1152]{1,0:T(8,128)(2,1)S(1)}, bf16[144,1152]{1,0:T(8,128)(2,1)}, u32[]{:S(2)}, u32[]{:S(2)}) collective-permute-start(bf16[144,1152]{1,0:T(8,128)(2,1)S(1)} %copy-done.98), channel_id=1, source_target_pairs={{0,4},{1,5},{2,6},{3,7},{4,0},{5,1},{6,2},{7,3},{8,12},{9,13},{10,... | collective-permute-start | bytes 995336 | tf_op jit(solution)/shard_map/ppermute | solution.py:69
  230.6 18.6 %collective-permute-start.33 = (bf16[144,1152]{1,0:T(8,128)(2,1)}, bf16[144,1152]{1,0:T(8,128)(2,1)}, u32[]{:S(2)}, u32[]{:S(2)}) collective-permute-start(bf16[144,1152]{1,0:T(8,128)(2,1)} %copy-done.99), channel_id=1, source_target_pairs={{0,4},{1,5},{2,6},{3,7},{4,0},{5,1},{6,2},{7,3},{8,12},{9,13},{10,... | collective-permute-start | bytes 995336 | tf_op jit(solution)/shard_map/ppermute | solution.py:69
  266.1 24.9 %collective-permute-start.36 = (bf16[256,1152]{1,0:T(8,128)(2,1)}, bf16[256,1152]{1,0:T(8,128)(2,1)}, u32[]{:S(2)}, u32[]{:S(2)}) collective-permute-start(bf16[256,1152]{1,0:T(8,128)(2,1)} %fusion.73), channel_id=1, source_target_pairs={{0,2},{1,3},{2,0},{3,1},{4,6},{5,7},{6,4},{7,5},{8,10},{9,11},{10,... | collective-permute-start | bytes 1769480 | tf_op jit(solution)/shard_map/ppermute | solution.py:69
  266.5 26.2 %collective-permute-start.39 = (bf16[256,1152]{1,0:T(8,128)(2,1)}, bf16[256,1152]{1,0:T(8,128)(2,1)}, u32[]{:S(2)}, u32[]{:S(2)}) collective-permute-start(bf16[256,1152]{1,0:T(8,128)(2,1)} %get-tuple-element.200), channel_id=1, source_target_pairs={{0,1},{1,0},{2,3},{3,2},{4,5},{5,4},{6,7},{7,6},{8,9},{9,8},{10,11... | collective-permute-start | bytes 1769480 | tf_op jit(solution)/shard_map/ppermute | solution.py:69
  267.8 19.0 %collective-permute-start.38 = (bf16[144,1152]{1,0:T(8,128)(2,1)}, bf16[144,1152]{1,0:T(8,128)(2,1)S(1)}, u32[]{:S(2)}, u32[]{:S(2)}) collective-permute-start(bf16[144,1152]{1,0:T(8,128)(2,1)} %collective-permute-done.31.refs_3_), channel_id=1, source_target_pairs={{0,4},{1,5},{2,6},{3,7},{4,0},{5,1},{6,2},{7,3},{8,12},{9,13},{10,... | collective-permute-start | bytes 995336 | tf_op jit(solution)/shard_map/ppermute | solution.py:69
  318.2 21.6 %all-to-all-start.4 = ((bf16[4,288,288]{2,1,0:T(8,128)(2,1)}), bf16[4,288,288]{2,1,0:T(8,128)(2,1)}, u32[]{:S(2)}, u32[]{:S(2)}) async-start(bf16[4,288,288]{2,1,0:T(8,128)(2,1)} %copy-done.57), calls=%async_computation.4 | async-start | bytes 1769472 | tf_op jit(solution)/shard_map/all_to_all | solution.py:539
  322.4 290.3 %reduce-scatter.3.cloned.1.call-start = ((), (), s32[]{:S(2)}) async-start(), calls=%async_computation.12 | async-start | bytes 5971968 | tf_op jit(solution)/shard_map/reduce_scatter | solution.py:588
  404.4 37.5 %collective-permute-start.52 = (bf16[256,1152]{1,0:T(8,128)(2,1)S(1)}, bf16[256,1152]{1,0:T(8,128)(2,1)}, u32[]{:S(2)}, u32[]{:S(2)}) collective-permute-start(bf16[256,1152]{1,0:T(8,128)(2,1)S(1)} %get-tuple-element.223), channel_id=1, source_target_pairs={{0,1},{1,0},{2,3},{3,2},{4,5},{5,4},{6,7},{7,6},{8,9},{9,8},{10,11... | collective-permute-start | bytes 1769480 | tf_op jit(solution)/shard_map/ppermute | solution.py:69
  404.6 37.4 %collective-permute-start.58 = (bf16[256,1152]{1,0:T(8,128)(2,1)S(1)}, bf16[256,1152]{1,0:T(8,128)(2,1)}, u32[]{:S(2)}, u32[]{:S(2)}) collective-permute-start(bf16[256,1152]{1,0:T(8,128)(2,1)S(1)} %get-tuple-element.234), channel_id=1, source_target_pairs={{0,1},{1,0},{2,3},{3,2},{4,5},{5,4},{6,7},{7,6},{8,9},{9,8},{10,11... | collective-permute-start | bytes 1769480 | tf_op jit(solution)/shard_map/ppermute | solution.py:69
  414.5 27.3 %collective-permute-start.57 = (bf16[256,1152]{1,0:T(8,128)(2,1)S(1)}, bf16[256,1152]{1,0:T(8,128)(2,1)S(1)}, u32[]{:S(2)}, u32[]{:S(2)}) collective-permute-start(bf16[256,1152]{1,0:T(8,128)(2,1)S(1)} %fusion.77), channel_id=1, source_target_pairs={{0,2},{1,3},{2,0},{3,1},{4,6},{5,7},{6,4},{7,5},{8,10},{9,11},{10,... | collective-permute-start | bytes 1769480 | tf_op jit(solution)/shard_map/ppermute | solution.py:69
  522.3 21.8 %collective-permute-start.65 = (bf16[256,1152]{1,0:T(8,128)(2,1)}, bf16[256,1152]{1,0:T(8,128)(2,1)}, u32[]{:S(2)}, u32[]{:S(2)}) collective-permute-start(bf16[256,1152]{1,0:T(8,128)(2,1)} %get-tuple-element.248), channel_id=1, source_target_pairs={{0,1},{1,0},{2,3},{3,2},{4,5},{5,4},{6,7},{7,6},{8,9},{9,8},{10,11... | collective-permute-start | bytes 1769480 | tf_op jit(solution)/shard_map/ppermute | solution.py:69
  534.9 30.3 %collective-permute-start.72 = (bf16[144,1152]{1,0:T(8,128)(2,1)S(1)}, bf16[144,1152]{1,0:T(8,128)(2,1)S(1)}, u32[]{:S(2)}, u32[]{:S(2)}) collective-permute-start(bf16[144,1152]{1,0:T(8,128)(2,1)S(1)} %get-tuple-element.255), channel_id=1, source_target_pairs={{0,4},{1,5},{2,6},{3,7},{4,0},{5,1},{6,2},{7,3},{8,12},{9,13},{10,... | collective-permute-start | bytes 995336 | tf_op jit(solution)/shard_map/ppermute | solution.py:69
  555.0 19.2 %collective-permute-start.77 = (bf16[144,1152]{1,0:T(8,128)(2,1)S(1)}, bf16[144,1152]{1,0:T(8,128)(2,1)S(1)}, u32[]{:S(2)}, u32[]{:S(2)}) collective-permute-start(bf16[144,1152]{1,0:T(8,128)(2,1)S(1)} %get-tuple-element.256), channel_id=1, source_target_pairs={{0,4},{1,5},{2,6},{3,7},{4,0},{5,1},{6,2},{7,3},{8,12},{9,13},{10,... | collective-permute-start | bytes 995336 | tf_op jit(solution)/shard_map/ppermute | solution.py:69
  555.5 64.0 %collective-permute-start.80 = (bf16[144,1152]{1,0:T(8,128)(2,1)}, bf16[144,1152]{1,0:T(8,128)(2,1)S(1)}, u32[]{:S(2)}, u32[]{:S(2)}) collective-permute-start(bf16[144,1152]{1,0:T(8,128)(2,1)} %get-tuple-element.257), channel_id=1, source_target_pairs={{0,4},{1,5},{2,6},{3,7},{4,0},{5,1},{6,2},{7,3},{8,12},{9,13},{10,... | collective-permute-start | bytes 995336 | tf_op jit(solution)/shard_map/ppermute | solution.py:69
  578.2 41.3 %collective-permute-start.81 = (bf16[144,1152]{1,0:T(8,128)(2,1)}, bf16[144,1152]{1,0:T(8,128)(2,1)}, u32[]{:S(2)}, u32[]{:S(2)}) collective-permute-start(bf16[144,1152]{1,0:T(8,128)(2,1)} %add_convert_fusion.11), channel_id=1, source_target_pairs={{0,8},{8,16},{16,24},{24,0},{1,9},{9,17},{17,25},{25,1},{2,10},{10... | collective-permute-start | bytes 995336 | tf_op jit(solution)/shard_map/ppermute | solution.py:81
  597.9 29.9 %collective-permute-start.75 = (bf16[256,1152]{1,0:T(8,128)(2,1)}, bf16[256,1152]{1,0:T(8,128)(2,1)S(1)}, u32[]{:S(2)}, u32[]{:S(2)}) collective-permute-start(bf16[256,1152]{1,0:T(8,128)(2,1)} %get-tuple-element.420), channel_id=1, source_target_pairs={{0,1},{1,0},{2,3},{3,2},{4,5},{5,4},{6,7},{7,6},{8,9},{9,8},{10,11... | collective-permute-start | bytes 1769480 | tf_op jit(solution)/shard_map/ppermute | solution.py:69
  615.9 21.8 %all-to-all-start.6 = ((bf16[8,144,432]{2,1,0:T(8,128)(2,1)}), bf16[8,144,432]{2,1,0:T(8,128)(2,1)S(1)}, u32[]{:S(2)}, u32[]{:S(2)}) async-start(bf16[8,144,432]{2,1,0:T(8,128)(2,1)} %pack_return.2), calls=%async_computation.7 | async-start | bytes 2359296 | tf_op jit(solution)/shard_map/all_to_all | solution.py:608
  619.5 157.1 %reduce-scatter.5.cloned.1.call-start = ((), (), s32[]{:S(2)}) async-start(), calls=%async_computation.13 | async-start | bytes 5971968 | tf_op jit(solution)/shard_map/reduce_scatter | solution.py:588
  622.3 157.3 %collective-permute-start.97 = (bf16[288,144]{1,0:T(8,128)(2,1)}, bf16[288,144]{1,0:T(8,128)(2,1)}, u32[]{:S(2)}, u32[]{:S(2)}) collective-permute-start(bf16[288,144]{1,0:T(8,128)(2,1)} %get-tuple-element.301), channel_id=1, source_target_pairs={{0,0},{5,1},{3,2},{4,3},{2,4},{7,5},{1,6},{6,7},{8,8},{13,9},{11,1... | collective-permute-start | bytes 248840 | tf_op jit(solution)/shard_map/ppermute | solution.py:147
  625.3 24.3 %collective-permute-start.76 = (bf16[256,1152]{1,0:T(8,128)(2,1)}, bf16[256,1152]{1,0:T(8,128)(2,1)}, u32[]{:S(2)}, u32[]{:S(2)}) collective-permute-start(bf16[256,1152]{1,0:T(8,128)(2,1)} %get-tuple-element.420), channel_id=1, source_target_pairs={{0,2},{1,3},{2,0},{3,1},{4,6},{5,7},{6,4},{7,5},{8,10},{9,11},{10,... | collective-permute-start | bytes 1769480 | tf_op jit(solution)/shard_map/ppermute | solution.py:69
  682.9 18.3 %all-to-all-start.7 = ((bf16[4,288,288]{2,1,0:T(8,128)(2,1)}), bf16[4,288,288]{2,1,0:T(8,128)(2,1)S(1)}, u32[]{:S(2)}, u32[]{:S(2)}) async-start(bf16[4,288,288]{2,1,0:T(8,128)(2,1)} %split_project.3), calls=%async_computation.8 | async-start | bytes 1769472 | tf_op jit(solution)/shard_map/all_to_all | solution.py:562
  723.6 31.4 %collective-permute-start.85 = (bf16[256,1152]{1,0:T(8,128)(2,1)S(1)}, bf16[256,1152]{1,0:T(8,128)(2,1)S(1)}, u32[]{:S(2)}, u32[]{:S(2)}) collective-permute-start(bf16[256,1152]{1,0:T(8,128)(2,1)S(1)} %get-tuple-element.296), channel_id=1, source_target_pairs={{0,1},{1,0},{2,3},{3,2},{4,5},{5,4},{6,7},{7,6},{8,9},{9,8},{10,11... | collective-permute-start | bytes 1769480 | tf_op jit(solution)/shard_map/ppermute | solution.py:69
  736.2 52.9 %collective-permute-start.98 = (bf16[288,144]{1,0:T(8,128)(2,1)S(1)}, bf16[288,144]{1,0:T(8,128)(2,1)S(1)}, u32[]{:S(2)}, u32[]{:S(2)}) collective-permute-start(bf16[288,144]{1,0:T(8,128)(2,1)S(1)} %copy-done.121), channel_id=1, source_target_pairs={{4,0},{2,1},{7,2},{1,3},{6,4},{0,5},{5,6},{3,7},{12,8},{10,9},{15,... | collective-permute-start | bytes 248840 | tf_op jit(solution)/shard_map/ppermute | solution.py:147
  750.9 38.2 %collective-permute-start.99 = (bf16[288,144]{1,0:T(8,128)(2,1)S(1)}, bf16[288,144]{1,0:T(8,128)(2,1)}, u32[]{:S(2)}, u32[]{:S(2)}) collective-permute-start(bf16[288,144]{1,0:T(8,128)(2,1)S(1)} %copy-done.119), channel_id=1, source_target_pairs={{1,0},{6,1},{0,2},{5,3},{3,4},{4,5},{2,6},{7,7},{9,8},{14,9},{8,10... | collective-permute-start | bytes 248840 | tf_op jit(solution)/shard_map/ppermute | solution.py:147
  761.6 22.5 %all-to-all-start.8 = ((f32[32,2,864]{2,1,0:T(2,128)}), f32[32,2,864]{2,1,0:T(2,128)S(1)}, u32[]{:S(2)}, u32[]{:S(2)}) async-start(f32[32,2,864]{2,1,0:T(2,128)} %bitcast.72), calls=%async_computation.9 | async-start | bytes 458752 | tf_op jit(solution)/shard_map/all_to_all | solution.py:1353
  784.2 20.6 %all-to-all-start.9 = ((bf16[8,144,432]{2,1,0:T(8,128)(2,1)}), bf16[8,144,432]{2,1,0:T(8,128)(2,1)S(1)}, u32[]{:S(2)}, u32[]{:S(2)}) async-start(bf16[8,144,432]{2,1,0:T(8,128)(2,1)} %pack_return.3), calls=%async_computation.11 | async-start | bytes 2359296 | tf_op jit(solution)/shard_map/all_to_all | solution.py:608
  (311 other events, 2632.2 us)
Sparse Core Ops, SparseCore 0:
  249.5 93.2 all-gather.2
  486.7 125.9 reduce-scatter.2
  637.8 116.7 reduce-scatter.4

commit v5 on v4

--- a/solution.py
+++ b/solution.py
@@ -462,7 +462,8 @@
             parts.append(got_ref[device][:, half * cols : (half + 1) * cols])
         expand_ref[half * cols : (half + 1) * cols] = side_by_side(parts).astype(F32)
     for s, unit in enumerate(unit_table(8, 2)):
-        reduce_ref[unit * cols : (unit + 1) * cols] = got_ref[s][:, 2 * cols :].astype(F32)
+        part = got_ref[s][:, 2 * cols :].astype(F32)
+        reduce_ref[:, unit * cols : (unit + 1) * cols] = part.T
 
 
 def split_attention_kernel(me_ref, joint_ref, project_ref, *outs):
@@ -608,8 +609,9 @@
     got = lax.all_to_all(chunks, SEQ, 0, 0, tiled=True)
     if not compact():
         return unpack_return_any(got)
-    outs = [((2 * cols, 4 * cols), F32), ((8 * cols, cols), F32)]
-    return rearrange(unpack_return_kernel, [got], outs, "unpack_return")
+    outs = [((2 * cols, 4 * cols), F32), ((cols, 8 * cols), F32)]
+    expand, reduce = rearrange(unpack_return_kernel, [got], outs, "unpack_return")
+    return expand, reduce.T
 
 
 def half_call(body, half, chunks, matrices, tokens, into, partial, name):

time: 830 us -> 829 us (level)
    unnamed x501 -> x500, local copies, waits for them, and re-layouts: 56 us -> 52.8 us
  transfers between devices with their start and end apart: 113 -> 113, of which waited for: 46 -> 45; matrix products, arithmetic and copies ran while one was open for 14% -> 15% of each run, Pallas kernels for 21% -> 21%
where the time goes in v5:
time: 829 us; the launch traced here: 817 us
  waiting for transfers between devices  263 us (32%)
  Pallas kernels  193 us (23%)
  starting transfers between devices  164 us (20%)
  local copies, waits for them, and re-layouts  70.3 us (8%)
  other arithmetic  69.2 us (8%)
  matrix products  39.8 us (5%)
  between operations  17.8 us (2%)
    ppermute x72, waiting for transfers between devices, exchange(): return lax.ppermute(value, SEQ, [(i, i ^ mask) for i in range(seq)])  171 us
    pallas_call x12, Pallas kernels, half_call(): pl.pallas_call(kernel, grid=(2,), in_specs=specs + [pl.BlockSpec(memory_s...  69.8 us
    ppermute x18, waiting for transfers between devices, from_plane(): lax.ppermute(value, 'dp', [(d, (d + back) % planes) for d in range(planes)])  56.8 us
    unnamed x500, local copies, waits for them, and re-layouts  52.8 us
    pallas_call x23, Pallas kernels, rearrange(): pl.pallas_call(body, in_specs=[pl.BlockSpec(memory_space=pltpu.SMEM)] + [...  52.5 us
    ppermute x72, starting transfers between devices, exchange(): return lax.ppermute(value, SEQ, [(i, i ^ mask) for i in range(seq)])  49.4 us
    ppermute x18, starting transfers between devices, from_plane(): lax.ppermute(value, 'dp', [(d, (d + back) % planes) for d in range(planes)])  49.2 us
    dot_general x8, matrix products, through_rows(): lax.dot_general(left, right, (((0,), (0,)), ((), ())), preferred_element_...  31.9 us
  transfers between devices with their start and end apart: 113, of which 45 were waited for; matrix products, arithmetic and copies ran while one was open for 15% of the time, Pallas kernels for 21%

profile of v5, /device:TPU:0, one launch (start us, length us, event | category | flops | bytes accessed | tf_op | source)
XLA Modules:
  0.0 817.2 jit_solution(996291081756508258)
XLA Ops:
  7.2 5.1 collective-permute-start
  27.1 4.7 all-to-all-start
  42.0 9.4 %collective-permute-done.6.refs_1_ = bf16[144,1152]{1,0:T(8,128)(2,1)S(1)} collective-permute-done((bf16[144,1152]{1,0:T(8,128)(2,1)S(1)}, bf16[144,1152]{1,0:T(8,128)(2,1)S(1)}, u32[]{:S(2)}, u32[]{:S(2)}) %collective-permute-start.6) | collective-permute-done | bytes 331808 | tf_op jit(solution)/shard_map/ppermute | solution.py:81
  55.2 5.2 all-to-all-done
  74.7 6.2 all-to-all-done.1.got_ref
  87.3 9.2 %collective-permute-done.14.refs_7_ = bf16[144,1152]{1,0:T(8,128)(2,1)S(1)} collective-permute-done((bf16[144,1152]{1,0:T(8,128)(2,1)}, bf16[144,1152]{1,0:T(8,128)(2,1)S(1)}, u32[]{:S(2)}, u32[]{:S(2)}) %collective-permute-start.14) | collective-permute-done | bytes 331808 | tf_op jit(solution)/shard_map/ppermute | solution.py:69
  123.4 6.3 collective-permute-done.17.refs_6_.refs_7_
  141.6 12.0 %collective-permute-done.18.refs_2_ = bf16[288,1152]{1,0:T(8,128)(2,1)} collective-permute-done((bf16[288,1152]{1,0:T(8,128)(2,1)}, bf16[288,1152]{1,0:T(8,128)(2,1)}, u32[]{:S(2)}, u32[]{:S(2)}) %collective-permute-start.18) | collective-permute-done | bytes 663584 | tf_op jit(solution)/shard_map/ppermute | solution.py:81
  154.6 10.1 %attend.3 = (bf16[1024,384]{1,0:T(8,128)(2,1)S(1)}, f32[1024,128]{1,0:T(8,128)S(1)}) custom-call(s32[3]{0:T(128)S(1)} %pad_add_fusion.2.me_ref, bf16[1024,1152]{1,0:T(8,128)(2,1)S(1)} %joint_far.2.q_ref.refs_0_.refs_1_.refs_2_.refs_3_.refs_4_.refs_5_, bf16[1024,1152]{1,0:T(8,128)(2,1)S(1)} %joint_far.2.q_ref.refs_0_.refs_1_.refs_2_.refs_3_.refs_4_.refs_5_, ...), custom_call_target="tpu_custom_call" | custom-call | flops 2684354560 | bytes 3145728 | tf_op jit(solution)/shard_map/attend/pallas_call | solution.py:881
  183.6 11.6 %collective-permute-start.25 = (bf16[144,1152]{1,0:T(8,128)(2,1)S(1)}, bf16[144,1152]{1,0:T(8,128)(2,1)S(1)}, u32[]{:S(2)}, u32[]{:S(2)}) collective-permute-start(bf16[144,1152]{1,0:T(8,128)(2,1)S(1)} %copy-done.98), channel_id=1, source_target_pairs={{0,8},{8,16},{16,24},{24,0},{1,9},{9,17},{17,25},{25,1},{2,10},{10... | collective-permute-start | bytes 995336 | tf_op jit(solution)/shard_map/ppermute | solution.py:81
  200.1 5.9 collective-permute-done.25.refs_1_
  214.7 12.8 %collective-permute-start.31 = (bf16[144,1152]{1,0:T(8,128)(2,1)S(1)}, bf16[144,1152]{1,0:T(8,128)(2,1)}, u32[]{:S(2)}, u32[]{:S(2)}) collective-permute-start(bf16[144,1152]{1,0:T(8,128)(2,1)S(1)} %copy-done.98), channel_id=1, source_target_pairs={{0,24},{8,0},{16,8},{24,16},{1,25},{9,1},{17,9},{25,17},{2,26},{10... | collective-permute-start | bytes 995336 | tf_op jit(solution)/shard_map/ppermute | solution.py:81
  233.7 5.3 open_forward.2
  239.1 8.7 %forward_near.2 = (bf16[1024,1152]{1,0:T(8,128)(2,1)S(1)}, bf16[1024,1152]{1,0:T(8,128)(2,1)}, bf16[256,1152]{1,0:T(8,128)(2,1)S(1)}, bf16[256,1152]{1,0:T(8,128)(2,1)}) custom-call(bf16[256,1152]{1,0:T(8,128)(2,1)S(1)} %add_convert_fusion.3.a_ref, bf16[256,1152]{1,0:T(8,128)(2,1)S(1)} %copy-done.78, bf16[1152,1152]{1,0:T(8,128)(2,1)} %get-tuple-element.189.refs_0_, ...), custom_call_target="tpu_custom_call" | custom-call | flops 2717908992 | bytes 5308416 | tf_op jit(solution)/shard_map/forward_near/pallas_call | solution.py:644
  253.1 8.4 %forward_far.2 = (bf16[1024,1152]{1,0:T(8,128)(2,1)S(1)}, bf16[1024,1152]{1,0:T(8,128)(2,1)}, bf16[256,1152]{1,0:T(8,128)(2,1)S(1)}, bf16[256,1152]{1,0:T(8,128)(2,1)S(1)}) custom-call(bf16[256,1152]{1,0:T(8,128)(2,1)S(1)} %collective-permute-done.27.a_ref, ...), custom_call_target="tpu_custom_call", output_to_operand_aliasing={{0}: (6, {}), {1}: (7, {})} | custom-call | flops 2717908992 | bytes 5308416 | tf_op jit(solution)/shard_map/forward_far/pallas_call | solution.py:644
  270.0 9.9 %collective-permute-done.37.refs_6_ = bf16[144,1152]{1,0:T(8,128)(2,1)S(1)} collective-permute-done((bf16[144,1152]{1,0:T(8,128)(2,1)}, bf16[144,1152]{1,0:T(8,128)(2,1)S(1)}, u32[]{:S(2)}, u32[]{:S(2)}) %collective-permute-start.37) | collective-permute-done | bytes 331808 | tf_op jit(solution)/shard_map/ppermute | solution.py:69
  279.9 6.9 collective-permute-done.38.refs_7_
  301.2 11.7 %collective-permute-done.40.a_ref = bf16[256,1152]{1,0:T(8,128)(2,1)S(1)} collective-permute-done((bf16[256,1152]{1,0:T(8,128)(2,1)S(1)}, bf16[256,1152]{1,0:T(8,128)(2,1)S(1)}, u32[]{:S(2)}, u32[]{:S(2)}) %collective-permute-start.40) | collective-permute-done | bytes 589856 | tf_op jit(solution)/shard_map/ppermute | solution.py:69
  323.1 8.8 %collective-permute-done.43.refs_6_.refs_7_ = bf16[256,768]{1,0:T(8,128)(2,1)} collective-permute-done((bf16[256,768]{1,0:T(8,128)(2,1)}, bf16[256,768]{1,0:T(8,128)(2,1)}, u32[]{:S(2)}, u32[]{:S(2)}) %collective-permute-start.43) | collective-permute-done | bytes 393248 | tf_op jit(solution)/shard_map/ppermute | solution.py:69
  331.9 6.3 attend.4
  342.7 6.3 attend.5
  352.0 12.8 %collective-permute-done.45 = bf16[256,1152]{1,0:T(8,128)(2,1)S(1)} collective-permute-done((bf16[256,1152]{1,0:T(8,128)(2,1)S(1)}, bf16[256,1152]{1,0:T(8,128)(2,1)S(1)}, u32[]{:S(2)}, u32[]{:S(2)}) %collective-permute-start.45) | collective-permute-done | bytes 589856 | tf_op jit(solution)/shard_map/ppermute | solution.py:69
  376.8 8.7 %forward_near.3 = (bf16[1024,1152]{1,0:T(8,128)(2,1)S(1)}, bf16[1024,1152]{1,0:T(8,128)(2,1)}, bf16[256,1152]{1,0:T(8,128)(2,1)S(1)}, bf16[256,1152]{1,0:T(8,128)(2,1)S(1)}) custom-call(bf16[256,1152]{1,0:T(8,128)(2,1)S(1)} %get-tuple-element.477.a_ref, bf16[256,1152]{1,0:T(8,128)(2,1)S(1)} %collective-permute-done.48.b_ref, bf16[1152,1152]{1,0:T(8,128)(2,1)} %copy-done.7, ...), custom_call_target="tpu_custom_call" | custom-call | flops 2717908992 | bytes 5308416 | tf_op jit(solution)/shard_map/forward_near/pallas_call | solution.py:644
  387.5 8.4 %forward_far.3 = (bf16[1024,1152]{1,0:T(8,128)(2,1)S(1)}, bf16[1024,1152]{1,0:T(8,128)(2,1)}, bf16[256,1152]{1,0:T(8,128)(2,1)S(1)}, bf16[256,1152]{1,0:T(8,128)(2,1)S(1)}) custom-call(bf16[256,1152]{1,0:T(8,128)(2,1)S(1)} %collective-permute-done.47.a_ref, ...), custom_call_target="tpu_custom_call", output_to_operand_aliasing={{0}: (6, {}), {1}: (7, {})} | custom-call | flops 2717908992 | bytes 5308416 | tf_op jit(solution)/shard_map/forward_far/pallas_call | solution.py:644
  395.9 6.8 backward_near.2
  404.9 7.2 backward_far.2
  416.1 13.7 %collective-permute-done.51 = bf16[256,1152]{1,0:T(8,128)(2,1)S(1)} collective-permute-done((bf16[256,1152]{1,0:T(8,128)(2,1)S(1)}, bf16[256,1152]{1,0:T(8,128)(2,1)S(1)}, u32[]{:S(2)}, u32[]{:S(2)}) %collective-permute-start.51) | collective-permute-done | bytes 589856 | tf_op jit(solution)/shard_map/ppermute | solution.py:69
  433.2 8.6 %collective-permute-done.57 = bf16[256,1152]{1,0:T(8,128)(2,1)S(1)} collective-permute-done((bf16[256,1152]{1,0:T(8,128)(2,1)S(1)}, bf16[256,1152]{1,0:T(8,128)(2,1)S(1)}, u32[]{:S(2)}, u32[]{:S(2)}) %collective-permute-start.57) | collective-permute-done | bytes 589856 | tf_op jit(solution)/shard_map/ppermute | solution.py:69
  457.1 6.8 collective-permute-done.60
  469.3 15.9 %attend_back.2 = (bf16[1024,1152]{1,0:T(8,128)(2,1)}, bf16[256,768]{1,0:T(8,128)(2,1)S(1)}, bf16[128,768]{1,0:T(8,128)(2,1)S(1)}) custom-call(s32[3]{0:T(128)S(1)} %pad_add_fusion.2.me_ref, bf16[1024,1152]{1,0:T(8,128)(2,1)} %copy-done, bf16[1024,1152]{1,0:T(8,128)(2,1)} %copy-done, bf16[1024,1152]{1,0:T(8,128)(2,1)} %copy-done, bf16[1024,1152]{1,0:T(8,128)(2,1)} %copy-done, ...), custom_call_target="tpu_custom_call" | custom-call | flops 6710886400 | bytes 7864320 | tf_op jit(solution)/shard_map/attend_back/pallas_call | solution.py:916
  486.6 13.0 %collective-permute-done.62 = bf16[256,768]{1,0:T(8,128)(2,1)} collective-permute-done((bf16[256,768]{1,0:T(8,128)(2,1)}, bf16[256,768]{1,0:T(8,128)(2,1)}, u32[]{:S(2)}, u32[]{:S(2)}) %collective-permute-start.62) | collective-permute-done | bytes 393248 | tf_op jit(solution)/shard_map/ppermute | solution.py:69
  536.1 6.8 collective-permute-done.64
  557.1 6.8 backward_near.3
  567.2 6.7 backward_far.3
  580.4 4.8 convolution_convert_fusion.2.reduce_ref
  585.2 9.6 %collective-permute-done.71 = bf16[256,1152]{1,0:T(8,128)(2,1)S(1)} collective-permute-done((bf16[256,1152]{1,0:T(8,128)(2,1)S(1)}, bf16[256,1152]{1,0:T(8,128)(2,1)S(1)}, u32[]{:S(2)}, u32[]{:S(2)}) %collective-permute-start.71) | collective-permute-done | bytes 589856 | tf_op jit(solution)/shard_map/ppermute | solution.py:69
  600.3 12.5 %reduce-scatter.3.cloned.1.call-done = bf16[1,288,1152]{2,1,0:T(8,128)(2,1)} async-done(((bf16[8,288,1152]{2,1,0:T(8,128)(2,1)}), bf16[1,288,1152]{2,1,0:T(8,128)(2,1)}) %reduce-scatter.3.cloned.1.call-update) | async-done | bytes 663568 | tf_op jit(solution)/shard_map/reduce_scatter | solution.py:589
  627.6 5.9 convolution_convert_fusion.1.expand_ref
  640.9 8.7 %collective-permute-done.76 = bf16[256,1152]{1,0:T(8,128)(2,1)} collective-permute-done((bf16[256,1152]{1,0:T(8,128)(2,1)}, bf16[256,1152]{1,0:T(8,128)(2,1)}, u32[]{:S(2)}, u32[]{:S(2)}) %collective-permute-start.76) | collective-permute-done | bytes 589856 | tf_op jit(solution)/shard_map/ppermute | solution.py:69
  649.6 7.2 multiply_reduce_fusion.1
  661.0 15.5 %attend_back.3 = (bf16[1024,1152]{1,0:T(8,128)(2,1)}, bf16[256,768]{1,0:T(8,128)(2,1)S(1)}, bf16[128,768]{1,0:T(8,128)(2,1)S(1)}) custom-call(s32[3]{0:T(128)S(1)} %pad_add_fusion.2.me_ref, bf16[1024,1152]{1,0:T(8,128)(2,1)} %copy-done.1, bf16[1024,1152]{1,0:T(8,128)(2,1)} %copy-done.1, bf16[1024,1152]{1,0:T(8,128)(2,1)} %copy-done.1, ...), custom_call_target="tpu_custom_call" | custom-call | flops 6710886400 | bytes 7864320 | tf_op jit(solution)/shard_map/attend_back/pallas_call | solution.py:916
  686.9 6.7 collective-permute-done.82
  695.6 6.5 convolution_convert_fusion.joint_ref
  708.9 8.6 %collective-permute-done.90 = bf16[144,1152]{1,0:T(8,128)(2,1)S(1)} collective-permute-done((bf16[144,1152]{1,0:T(8,128)(2,1)S(1)}, bf16[144,1152]{1,0:T(8,128)(2,1)S(1)}, u32[]{:S(2)}, u32[]{:S(2)}) %collective-permute-start.90) | collective-permute-done | bytes 331808 | tf_op jit(solution)/shard_map/ppermute | solution.py:69
  728.4 5.9 collective-permute-done.91
  737.7 14.0 %collective-permute-done.92 = bf16[144,1152]{1,0:T(8,128)(2,1)S(1)} collective-permute-done((bf16[144,1152]{1,0:T(8,128)(2,1)S(1)}, bf16[144,1152]{1,0:T(8,128)(2,1)S(1)}, u32[]{:S(2)}, u32[]{:S(2)}) %collective-permute-start.92) | collective-permute-done | bytes 331808 | tf_op jit(solution)/shard_map/ppermute | solution.py:81
  761.9 8.6 %all-to-all-start.8 = ((f32[32,2,864]{2,1,0:T(2,128)}), f32[32,2,864]{2,1,0:T(2,128)S(1)}, u32[]{:S(2)}, u32[]{:S(2)}) async-start(f32[32,2,864]{2,1,0:T(2,128)} %bitcast.73), calls=%async_computation.9 | async-start | bytes 458752 | tf_op jit(solution)/shard_map/all_to_all | solution.py:1355
  795.2 10.2 %all-to-all-done.9.got_ref = bf16[8,144,432]{2,1,0:T(8,128)(2,1)S(1)} async-done(((bf16[8,144,432]{2,1,0:T(8,128)(2,1)}), bf16[8,144,432]{2,1,0:T(8,128)(2,1)S(1)}, u32[]{:S(2)}, u32[]{:S(2)}) %all-to-all-start.9) | async-done | bytes 995360 | tf_op jit(solution)/shard_map/all_to_all | solution.py:609
  (936 shorter events, 381.6 us)
Async XLA Ops:
  27.1 33.3 %all-to-all-start = ((f32[32,2,2,864]{3,2,1,0:T(2,128)}), f32[32,2,2,864]{3,2,1,0:T(2,128)}, u32[]{:S(2)}, u32[]{:S(2)}) async-start(f32[32,2,2,864]{3,2,1,0:T(2,128)} %copy.123), calls=%async_computation | async-start | bytes 917504 | tf_op jit(solution)/shard_map/all_to_all | solution.py:1226
  39.5 27.2 %collective-permute-start.8 = (bf16[144,1152]{1,0:T(8,128)(2,1)S(1)}, bf16[144,1152]{1,0:T(8,128)(2,1)}, u32[]{:S(2)}, u32[]{:S(2)}) collective-permute-start(bf16[144,1152]{1,0:T(8,128)(2,1)S(1)} %get-tuple-element.157.refs_0_), channel_id=1, source_target_pairs={{0,16},{8,24},{16,0},{24,8},{1,17},{9,25},{17,1},{25,9},{2,18},{10... | collective-permute-start | bytes 995336 | tf_op jit(solution)/shard_map/ppermute | solution.py:81
  60.4 20.4 %all-to-all-start.1 = ((bf16[8,144,432]{2,1,0:T(8,128)(2,1)}), bf16[8,144,432]{2,1,0:T(8,128)(2,1)S(1)}, u32[]{:S(2)}, u32[]{:S(2)}) async-start(bf16[8,144,432]{2,1,0:T(8,128)(2,1)} %pack_forward.2), calls=%async_computation.1 | async-start | bytes 2359296 | tf_op jit(solution)/shard_map/all_to_all | solution.py:515
  66.8 20.2 %collective-permute-start.13 = (bf16[144,1152]{1,0:T(8,128)(2,1)}, bf16[144,1152]{1,0:T(8,128)(2,1)}, u32[]{:S(2)}, u32[]{:S(2)}) collective-permute-start(bf16[144,1152]{1,0:T(8,128)(2,1)} %collective-permute-done.8.refs_2_), channel_id=1, source_target_pairs={{0,4},{1,5},{2,6},{3,7},{4,0},{5,1},{6,2},{7,3},{8,12},{9,13},{10,... | collective-permute-start | bytes 995336 | tf_op jit(solution)/shard_map/ppermute | solution.py:69
  81.8 19.9 %collective-permute-start.12 = (bf16[256,1152]{1,0:T(8,128)(2,1)S(1)}, bf16[256,1152]{1,0:T(8,128)(2,1)S(1)}, u32[]{:S(2)}, u32[]{:S(2)}) collective-permute-start(bf16[256,1152]{1,0:T(8,128)(2,1)S(1)} %fusion.16.a_ref), channel_id=1, source_target_pairs={{0,1},{1,0},{2,3},{3,2},{4,5},{5,4},{6,7},{7,6},{8,9},{9,8},{10,11... | collective-permute-start | bytes 1769480 | tf_op jit(solution)/shard_map/ppermute | solution.py:69
  81.9 21.9 %collective-permute-start.15 = (bf16[288,1152]{1,0:T(8,128)(2,1)S(1)}, bf16[288,1152]{1,0:T(8,128)(2,1)S(1)}, u32[]{:S(2)}, u32[]{:S(2)}) collective-permute-start(bf16[288,1152]{1,0:T(8,128)(2,1)S(1)} %unpack_forward.2.refs_0_), channel_id=1, source_target_pairs={{0,8},{8,16},{16,24},{24,0},{1,9},{9,17},{17,25},{25,1},{2,10},{10... | collective-permute-start | bytes 1990664 | tf_op jit(solution)/shard_map/ppermute | solution.py:81
  83.6 20.2 %collective-permute-start.11 = (bf16[256,1152]{1,0:T(8,128)(2,1)S(1)}, bf16[256,1152]{1,0:T(8,128)(2,1)S(1)}, u32[]{:S(2)}, u32[]{:S(2)}) collective-permute-start(bf16[256,1152]{1,0:T(8,128)(2,1)S(1)} %fusion.16.a_ref), channel_id=1, source_target_pairs={{0,2},{1,3},{2,0},{3,1},{4,6},{5,7},{6,4},{7,5},{8,10},{9,11},{10,... | collective-permute-start | bytes 1769480 | tf_op jit(solution)/shard_map/ppermute | solution.py:69
  114.4 19.0 %all-to-all-start.3 = ((bf16[4,288,288]{2,1,0:T(8,128)(2,1)}), bf16[4,288,288]{2,1,0:T(8,128)(2,1)S(1)}, u32[]{:S(2)}, u32[]{:S(2)}) async-start(bf16[4,288,288]{2,1,0:T(8,128)(2,1)} %copy-done.54), calls=%async_computation.3 | async-start | bytes 1769472 | tf_op jit(solution)/shard_map/all_to_all | solution.py:540
  119.4 34.1 %collective-permute-start.18 = (bf16[288,1152]{1,0:T(8,128)(2,1)}, bf16[288,1152]{1,0:T(8,128)(2,1)}, u32[]{:S(2)}, u32[]{:S(2)}) collective-permute-start(bf16[288,1152]{1,0:T(8,128)(2,1)} %copy-done.21), channel_id=1, source_target_pairs={{0,16},{8,24},{16,0},{24,8},{1,17},{9,25},{17,1},{25,9},{2,18},{10... | collective-permute-start | bytes 1990664 | tf_op jit(solution)/shard_map/ppermute | solution.py:81
  134.4 32.9 %all-to-all-start.2 = ((bf16[8,144,432]{2,1,0:T(8,128)(2,1)}), bf16[8,144,432]{2,1,0:T(8,128)(2,1)}, u32[]{:S(2)}, u32[]{:S(2)}) async-start(bf16[8,144,432]{2,1,0:T(8,128)(2,1)} %pack_forward.3), calls=%async_computation.2 | async-start | bytes 2359296 | tf_op jit(solution)/shard_map/all_to_all | solution.py:515
  138.6 231.6 %all-gather.3.cloned.1.call-start = ((), (), s32[]{:S(2)}) async-start(), calls=%async_computation.14 | async-start | bytes 5971968 | tf_op jit(solution)/shard_map/all_gather | solution.py:524
  139.0 31.1 %collective-permute-start.19 = (bf16[288,1152]{1,0:T(8,128)(2,1)}, bf16[288,1152]{1,0:T(8,128)(2,1)}, u32[]{:S(2)}, u32[]{:S(2)}) collective-permute-start(bf16[288,1152]{1,0:T(8,128)(2,1)} %copy-done.21), channel_id=1, source_target_pairs={{0,24},{8,0},{16,8},{24,16},{1,25},{9,1},{17,9},{25,17},{2,26},{10... | collective-permute-start | bytes 1990664 | tf_op jit(solution)/shard_map/ppermute | solution.py:81
  139.3 30.8 %collective-permute-start.20 = (bf16[288,1152]{1,0:T(8,128)(2,1)}, bf16[288,1152]{1,0:T(8,128)(2,1)}, u32[]{:S(2)}, u32[]{:S(2)}) collective-permute-start(bf16[288,1152]{1,0:T(8,128)(2,1)} %copy-done.21), channel_id=1, source_target_pairs={{0,4},{1,5},{2,6},{3,7},{4,0},{5,1},{6,2},{7,3},{8,12},{9,13},{10,... | collective-permute-start | bytes 1990664 | tf_op jit(solution)/shard_map/ppermute | solution.py:69
  174.4 31.5 %collective-permute-start.24 = (bf16[288,1152]{1,0:T(8,128)(2,1)}, bf16[288,1152]{1,0:T(8,128)(2,1)}, u32[]{:S(2)}, u32[]{:S(2)}) collective-permute-start(bf16[288,1152]{1,0:T(8,128)(2,1)} %collective-permute-done.18.refs_2_), channel_id=1, source_target_pairs={{0,4},{1,5},{2,6},{3,7},{4,0},{5,1},{6,2},{7,3},{8,12},{9,13},{10,... | collective-permute-start | bytes 1990664 | tf_op jit(solution)/shard_map/ppermute | solution.py:69
  175.6 31.1 %collective-permute-start.23 = (bf16[288,1152]{1,0:T(8,128)(2,1)S(1)}, bf16[288,1152]{1,0:T(8,128)(2,1)}, u32[]{:S(2)}, u32[]{:S(2)}) collective-permute-start(bf16[288,1152]{1,0:T(8,128)(2,1)S(1)} %copy-done.67), channel_id=1, source_target_pairs={{0,4},{1,5},{2,6},{3,7},{4,0},{5,1},{6,2},{7,3},{8,12},{9,13},{10,... | collective-permute-start | bytes 1990664 | tf_op jit(solution)/shard_map/ppermute | solution.py:69
  179.5 27.2 %collective-permute-start.26 = (bf16[256,1152]{1,0:T(8,128)(2,1)}, bf16[256,1152]{1,0:T(8,128)(2,1)}, u32[]{:S(2)}, u32[]{:S(2)}) collective-permute-start(bf16[256,1152]{1,0:T(8,128)(2,1)} %get-tuple-element.186), channel_id=1, source_target_pairs={{0,1},{1,0},{2,3},{3,2},{4,5},{5,4},{6,7},{7,6},{8,9},{9,8},{10,11... | collective-permute-start | bytes 1769480 | tf_op jit(solution)/shard_map/ppermute | solution.py:69
  183.6 22.3 %collective-permute-start.25 = (bf16[144,1152]{1,0:T(8,128)(2,1)S(1)}, bf16[144,1152]{1,0:T(8,128)(2,1)S(1)}, u32[]{:S(2)}, u32[]{:S(2)}) collective-permute-start(bf16[144,1152]{1,0:T(8,128)(2,1)S(1)} %copy-done.98), channel_id=1, source_target_pairs={{0,8},{8,16},{16,24},{24,0},{1,9},{9,17},{17,25},{25,1},{2,10},{10... | collective-permute-start | bytes 995336 | tf_op jit(solution)/shard_map/ppermute | solution.py:81
  197.6 29.8 %collective-permute-start.29 = (bf16[288,1152]{1,0:T(8,128)(2,1)}, bf16[288,1152]{1,0:T(8,128)(2,1)S(1)}, u32[]{:S(2)}, u32[]{:S(2)}) collective-permute-start(bf16[288,1152]{1,0:T(8,128)(2,1)} %collective-permute-done.19.refs_3_), channel_id=1, source_target_pairs={{0,4},{1,5},{2,6},{3,7},{4,0},{5,1},{6,2},{7,3},{8,12},{9,13},{10,... | collective-permute-start | bytes 1990664 | tf_op jit(solution)/shard_map/ppermute | solution.py:69
  210.0 19.8 %collective-permute-start.28 = (bf16[256,1152]{1,0:T(8,128)(2,1)S(1)}, bf16[256,1152]{1,0:T(8,128)(2,1)S(1)}, u32[]{:S(2)}, u32[]{:S(2)}) collective-permute-start(bf16[256,1152]{1,0:T(8,128)(2,1)S(1)} %add_convert_fusion.3.a_ref), channel_id=1, source_target_pairs={{0,1},{1,0},{2,3},{3,2},{4,5},{5,4},{6,7},{7,6},{8,9},{9,8},{10,11... | collective-permute-start | bytes 1769480 | tf_op jit(solution)/shard_map/ppermute | solution.py:69
  210.8 38.3 %collective-permute-start.27 = (bf16[256,1152]{1,0:T(8,128)(2,1)S(1)}, bf16[256,1152]{1,0:T(8,128)(2,1)S(1)}, u32[]{:S(2)}, u32[]{:S(2)}) collective-permute-start(bf16[256,1152]{1,0:T(8,128)(2,1)S(1)} %add_convert_fusion.3.a_ref), channel_id=1, source_target_pairs={{0,2},{1,3},{2,0},{3,1},{4,6},{5,7},{6,4},{7,5},{8,10},{9,11},{10,... | collective-permute-start | bytes 1769480 | tf_op jit(solution)/shard_map/ppermute | solution.py:69
  212.5 36.6 %collective-permute-start.30 = (bf16[144,1152]{1,0:T(8,128)(2,1)S(1)}, bf16[144,1152]{1,0:T(8,128)(2,1)}, u32[]{:S(2)}, u32[]{:S(2)}) collective-permute-start(bf16[144,1152]{1,0:T(8,128)(2,1)S(1)} %copy-done.98), channel_id=1, source_target_pairs={{0,16},{8,24},{16,0},{24,8},{1,17},{9,25},{17,1},{25,9},{2,18},{10... | collective-permute-start | bytes 995336 | tf_op jit(solution)/shard_map/ppermute | solution.py:81
  214.7 34.5 %collective-permute-start.31 = (bf16[144,1152]{1,0:T(8,128)(2,1)S(1)}, bf16[144,1152]{1,0:T(8,128)(2,1)}, u32[]{:S(2)}, u32[]{:S(2)}) collective-permute-start(bf16[144,1152]{1,0:T(8,128)(2,1)S(1)} %copy-done.98), channel_id=1, source_target_pairs={{0,24},{8,0},{16,8},{24,16},{1,25},{9,1},{17,9},{25,17},{2,26},{10... | collective-permute-start | bytes 995336 | tf_op jit(solution)/shard_map/ppermute | solution.py:81
  228.3 20.9 %collective-permute-start.32 = (bf16[144,1152]{1,0:T(8,128)(2,1)S(1)}, bf16[144,1152]{1,0:T(8,128)(2,1)}, u32[]{:S(2)}, u32[]{:S(2)}) collective-permute-start(bf16[144,1152]{1,0:T(8,128)(2,1)S(1)} %copy-done.98), channel_id=1, source_target_pairs={{0,4},{1,5},{2,6},{3,7},{4,0},{5,1},{6,2},{7,3},{8,12},{9,13},{10,... | collective-permute-start | bytes 995336 | tf_op jit(solution)/shard_map/ppermute | solution.py:69
  230.5 18.6 %collective-permute-start.33 = (bf16[144,1152]{1,0:T(8,128)(2,1)}, bf16[144,1152]{1,0:T(8,128)(2,1)}, u32[]{:S(2)}, u32[]{:S(2)}) collective-permute-start(bf16[144,1152]{1,0:T(8,128)(2,1)} %copy-done.99), channel_id=1, source_target_pairs={{0,4},{1,5},{2,6},{3,7},{4,0},{5,1},{6,2},{7,3},{8,12},{9,13},{10,... | collective-permute-start | bytes 995336 | tf_op jit(solution)/shard_map/ppermute | solution.py:69
  266.1 24.9 %collective-permute-start.36 = (bf16[256,1152]{1,0:T(8,128)(2,1)}, bf16[256,1152]{1,0:T(8,128)(2,1)}, u32[]{:S(2)}, u32[]{:S(2)}) collective-permute-start(bf16[256,1152]{1,0:T(8,128)(2,1)} %fusion.73), channel_id=1, source_target_pairs={{0,2},{1,3},{2,0},{3,1},{4,6},{5,7},{6,4},{7,5},{8,10},{9,11},{10,... | collective-permute-start | bytes 1769480 | tf_op jit(solution)/shard_map/ppermute | solution.py:69
  266.5 26.3 %collective-permute-start.39 = (bf16[256,1152]{1,0:T(8,128)(2,1)}, bf16[256,1152]{1,0:T(8,128)(2,1)}, u32[]{:S(2)}, u32[]{:S(2)}) collective-permute-start(bf16[256,1152]{1,0:T(8,128)(2,1)} %get-tuple-element.200), channel_id=1, source_target_pairs={{0,1},{1,0},{2,3},{3,2},{4,5},{5,4},{6,7},{7,6},{8,9},{9,8},{10,11... | collective-permute-start | bytes 1769480 | tf_op jit(solution)/shard_map/ppermute | solution.py:69
  267.7 19.1 %collective-permute-start.38 = (bf16[144,1152]{1,0:T(8,128)(2,1)}, bf16[144,1152]{1,0:T(8,128)(2,1)S(1)}, u32[]{:S(2)}, u32[]{:S(2)}) collective-permute-start(bf16[144,1152]{1,0:T(8,128)(2,1)} %collective-permute-done.31.refs_3_), channel_id=1, source_target_pairs={{0,4},{1,5},{2,6},{3,7},{4,0},{5,1},{6,2},{7,3},{8,12},{9,13},{10,... | collective-permute-start | bytes 995336 | tf_op jit(solution)/shard_map/ppermute | solution.py:69
  318.2 21.6 %all-to-all-start.4 = ((bf16[4,288,288]{2,1,0:T(8,128)(2,1)}), bf16[4,288,288]{2,1,0:T(8,128)(2,1)}, u32[]{:S(2)}, u32[]{:S(2)}) async-start(bf16[4,288,288]{2,1,0:T(8,128)(2,1)} %copy-done.55), calls=%async_computation.4 | async-start | bytes 1769472 | tf_op jit(solution)/shard_map/all_to_all | solution.py:540
  322.4 290.3 %reduce-scatter.3.cloned.1.call-start = ((), (), s32[]{:S(2)}) async-start(), calls=%async_computation.12 | async-start | bytes 5971968 | tf_op jit(solution)/shard_map/reduce_scatter | solution.py:589
  404.4 37.5 %collective-permute-start.52 = (bf16[256,1152]{1,0:T(8,128)(2,1)S(1)}, bf16[256,1152]{1,0:T(8,128)(2,1)}, u32[]{:S(2)}, u32[]{:S(2)}) collective-permute-start(bf16[256,1152]{1,0:T(8,128)(2,1)S(1)} %get-tuple-element.223), channel_id=1, source_target_pairs={{0,1},{1,0},{2,3},{3,2},{4,5},{5,4},{6,7},{7,6},{8,9},{9,8},{10,11... | collective-permute-start | bytes 1769480 | tf_op jit(solution)/shard_map/ppermute | solution.py:69
  404.6 37.4 %collective-permute-start.58 = (bf16[256,1152]{1,0:T(8,128)(2,1)S(1)}, bf16[256,1152]{1,0:T(8,128)(2,1)}, u32[]{:S(2)}, u32[]{:S(2)}) collective-permute-start(bf16[256,1152]{1,0:T(8,128)(2,1)S(1)} %get-tuple-element.234), channel_id=1, source_target_pairs={{0,1},{1,0},{2,3},{3,2},{4,5},{5,4},{6,7},{7,6},{8,9},{9,8},{10,11... | collective-permute-start | bytes 1769480 | tf_op jit(solution)/shard_map/ppermute | solution.py:69
  414.5 27.3 %collective-permute-start.57 = (bf16[256,1152]{1,0:T(8,128)(2,1)S(1)}, bf16[256,1152]{1,0:T(8,128)(2,1)S(1)}, u32[]{:S(2)}, u32[]{:S(2)}) collective-permute-start(bf16[256,1152]{1,0:T(8,128)(2,1)S(1)} %fusion.77), channel_id=1, source_target_pairs={{0,2},{1,3},{2,0},{3,1},{4,6},{5,7},{6,4},{7,5},{8,10},{9,11},{10,... | collective-permute-start | bytes 1769480 | tf_op jit(solution)/shard_map/ppermute | solution.py:69
  522.3 21.8 %collective-permute-start.65 = (bf16[256,1152]{1,0:T(8,128)(2,1)}, bf16[256,1152]{1,0:T(8,128)(2,1)}, u32[]{:S(2)}, u32[]{:S(2)}) collective-permute-start(bf16[256,1152]{1,0:T(8,128)(2,1)} %get-tuple-element.248), channel_id=1, source_target_pairs={{0,1},{1,0},{2,3},{3,2},{4,5},{5,4},{6,7},{7,6},{8,9},{9,8},{10,11... | collective-permute-start | bytes 1769480 | tf_op jit(solution)/shard_map/ppermute | solution.py:69
  534.9 30.3 %collective-permute-start.72 = (bf16[144,1152]{1,0:T(8,128)(2,1)S(1)}, bf16[144,1152]{1,0:T(8,128)(2,1)S(1)}, u32[]{:S(2)}, u32[]{:S(2)}) collective-permute-start(bf16[144,1152]{1,0:T(8,128)(2,1)S(1)} %get-tuple-element.255), channel_id=1, source_target_pairs={{0,4},{1,5},{2,6},{3,7},{4,0},{5,1},{6,2},{7,3},{8,12},{9,13},{10,... | collective-permute-start | bytes 995336 | tf_op jit(solution)/shard_map/ppermute | solution.py:69
  555.0 19.2 %collective-permute-start.77 = (bf16[144,1152]{1,0:T(8,128)(2,1)S(1)}, bf16[144,1152]{1,0:T(8,128)(2,1)S(1)}, u32[]{:S(2)}, u32[]{:S(2)}) collective-permute-start(bf16[144,1152]{1,0:T(8,128)(2,1)S(1)} %get-tuple-element.256), channel_id=1, source_target_pairs={{0,4},{1,5},{2,6},{3,7},{4,0},{5,1},{6,2},{7,3},{8,12},{9,13},{10,... | collective-permute-start | bytes 995336 | tf_op jit(solution)/shard_map/ppermute | solution.py:69
  555.5 64.0 %collective-permute-start.80 = (bf16[144,1152]{1,0:T(8,128)(2,1)}, bf16[144,1152]{1,0:T(8,128)(2,1)S(1)}, u32[]{:S(2)}, u32[]{:S(2)}) collective-permute-start(bf16[144,1152]{1,0:T(8,128)(2,1)} %get-tuple-element.257), channel_id=1, source_target_pairs={{0,4},{1,5},{2,6},{3,7},{4,0},{5,1},{6,2},{7,3},{8,12},{9,13},{10,... | collective-permute-start | bytes 995336 | tf_op jit(solution)/shard_map/ppermute | solution.py:69
  578.2 41.3 %collective-permute-start.81 = (bf16[144,1152]{1,0:T(8,128)(2,1)}, bf16[144,1152]{1,0:T(8,128)(2,1)}, u32[]{:S(2)}, u32[]{:S(2)}) collective-permute-start(bf16[144,1152]{1,0:T(8,128)(2,1)} %add_convert_fusion.11), channel_id=1, source_target_pairs={{0,8},{8,16},{16,24},{24,0},{1,9},{9,17},{17,25},{25,1},{2,10},{10... | collective-permute-start | bytes 995336 | tf_op jit(solution)/shard_map/ppermute | solution.py:81
  597.9 29.8 %collective-permute-start.75 = (bf16[256,1152]{1,0:T(8,128)(2,1)}, bf16[256,1152]{1,0:T(8,128)(2,1)S(1)}, u32[]{:S(2)}, u32[]{:S(2)}) collective-permute-start(bf16[256,1152]{1,0:T(8,128)(2,1)} %get-tuple-element.420), channel_id=1, source_target_pairs={{0,1},{1,0},{2,3},{3,2},{4,5},{5,4},{6,7},{7,6},{8,9},{9,8},{10,11... | collective-permute-start | bytes 1769480 | tf_op jit(solution)/shard_map/ppermute | solution.py:69
  615.9 21.6 %all-to-all-start.6 = ((bf16[8,144,432]{2,1,0:T(8,128)(2,1)}), bf16[8,144,432]{2,1,0:T(8,128)(2,1)S(1)}, u32[]{:S(2)}, u32[]{:S(2)}) async-start(bf16[8,144,432]{2,1,0:T(8,128)(2,1)} %pack_return.2), calls=%async_computation.7 | async-start | bytes 2359296 | tf_op jit(solution)/shard_map/all_to_all | solution.py:609
  619.5 158.3 %reduce-scatter.5.cloned.1.call-start = ((), (), s32[]{:S(2)}) async-start(), calls=%async_computation.13 | async-start | bytes 5971968 | tf_op jit(solution)/shard_map/reduce_scatter | solution.py:589
  622.3 158.5 %collective-permute-start.97 = (bf16[288,144]{1,0:T(8,128)(2,1)}, bf16[288,144]{1,0:T(8,128)(2,1)}, u32[]{:S(2)}, u32[]{:S(2)}) collective-permute-start(bf16[288,144]{1,0:T(8,128)(2,1)} %get-tuple-element.301), channel_id=1, source_target_pairs={{0,0},{5,1},{3,2},{4,3},{2,4},{7,5},{1,6},{6,7},{8,8},{13,9},{11,1... | collective-permute-start | bytes 248840 | tf_op jit(solution)/shard_map/ppermute | solution.py:147
  625.1 24.5 %collective-permute-start.76 = (bf16[256,1152]{1,0:T(8,128)(2,1)}, bf16[256,1152]{1,0:T(8,128)(2,1)}, u32[]{:S(2)}, u32[]{:S(2)}) collective-permute-start(bf16[256,1152]{1,0:T(8,128)(2,1)} %get-tuple-element.420), channel_id=1, source_target_pairs={{0,2},{1,3},{2,0},{3,1},{4,6},{5,7},{6,4},{7,5},{8,10},{9,11},{10,... | collective-permute-start | bytes 1769480 | tf_op jit(solution)/shard_map/ppermute | solution.py:69
  683.2 18.9 %all-to-all-start.7 = ((bf16[4,288,288]{2,1,0:T(8,128)(2,1)}), bf16[4,288,288]{2,1,0:T(8,128)(2,1)S(1)}, u32[]{:S(2)}, u32[]{:S(2)}) async-start(bf16[4,288,288]{2,1,0:T(8,128)(2,1)} %split_project.3), calls=%async_computation.8 | async-start | bytes 1769472 | tf_op jit(solution)/shard_map/all_to_all | solution.py:563
  724.2 32.0 %collective-permute-start.85 = (bf16[256,1152]{1,0:T(8,128)(2,1)S(1)}, bf16[256,1152]{1,0:T(8,128)(2,1)S(1)}, u32[]{:S(2)}, u32[]{:S(2)}) collective-permute-start(bf16[256,1152]{1,0:T(8,128)(2,1)S(1)} %get-tuple-element.296), channel_id=1, source_target_pairs={{0,1},{1,0},{2,3},{3,2},{4,5},{5,4},{6,7},{7,6},{8,9},{9,8},{10,11... | collective-permute-start | bytes 1769480 | tf_op jit(solution)/shard_map/ppermute | solution.py:69
  737.6 52.1 %collective-permute-start.98 = (bf16[288,144]{1,0:T(8,128)(2,1)S(1)}, bf16[288,144]{1,0:T(8,128)(2,1)S(1)}, u32[]{:S(2)}, u32[]{:S(2)}) collective-permute-start(bf16[288,144]{1,0:T(8,128)(2,1)S(1)} %copy-done.121), channel_id=1, source_target_pairs={{4,0},{2,1},{7,2},{1,3},{6,4},{0,5},{5,6},{3,7},{12,8},{10,9},{15,... | collective-permute-start | bytes 248840 | tf_op jit(solution)/shard_map/ppermute | solution.py:147
  751.7 38.0 %collective-permute-start.99 = (bf16[288,144]{1,0:T(8,128)(2,1)S(1)}, bf16[288,144]{1,0:T(8,128)(2,1)}, u32[]{:S(2)}, u32[]{:S(2)}) collective-permute-start(bf16[288,144]{1,0:T(8,128)(2,1)S(1)} %copy-done.119), channel_id=1, source_target_pairs={{1,0},{6,1},{0,2},{5,3},{3,4},{4,5},{2,6},{7,7},{9,8},{14,9},{8,10... | collective-permute-start | bytes 248840 | tf_op jit(solution)/shard_map/ppermute | solution.py:147
  761.9 23.2 %all-to-all-start.8 = ((f32[32,2,864]{2,1,0:T(2,128)}), f32[32,2,864]{2,1,0:T(2,128)S(1)}, u32[]{:S(2)}, u32[]{:S(2)}) async-start(f32[32,2,864]{2,1,0:T(2,128)} %bitcast.73), calls=%async_computation.9 | async-start | bytes 458752 | tf_op jit(solution)/shard_map/all_to_all | solution.py:1355
  785.1 20.3 %all-to-all-start.9 = ((bf16[8,144,432]{2,1,0:T(8,128)(2,1)}), bf16[8,144,432]{2,1,0:T(8,128)(2,1)S(1)}, u32[]{:S(2)}, u32[]{:S(2)}) async-start(bf16[8,144,432]{2,1,0:T(8,128)(2,1)} %pack_return.3), calls=%async_computation.11 | async-start | bytes 2359296 | tf_op jit(solution)/shard_map/all_to_all | solution.py:609
  (311 other events, 2641.6 us)
Sparse Core Ops, SparseCore 0:
  249.4 93.3 all-gather.2
  486.7 125.9 reduce-scatter.2
  637.6 117.3 reduce-scatter.4
